TPU v7x, 32 devices: a whole 2x2x4 slice. The times are simulated.
32 devices in a mesh: dp: 2 (over x), mp: 16 (over z, y, core).
Axes of the slice: x: 2, y: 2, z: 4, core: 2. Of those that a mesh axis runs over, the one named last changes fastest.
Arguments:
- tokens: bfloat16 [1024, 16384], P('dp', 'mp'), may hold values from -6 to 6
- block_weight: bfloat16 [7, 256, 32768], P(None, None, 'mp'), may hold values from -0.125 to 0.125
- left_factor: bfloat16 [16384, 256], P('mp'), may hold values from -0.046875 to 0.046875
- right_factor: bfloat16 [256, 32768], P(None, 'mp'), may hold values from -0.375 to 0.375
- out_cotangent: bfloat16 [1024, 32768], P('dp', 'mp'), may hold values from -6 to 6
Outputs:
- activated: bfloat16 [1024, 32768], P('dp', 'mp')
- input_grad: bfloat16 [1024, 16384], P('dp', 'mp')
- weight_grad: bfloat16 [7, 256, 32768], P(None, 'dp', 'mp')
- left_grad: bfloat16 [16384, 256], P('mp')
- right_grad: bfloat16 [256, 32768], P(None, 'mp')
All inputs are finite; a program needn't handle non-finite values.
Results may differ from a plain program's by a relative error of at most 0.0062.
Values may be sent and summed in bfloat16 or wider, within the bound.
No kernel may reach another device: no remote copies, remote signals or barrier semaphores. Data moves between devices by JAX's collectives and lax.ppermute only.
A program may use at most 128 MiB of HBM per device.

v0:
```python
import jax
import jax.numpy as jnp
from jax import lax
from jax.sharding import PartitionSpec as P

gelu_scale = 0.7978845608028654
gelu_cubic = 0.044715


def from_partner(shard, axis, distance):
    return lax.ppermute(shard, axis, [(i, i ^ 1 << distance) for i in range(lax.axis_size(axis))])


def gelu_parts(preact):
    inner = gelu_scale * (preact + gelu_cubic * preact * preact * preact)
    tangent = jnp.tanh(inner)
    value = 0.5 * preact * (1.0 + tangent)
    slope = 0.5 * (1.0 + tangent) + 0.5 * preact * (1.0 - tangent * tangent) * gelu_scale * (
        1.0 + 3.0 * gelu_cubic * preact * preact
    )
    return (value, slope)


def flip_groups(blocks, distance):
    full_shape = blocks.shape
    group_count = full_shape[1]
    split_view = blocks.reshape(
        (full_shape[0], group_count // (2 * distance), 2, distance) + full_shape[2:]
    )
    return jnp.flip(split_view, axis=2).reshape(full_shape)


def on_device(tokens, block_weight, left_factor, right_factor, out_cotangent):
    tok_rows = tokens.shape[0]
    local_width = tokens.shape[1]
    tap_count = block_weight.shape[0]
    block_size = block_weight.shape[1]
    hidden_local = block_weight.shape[2]
    group_count = local_width // block_size
    local_bits = group_count.bit_length() - 1
    tok_blocks = tokens.reshape(tok_rows, group_count, block_size)
    tap_inputs = [tok_blocks]
    for tap_index in range(1, tap_count):
        level_bit = tap_index - 1
        if level_bit < local_bits:
            tap_inputs.append(flip_groups(tok_blocks, 1 << level_bit))
        else:
            partner = from_partner(tokens, "mp", level_bit - local_bits)
            tap_inputs.append(partner.reshape(tok_rows, group_count, block_size))
    stacked = jnp.stack(tap_inputs, axis=2)
    weight_view = block_weight.reshape(tap_count, block_size, group_count, 2 * block_size)
    butterfly = jnp.einsum(
        "tgkc,kcgh->tgh", stacked, weight_view, preferred_element_type=jnp.float32
    )
    butterfly = butterfly.reshape(tok_rows, hidden_local)
    latent = lax.psum(jnp.dot(tokens, left_factor, preferred_element_type=jnp.float32), "mp")
    latent_bf = latent.astype(jnp.bfloat16)
    preact = butterfly + jnp.dot(latent_bf, right_factor, preferred_element_type=jnp.float32)
    value, slope = gelu_parts(preact)
    activated = value.astype(jnp.bfloat16)
    grad_pre = (out_cotangent.astype(jnp.float32) * slope).astype(jnp.bfloat16)
    latent_term = lax.dot_general(
        grad_pre, right_factor, (((1,), (1,)), ((), ())), preferred_element_type=jnp.float32
    )
    latent_grad = lax.psum(latent_term, "mp").astype(jnp.bfloat16)
    left_part = lax.dot_general(
        tokens, latent_grad, (((0,), (0,)), ((), ())), preferred_element_type=jnp.float32
    )
    right_part = lax.dot_general(
        latent_bf, grad_pre, (((0,), (0,)), ((), ())), preferred_element_type=jnp.float32
    )
    left_sum, right_sum = lax.psum((left_part, right_part), "dp")
    grad_view = grad_pre.reshape(tok_rows, group_count, 2 * block_size)
    spread = jnp.einsum(
        "tgh,kcgh->tgkc", grad_view, weight_view, preferred_element_type=jnp.float32
    )
    input_sum = spread[:, :, 0]
    for tap_index in range(1, tap_count):
        level_bit = tap_index - 1
        piece = spread[:, :, tap_index]
        if level_bit < local_bits:
            input_sum = input_sum + flip_groups(piece, 1 << level_bit)
        else:
            returned = from_partner(
                piece.reshape(tok_rows, local_width), "mp", level_bit - local_bits
            )
            input_sum = input_sum + returned.reshape(tok_rows, group_count, block_size)
    low_rank = lax.dot_general(
        latent_grad, left_factor, (((1,), (1,)), ((), ())), preferred_element_type=jnp.float32
    )
    input_grad = (input_sum.reshape(tok_rows, local_width) + low_rank).astype(jnp.bfloat16)
    partial_value = jnp.einsum(
        "tgkc,tgh->kcgh", stacked, grad_view, preferred_element_type=jnp.float32
    )
    partial_value = partial_value.reshape(tap_count, block_size, hidden_local)
    weight_grad = lax.psum_scatter(partial_value, "dp", scatter_dimension=1, tiled=True).astype(
        jnp.bfloat16
    )
    return (
        activated,
        input_grad,
        weight_grad,
        left_sum.astype(jnp.bfloat16),
        right_sum.astype(jnp.bfloat16),
    )


def solution(mesh):
    return jax.shard_map(
        on_device,
        mesh=mesh,
        in_specs=(P("dp", "mp"), P(None, None, "mp"), P("mp", None), P(None, "mp"), P("dp", "mp")),
        out_specs=(P("dp", "mp"), P("dp", "mp"), P(None, "dp", "mp"), P("mp", None), P(None, "mp")),
        check_vma=False,
    )
```

profile of v0, /device:TPU:0, one launch (start us, length us, event | category | flops | bytes accessed | tf_op | source)
XLA Modules:
  0.0 494.8 jit_solution(89540105913356088)
XLA Ops:
  7.2 1.6 copy.25
  8.9 4.1 collective-permute-start.3
  13.0 1.6 collective-permute-start.2
  14.6 1.5 collective-permute-start.1
  16.1 2.6 reshape_reshape.7
  18.7 1.6 reshape_reshape.6
  20.3 2.3 fusion.21
  22.5 1.3 copy.32
  23.8 2.3 copy.27
  26.2 2.3 rev.17
  28.5 2.3 copy.26
  30.8 2.3 rev.16
  33.1 2.3 constant_dynamic-update-slice_fusion.6
  35.4 2.3 constant_dynamic-update-slice_fusion.5
  38.7 79.3 %all-reduce.4 = bf16[512,256]{1,0:T(8,128)(2,1)S(1)} all-reduce(f32[512,256]{1,0:T(8,128)} %fusion.21), channel_id=1, replica_groups=mesh['dp'=2,'mp'=16] {'mp'}, use_global_device_ids=true, to_apply=%region_0.1 | all-reduce | flops 131072 | bytes 786432 | tf_op jit(solution)/shard_map/psum | solution.py:56
  118.0 2.4 copy.36
  120.4 2.3 copy.35
  122.7 2.3 copy.34
  124.9 2.3 copy.33
  127.3 2.4 constant_dynamic-update-slice_fusion.3
  129.6 2.3 constant_dynamic-update-slice_fusion.2
  132.9 1.1 constant_dynamic-update-slice_fusion
  134.0 11.2 %fusion = f32[4,512,512,1]{1,2,3,0:T(8,128)} fusion(bf16[512,4,7,256]{3,0,2,1:T(8,128)(2,1)} %constant_dynamic-update-slice_fusion, bf16[7,32,4,8,512]{4,3,2,1,0:T(8,128)(2,1)} %bitcast.54), kind=kOutput, calls=%fused_computation.2 | convolution fusion | flops 3758096384 | bytes 18874368 | tf_op jit(solution)/shard_map/tgkc,kcgh->tgh/dot_general | solution.py:52
  145.3 5.4 %copy.38 = f32[512,2048]{1,0:T(8,128)} copy(f32[512,2048]{0,1:T(8,128)} %bitcast.66) | data formatting | bytes 8388608 | tf_op jit(solution)/shard_map/reshape | solution.py:55
  150.7 6.8 %fusion.11 = (bf16[512,2048]{1,0:T(8,128)(2,1)}, bf16[512,2048]{1,0:T(8,128)(2,1)}) fusion(bf16[512,2048]{1,0:T(8,128)(2,1)} %param.9, f32[512,2048]{1,0:T(8,128)} %copy.38, bf16[512,256]{1,0:T(8,128)(2,1)S(1)} %all-reduce.4, bf16[256,2048]{1,0:T(8,128)(2,1)S(1)} %copy-done), kind=kOutput, calls=%fused_computation.15 | convolution fusion | flops 560988160 | bytes 11796480 | tf_op jit(solution)/shard_map/dot_general | solution.py:58
  157.5 4.5 reshape.38
  162.0 4.3 copy.54
  166.2 12.9 %convolution_bitcast_fusion = f32[7,256,4,512]{1,3,0,2:T(8,128)} fusion(bf16[512,4,512,1]{0,2,3,1:T(8,128)(2,1)} %copy.54, bf16[512,4,7,256]{3,0,2,1:T(8,128)(2,1)} %constant_dynamic-update-slice_fusion), kind=kOutput, calls=%fused_computation | convolution fusion | flops 3758096384 | bytes 24117248 | tf_op jit(solution)/shard_map/tgkc,tgh->kcgh/dot_general | solution.py:92
  179.1 11.9 %copy.49 = f32[7,256,4,512]{1,3,2,0:T(8,128)} copy(f32[7,256,4,512]{1,3,0,2:T(8,128)} %convolution_bitcast_fusion) | data formatting | bytes 29360128 | tf_op jit(solution)/shard_map/tgkc,tgh->kcgh/transpose | solution.py:92
  191.0 13.2 %convolution_bitcast_fusion.1 = f32[512,4,7,256]{0,3,2,1:T(8,128)} fusion(bf16[512,4,512,1]{0,2,3,1:T(8,128)(2,1)} %copy.54, bf16[7,32,4,8,512]{4,3,2,1,0:T(8,128)(2,1)} %bitcast.55), kind=kOutput, calls=%fused_computation.1 | convolution fusion | flops 3758096384 | bytes 24117248 | tf_op jit(solution)/shard_map/tgh,kcgh->tgkc/dot_general | solution.py:74
  204.3 11.0 %fusion.20 = (f32[512,4,1,256]{0,3,2,1:T(8,128)}, f32[512,4,1,256]{0,3,2,1:T(8,128)}, f32[512,4,1,256]{0,3,2,1:T(8,128)}, f32[512,4,1,256]{0,3,2,1:T(8,128)}, f3...) fusion(f32[512,4,7,256]{0,3,2,1:T(8,128)} %convolution_bitcast_fusion.1), kind=kLoop, calls=%fused_computation.33 | loop fusion | bytes 29360128 | tf_op jit(solution)/shard_map/slice | solution.py:80
  215.2 2.9 copy.47
  218.1 3.0 copy.46
  221.1 2.9 copy.45
  224.0 2.9 copy.44
  226.9 1.4 collective-permute-start.7
  228.3 2.4 fusion.22
  230.6 147.6 %all-reduce.5 = bf16[512,256]{1,0:T(8,128)(2,1)S(1)} all-reduce(f32[512,256]{1,0:T(8,128)S(1)} %fusion.22), channel_id=1, replica_groups=mesh['dp'=2,'mp'=16] {'mp'}, use_global_device_ids=true, to_apply=%region_1.2 | all-reduce | flops 131072 | bytes 786432 | tf_op jit(solution)/shard_map/psum | solution.py:65
  378.7 3.8 fusion.23
  382.5 71.0 %all-reduce.6 = (bf16[1024,256]{0,1:T(8,128)(2,1)S(1)}, bf16[256,2048]{1,0:T(8,128)(2,1)}) all-reduce(f32[1024,256]{0,1:T(8,128)S(1)} %convolution_bitcast_fusion.2, f32[256,2048]{1,0:T(8,128)} %fusion.23), channel_id=1, replica_groups=mesh['dp'=2,'mp'=16] {'dp'}, use_global_device_ids=true, to_apply=%region_3.4 | all-reduce | flops 786432 | bytes 4718592 | tf_op jit(solution)/shard_map/psum | solution.py:72
  454.5 3.1 rev.18
  457.6 2.9 copy.57
  460.5 3.1 rev.19
  463.6 3.0 copy.58
  466.6 2.9 copy.42
  469.5 7.1 %add_convert_fusion = bf16[512,1024]{1,0:T(8,128)(2,1)} fusion(f32[512,1024]{1,0:T(8,128)} %collective-permute-done.7, f32[512,1024]{1,0:T(8,128)} %collective-permute-done.6, f32[512,1024]{1,0:T(8,128)} %collective-permute-done.5, f32[512,1024]{1,0:T(8,128)} %collective-permute-done.4, f32[512,1024]{1,0:T(8,128)} %copy.58, f32[512,1024]{1,0:T(8,128)} %copy.42, ...), kind=kOutput, calls=%fused_computation.18 | convolution fusion | flops 272629760 | bytes 16515072 | tf_op jit(solution)/shard_map/dot_general | solution.py:88
  476.5 5.3 %convert_element_type.33 = bf16[7,128,2048]{1,2,0:T(8,128)(2,1)} convert(f32[7,128,2048]{1,2,0:T(8,128)} %reduce-scatter.2.cloned.1.call-done) | non-fusion elementwise | flops 1835008 | bytes 11010048 | tf_op jit(solution)/shard_map/convert_element_type | solution.py:96
  481.9 6.1 %copy.50 = bf16[7,128,2048]{2,1,0:T(8,128)(2,1)} copy(bf16[7,128,2048]{1,2,0:T(8,128)(2,1)} %convert_element_type.33) | data formatting | bytes 7340032
  (33 shorter events, 3.7 us)
Async XLA Ops:
  7.2 143.5 %copy-start = (bf16[256,2048]{1,0:T(8,128)(2,1)S(1)}, bf16[256,2048]{1,0:T(8,128)(2,1)}, u32[]{:S(2)}) copy-start(bf16[256,2048]{1,0:T(8,128)(2,1)} %param.8) | copy-start | bytes 3145732
  7.2 11.5 %copy-start.1 = (bf16[512,1024]{1,0:T(8,128)(2,1)S(1)}, bf16[512,1024]{1,0:T(8,128)(2,1)}, u32[]{:S(2)}) copy-start(bf16[512,1024]{1,0:T(8,128)(2,1)} %param.5) | copy-start | bytes 3145732
  7.2 469.4 %reduce-scatter.2.cloned.1.call-start = ((), (), s32[]{:S(2)}) async-start(), calls=%async_computation.1 | async-start | bytes 22020096 | tf_op jit(solution)/shard_map/reduce_scatter | solution.py:96
  8.9 109.2 %collective-permute-start.3 = (bf16[512,1024]{0,1:T(8,128)(2,1)S(1)}, bf16[512,1024]{0,1:T(8,128)(2,1)}, u32[]{:S(2)}, u32[]{:S(2)}) collective-permute-start(bf16[512,1024]{0,1:T(8,128)(2,1)S(1)} %copy.25), channel_id=1, source_target_pairs={{0,8},{1,9},{2,10},{3,11},{4,12},{5,13},{6,14},{7,15},{8,0},{9,1},... | collective-permute-start | bytes 3145736 | tf_op jit(solution)/shard_map/ppermute | solution.py:11
  13.0 107.4 %collective-permute-start.2 = (bf16[512,1024]{0,1:T(8,128)(2,1)S(1)}, bf16[512,1024]{0,1:T(8,128)(2,1)}, u32[]{:S(2)}, u32[]{:S(2)}) collective-permute-start(bf16[512,1024]{0,1:T(8,128)(2,1)S(1)} %copy.25), channel_id=1, source_target_pairs={{0,4},{1,5},{2,6},{3,7},{4,0},{5,1},{6,2},{7,3},{8,12},{9,13},{10,... | collective-permute-start | bytes 3145736 | tf_op jit(solution)/shard_map/ppermute | solution.py:11
  14.6 108.1 %collective-permute-start.1 = (bf16[512,1024]{0,1:T(8,128)(2,1)S(1)}, bf16[512,1024]{0,1:T(8,128)(2,1)}, u32[]{:S(2)}, u32[]{:S(2)}) collective-permute-start(bf16[512,1024]{0,1:T(8,128)(2,1)S(1)} %copy.25), channel_id=1, source_target_pairs={{0,2},{1,3},{2,0},{3,1},{4,6},{5,7},{6,4},{7,5},{8,10},{9,11},{10,... | collective-permute-start | bytes 3145736 | tf_op jit(solution)/shard_map/ppermute | solution.py:11
  16.1 108.8 %collective-permute-start = (bf16[512,1024]{0,1:T(8,128)(2,1)S(1)}, bf16[512,1024]{0,1:T(8,128)(2,1)}, u32[]{:S(2)}, u32[]{:S(2)}) collective-permute-start(bf16[512,1024]{0,1:T(8,128)(2,1)S(1)} %copy.25), channel_id=1, source_target_pairs={{0,1},{1,0},{2,3},{3,2},{4,5},{5,4},{6,7},{7,6},{8,9},{9,8},{10,11... | collective-permute-start | bytes 3145736 | tf_op jit(solution)/shard_map/ppermute | solution.py:11
  33.1 4.6 copy-start.4
  118.0 32.6 %copy-start.6 = (bf16[512,256]{1,0:T(8,128)(2,1)}, bf16[512,256]{1,0:T(8,128)(2,1)S(1)}, u32[]{:S(2)}) copy-start(bf16[512,256]{1,0:T(8,128)(2,1)S(1)} %all-reduce.4) | copy-start | bytes 786436
  124.9 8.0 %copy-start.2 = (bf16[512,4,1,256]{3,0,2,1:T(8,128)(2,1)S(1)}, bf16[512,4,1,256]{3,0,2,1:T(8,128)(2,1)}, u32[]{:S(2)}) copy-start(bf16[512,4,1,256]{3,0,2,1:T(8,128)(2,1)} %copy.36) | copy-start | bytes 3145732
  127.3 4.6 copy-start.3
  226.8 242.6 %collective-permute-start.4 = (f32[512,1024]{1,0:T(8,128)}, f32[512,1024]{1,0:T(8,128)}, u32[]{:S(2)}, u32[]{:S(2)}) collective-permute-start(f32[512,1024]{1,0:T(8,128)} %copy.44), channel_id=1, source_target_pairs={{0,1},{1,0},{2,3},{3,2},{4,5},{5,4},{6,7},{7,6},{8,9},{9,8},{10,11... | collective-permute-start | bytes 6291464 | tf_op jit(solution)/shard_map/ppermute | solution.py:11
  226.8 242.6 %collective-permute-start.5 = (f32[512,1024]{1,0:T(8,128)}, f32[512,1024]{1,0:T(8,128)}, u32[]{:S(2)}, u32[]{:S(2)}) collective-permute-start(f32[512,1024]{1,0:T(8,128)} %copy.45), channel_id=1, source_target_pairs={{0,2},{1,3},{2,0},{3,1},{4,6},{5,7},{6,4},{7,5},{8,10},{9,11},{10,... | collective-permute-start | bytes 6291464 | tf_op jit(solution)/shard_map/ppermute | solution.py:11
  226.8 242.6 %collective-permute-start.6 = (f32[512,1024]{1,0:T(8,128)}, f32[512,1024]{1,0:T(8,128)}, u32[]{:S(2)}, u32[]{:S(2)}) collective-permute-start(f32[512,1024]{1,0:T(8,128)} %copy.46), channel_id=1, source_target_pairs={{0,4},{1,5},{2,6},{3,7},{4,0},{5,1},{6,2},{7,3},{8,12},{9,13},{10,... | collective-permute-start | bytes 6291464 | tf_op jit(solution)/shard_map/ppermute | solution.py:11
  226.9 242.5 %collective-permute-start.7 = (f32[512,1024]{1,0:T(8,128)}, f32[512,1024]{1,0:T(8,128)}, u32[]{:S(2)}, u32[]{:S(2)}) collective-permute-start(f32[512,1024]{1,0:T(8,128)} %copy.47), channel_id=1, source_target_pairs={{0,8},{1,9},{2,10},{3,11},{4,12},{5,13},{6,14},{7,15},{8,0},{9,1},... | collective-permute-start | bytes 6291464 | tf_op jit(solution)/shard_map/ppermute | solution.py:11
  463.6 5.9 %copy-start.5 = (bf16[1024,256]{1,0:T(8,128)(2,1)S(1)}, bf16[1024,256]{1,0:T(8,128)(2,1)}, u32[]{:S(2)}) copy-start(bf16[1024,256]{1,0:T(8,128)(2,1)} %param.7) | copy-start | bytes 1572868
Sparse Core Ops, SparseCore 0:
  191.1 164.3 reduce-scatter.1
where the time goes:
time: 497 us; the launch traced here: 495 us
  blocking collectives  298 us (60%)
  local copies, waits for them, and re-layouts  109 us (22%)
  matrix products  60.1 us (12%)
  between operations  14.2 us (3%)
  starting transfers between devices  8.66 us (2%)
  other arithmetic  5.35 us (1%)
    psum x1, blocking collectives, on_device(): latent_grad = lax.psum(latent_term, 'mp').astype(jnp.bfloat16)  148 us
    psum x1, blocking collectives, on_device(): lax.psum(jnp.dot(tokens, left_factor, preferred_element_type=jnp.float32)...  79.3 us
    psum x1, blocking collectives, on_device(): left_sum, right_sum = lax.psum((left_part, right_part), 'dp')  71 us
    unnamed x23, local copies, waits for them, and re-layouts  20 us
    dot_general x1, matrix products, on_device(): jnp.einsum('tgh,kcgh->tgkc', grad_view, weight_view, preferred_element_ty...  13.2 us
    dot_general x1, matrix products, on_device(): jnp.einsum('tgkc,tgh->kcgh', stacked, grad_view, preferred_element_type=j...  12.9 us
    transpose x1, local copies, waits for them, and re-layouts, on_device(): jnp.einsum('tgkc,tgh->kcgh', stacked, grad_view, preferred_element_type=j...  11.9 us
    another operation x4, local copies, waits for them, and re-layouts, on_device(): piece.reshape(tok_rows, local_width)  11.6 us
  transfers between devices with their start and end apart: 9, of which 0 were waited for; matrix products, arithmetic and copies ran while one was open for 19% of the time, Pallas kernels for 0%

commit v1 on v0

v1 whole, which is shorter than its diff:
```python
import functools

import jax
import jax.numpy as jnp
from jax import lax
from jax.experimental import pallas as pl
from jax.experimental.pallas import tpu as pltpu
from jax.sharding import PartitionSpec as P

gelu_scale = 0.7978845608028654
gelu_cubic = 0.044715
f32 = jnp.float32
bf16 = jnp.bfloat16
NT = (((1,), (1,)), ((), ()))
TN = (((0,), (0,)), ((), ()))
VMEM_BYTES = 48 * 1024 * 1024


def from_partner(shard, axis, distance):
    return lax.ppermute(shard, axis, [(i, i ^ 1 << distance) for i in range(lax.axis_size(axis))])


def gelu_parts(preact):
    inner = gelu_scale * (preact + gelu_cubic * preact * preact * preact)
    tangent = jnp.tanh(inner)
    value = 0.5 * preact * (1.0 + tangent)
    slope = 0.5 * (1.0 + tangent) + 0.5 * preact * (1.0 - tangent * tangent) * gelu_scale * (
        1.0 + 3.0 * gelu_cubic * preact * preact
    )
    return (value, slope)


def params():
    return pltpu.CompilerParams(vmem_limit_bytes=VMEM_BYTES)


def cost(flops, moved, transcendentals=0):
    return pl.CostEstimate(flops=flops, bytes_accessed=moved, transcendentals=transcendentals)


def forward_body(local_taps, remote_taps, aliased, idx_ref, *refs):
    refs = list(refs)
    take = lambda n: [refs.pop(0) for _ in range(n)]
    own = take(local_taps)
    remote = take(remote_taps)
    latent_refs = take(2)
    weight_ref, right_ref, cot_ref = take(3)
    take(1 if aliased else 0)
    act_ref, grad_ref = take(2)
    terms = take(remote_taps)
    local_ref, latent_term_ref = take(2)
    group = pl.program_id(0)
    taps, block, hidden = weight_ref.shape
    weights = weight_ref[...].reshape(taps * block, hidden)
    inputs = jnp.concatenate([r[...] for r in own + remote], axis=1)
    latent = jnp.concatenate([r[0] for r in latent_refs], axis=0)
    right = right_ref[...]
    preact = jnp.dot(inputs, weights, preferred_element_type=f32)
    preact = preact + jnp.dot(latent, right, preferred_element_type=f32)
    value, slope = gelu_parts(preact)
    act_ref[...] = value.astype(bf16)
    grad = (cot_ref[...].astype(f32) * slope).astype(bf16)
    grad_ref[...] = grad
    spread = lax.dot_general(grad, weights, NT, preferred_element_type=f32)
    for k in range(remote_taps):
        lo = (local_taps + k) * block
        terms[k][...] = spread[:, lo : lo + block].astype(bf16)

    @pl.when(group == 0)
    def _():
        local_ref[...] = jnp.zeros_like(local_ref)
        latent_term_ref[...] = jnp.zeros_like(latent_term_ref)

    for k in range(local_taps):
        target = group if k == 0 else group ^ (1 << (k - 1))
        cols = pl.ds(pl.multiple_of(target * block, block), block)
        local_ref[:, cols] += spread[:, k * block : (k + 1) * block]
    latent_term_ref[...] += lax.dot_general(grad, right, NT, preferred_element_type=f32)


def forward_chunk(chunk, idx, tokens, remote, latent, weight, right, cotangent, act_before):
    rows, width = remote[0].shape
    taps, block, hidden_local = weight.shape
    groups = width // block
    hidden = hidden_local // groups
    local_taps = taps - len(remote)
    quarter, rank = latent.shape[1:]
    own_spec = lambda k: pl.BlockSpec(
        (rows, block), lambda g, idx: (chunk, g if k == 0 else g ^ (1 << (k - 1)))
    )
    latent_spec = lambda k: pl.BlockSpec((1, quarter, rank), lambda g, idx: (idx[0] ^ k, 0, 0))
    in_specs = [own_spec(k) for k in range(local_taps)]
    in_specs += [pl.BlockSpec((rows, block), lambda g, idx: (0, g))] * len(remote)
    in_specs += [latent_spec(2 * chunk), latent_spec(2 * chunk + 1)]
    in_specs += [
        pl.BlockSpec((taps, block, hidden), lambda g, idx: (0, 0, g)),
        pl.BlockSpec((rank, hidden), lambda g, idx: (0, g)),
        pl.BlockSpec((rows, hidden), lambda g, idx: (chunk, g)),
    ]
    args = [tokens] * local_taps + list(remote) + [latent, latent, weight, right, cotangent]
    aliases = {}
    if act_before is not None:
        in_specs.append(pl.BlockSpec(memory_space=pl.ANY))
        args.append(act_before)
        aliases = {len(args): 0}
    out_specs = [
        pl.BlockSpec((rows, hidden), lambda g, idx: (chunk, g)),
        pl.BlockSpec((rows, hidden), lambda g, idx: (0, g)),
    ]
    out_specs += [pl.BlockSpec((rows, block), lambda g, idx: (0, g))] * len(remote)
    out_specs += [
        pl.BlockSpec((rows, width), lambda g, idx: (0, 0)),
        pl.BlockSpec((rows, rank), lambda g, idx: (0, 0)),
    ]
    shape = jax.ShapeDtypeStruct
    out_shape = [shape(cotangent.shape, bf16), shape((rows, hidden_local), bf16)]
    out_shape += [shape((rows, width), bf16)] * len(remote)
    out_shape += [shape((rows, width), f32), shape((rows, rank), f32)]
    outs = pl.pallas_call(
        functools.partial(forward_body, local_taps, len(remote), act_before is not None),
        grid_spec=pltpu.PrefetchScalarGridSpec(
            num_scalar_prefetch=1, grid=(groups,), in_specs=in_specs, out_specs=out_specs
        ),
        out_shape=out_shape,
        input_output_aliases=aliases,
        compiler_params=params(),
        cost_estimate=cost(
            4 * rows * hidden_local * (taps * block + rank),
            2 * (weight.size + right.size + 3 * rows * hidden_local + 12 * rows * width),
            rows * hidden_local,
        ),
        name="forward_chunk",
    )(idx, *args)
    act, grad = outs[:2]
    return act, grad, outs[2 : 2 + len(remote)], outs[-2], outs[-1]


def halves_body(idx_ref, *refs):
    for src, dst in zip(refs[: len(refs) // 2], refs[len(refs) // 2 :]):
        dst[...] = src[...]


def column_halves(which, arrays, block):
    rows, width = arrays[0].shape
    half = block // 2
    return pl.pallas_call(
        halves_body,
        grid_spec=pltpu.PrefetchScalarGridSpec(
            num_scalar_prefetch=1,
            grid=(width // block,),
            in_specs=[pl.BlockSpec((rows, half), lambda j, which: (0, 2 * j + which[0]))]
            * len(arrays),
            out_specs=[pl.BlockSpec((rows, half), lambda j, which: (0, j))] * len(arrays),
        ),
        out_shape=[jax.ShapeDtypeStruct((rows, width // 2), bf16)] * len(arrays),
        compiler_params=params(),
        cost_estimate=cost(0, 2 * rows * width * len(arrays)),
        name="column_halves",
    )(which, *arrays)


def in_dp_order(idx_ref, near, far):
    first = idx_ref[1] == 0
    return jnp.concatenate([jnp.where(first, near, far), jnp.where(first, far, near)], axis=0)


def weights_body(local_taps, remote_taps, idx_ref, *refs):
    refs = list(refs)
    take = lambda n: [refs.pop(0)[...] for _ in range(n)]
    own = take(local_taps)
    remote = [jnp.concatenate(take(2), axis=0) for _ in range(remote_taps)]
    far_own = take(local_taps)
    far_remote = [jnp.concatenate(take(2), axis=0) for _ in range(remote_taps)]
    grad = jnp.concatenate(take(2), axis=0)
    far_grad = jnp.concatenate(take(2), axis=0)
    latent_ref, far_latent_ref, weight_ref, right_ref = refs
    order = [k ^ idx_ref[0] for k in range(latent_ref.shape[0])]
    latent = jnp.concatenate([latent_ref[k] for k in order], axis=0)
    far_latent = jnp.concatenate([far_latent_ref[k] for k in order], axis=0)
    near = jnp.concatenate(own + remote, axis=1)
    far = jnp.concatenate(far_own + far_remote, axis=1)
    total = lax.dot_general(near, grad, TN, preferred_element_type=f32)
    total = total + lax.dot_general(far, far_grad, TN, preferred_element_type=f32)
    weight_ref[...] = total.reshape(weight_ref.shape).astype(bf16)
    latents, grads = in_dp_order(idx_ref, latent, far_latent), in_dp_order(idx_ref, grad, far_grad)
    right = lax.dot_general(latents, grads, TN, preferred_element_type=f32)
    right_ref[...] = right.astype(bf16)


def weight_grads(idx, tokens, remote, far_tokens, far_remote, grads, latent, far_latent, taps, block):
    rows, width = tokens.shape
    chunk_rows = grads[0].shape[0]
    hidden_local = grads[0].shape[1]
    groups = width // block
    half = block // 2
    hidden = hidden_local // groups
    local_taps = taps - len(remote)
    rank = latent.shape[2]
    own_spec = lambda k: pl.BlockSpec(
        (rows, half), lambda g, idx: (0, 2 * (g if k == 0 else g ^ (1 << (k - 1))) + idx[1])
    )
    own_specs = [own_spec(k) for k in range(local_taps)]
    remote_specs = [pl.BlockSpec((chunk_rows, half), lambda g, idx: (0, 2 * g + idx[1]))] * (
        2 * len(remote)
    )
    far_specs = [pl.BlockSpec((chunk_rows, half), lambda g, idx: (0, g))] * (2 * len(remote))
    grad_specs = [pl.BlockSpec((chunk_rows, hidden), lambda g, idx: (0, g))] * 4
    latent_spec = pl.BlockSpec(latent.shape, lambda g, idx: (0, 0, 0))
    return pl.pallas_call(
        functools.partial(weights_body, local_taps, len(remote)),
        grid_spec=pltpu.PrefetchScalarGridSpec(
            num_scalar_prefetch=1,
            grid=(groups,),
            in_specs=own_specs + remote_specs + own_specs + far_specs + grad_specs + [latent_spec] * 2,
            out_specs=[
                pl.BlockSpec((taps, half, hidden), lambda g, idx: (0, 0, g)),
                pl.BlockSpec((rank, hidden), lambda g, idx: (0, g)),
            ],
        ),
        out_shape=[
            jax.ShapeDtypeStruct((taps, half, hidden_local), bf16),
            jax.ShapeDtypeStruct((rank, hidden_local), bf16),
        ],
        compiler_params=params(),
        cost_estimate=cost(
            4 * rows * hidden_local * (taps * half + rank),
            2 * (taps * half * hidden_local + 4 * rows * hidden_local + 10 * rows * width),
        ),
        name="weight_grads",
    )(
        idx,
        *([tokens] * local_taps),
        *[c for pair in remote for c in pair],
        *([far_tokens] * local_taps),
        *[c for pair in far_remote for c in pair],
        *grads,
        latent,
        far_latent,
    )


def inputs_body(n_terms, idx_ref, *refs):
    refs = list(refs)
    pair = lambda: jnp.concatenate([refs.pop(0)[...], refs.pop(0)[...]], axis=0)
    total = pair()
    for _ in range(n_terms):
        total = total + pair().astype(f32)
    tokens_ref, far_tokens_ref, left_ref, latent_ref, far_latent_ref, input_ref, left_grad_ref = refs
    order = [k ^ idx_ref[0] for k in range(latent_ref.shape[0])]
    latent = jnp.concatenate([latent_ref[k] for k in order], axis=0)
    far_latent = jnp.concatenate([far_latent_ref[k] for k in order], axis=0)
    low_rank = lax.dot_general(latent, left_ref[...], NT, preferred_element_type=f32)
    input_ref[...] = (total + low_rank).astype(bf16)
    tokens = in_dp_order(idx_ref, tokens_ref[...], far_tokens_ref[...])
    latents = in_dp_order(idx_ref, latent, far_latent)
    left = lax.dot_general(tokens, latents, TN, preferred_element_type=f32)
    left_grad_ref[...] = left.astype(bf16)


def input_grads(idx, local, terms, tokens, far_tokens, left, latent, far_latent, block):
    rows, width = tokens.shape
    rank = left.shape[1]
    chunk_rows = local[0].shape[0]
    chunk_spec = pl.BlockSpec((chunk_rows, block), lambda g, idx: (0, g))
    token_spec = pl.BlockSpec((rows, block), lambda g, idx: (0, g))
    left_spec = pl.BlockSpec((block, rank), lambda g, idx: (g, 0))
    latent_spec = pl.BlockSpec(latent.shape, lambda g, idx: (0, 0, 0))
    return pl.pallas_call(
        functools.partial(inputs_body, len(terms)),
        grid_spec=pltpu.PrefetchScalarGridSpec(
            num_scalar_prefetch=1,
            grid=(width // block,),
            in_specs=[chunk_spec] * (2 + 2 * len(terms))
            + [token_spec, token_spec, left_spec, latent_spec, latent_spec],
            out_specs=[token_spec, left_spec],
        ),
        out_shape=[
            jax.ShapeDtypeStruct(tokens.shape, bf16),
            jax.ShapeDtypeStruct(left.shape, bf16),
        ],
        compiler_params=params(),
        cost_estimate=cost(6 * rows * width * rank, 20 * rows * width),
        name="input_grads",
    )(idx, *local, *[c for pair in terms for c in pair], tokens, far_tokens, left, latent, far_latent)


def summed_over_mp(part):
    bits = lax.axis_size("mp").bit_length() - 1
    index = lax.axis_index("mp")
    for bit in range(2):
        half = part.shape[0] // 2
        mine = (index >> bit) & 1
        sent = lax.dynamic_slice_in_dim(part, (1 - mine) * half, half, 0)
        kept = lax.dynamic_slice_in_dim(part, mine * half, half, 0)
        part = kept + from_partner(sent, "mp", bit)
    for bit in range(2, bits):
        part = part + from_partner(part, "mp", bit)
    stack = part.astype(bf16)[None]
    for bit in (1, 0):
        stack = jnp.concatenate([stack, from_partner(stack, "mp", bit)], axis=0)
    return stack


def on_device(tokens, block_weight, left_factor, right_factor, out_cotangent):
    rows, width = tokens.shape
    taps, block, _ = block_weight.shape
    groups = width // block
    local_bits = groups.bit_length() - 1
    remote_bits = range(taps - 1 - local_bits)
    mp_index = lax.axis_index("mp")
    dp_index = lax.axis_index("dp")
    place = 2 * (mp_index & 1) + ((mp_index >> 1) & 1)
    idx = jnp.stack([place, dp_index]).astype(jnp.int32)
    mine = dp_index.reshape(1).astype(jnp.int32)
    theirs = 1 - mine
    half_rows = rows // 2
    chunks = [tokens[:half_rows], tokens[half_rows:]]

    received = [[from_partner(c, "mp", bit) for bit in remote_bits] for c in chunks]
    far_tokens = from_partner(tokens, "dp", 0)
    latent = summed_over_mp(jnp.dot(tokens, left_factor, preferred_element_type=f32))
    far_latent = from_partner(latent, "dp", 0)

    act, grads, far_grads, terms, local, latent_terms = None, [], [], [], [], []
    far_received = []
    for chunk in range(2):
        sent = column_halves(theirs, received[chunk][2:], block)
        far_received.append([from_partner(c, "dp", 0) for c in sent])
        act, grad, out_terms, local_sum, latent_term = forward_chunk(
            chunk, idx, tokens, received[chunk], latent, block_weight, right_factor, out_cotangent, act
        )
        terms.append([from_partner(t, "mp", bit) for bit, t in zip(remote_bits, out_terms)])
        far_grads.append(from_partner(grad, "dp", 0))
        grads.append(grad)
        local.append(local_sum)
        latent_terms.append(latent_term)
    far_half = column_halves(mine, [far_tokens], block)[0]
    far_low = [from_partner(far_half, "mp", bit) for bit in remote_bits[:2]]
    far_low = [[c[:half_rows], c[half_rows:]] for c in far_low]
    far_pairs = far_low + [list(p) for p in zip(*far_received)]

    latent_grad = summed_over_mp(jnp.concatenate(latent_terms, axis=0))
    far_latent_grad = from_partner(latent_grad, "dp", 0)
    weight_grad, right_grad = weight_grads(
        idx,
        tokens,
        list(zip(*received)),
        far_tokens,
        far_pairs,
        grads + far_grads,
        latent,
        far_latent,
        taps,
        block,
    )
    input_grad, left_grad = input_grads(
        idx,
        local,
        list(zip(*terms)),
        tokens,
        far_tokens,
        left_factor,
        latent_grad,
        far_latent_grad,
        block,
    )
    return act, input_grad, weight_grad, left_grad, right_grad


def flip_groups(blocks, distance):
    full_shape = blocks.shape
    group_count = full_shape[1]
    split_view = blocks.reshape(
        (full_shape[0], group_count // (2 * distance), 2, distance) + full_shape[2:]
    )
    return jnp.flip(split_view, axis=2).reshape(full_shape)


def on_device_general(tokens, block_weight, left_factor, right_factor, out_cotangent):
    tok_rows = tokens.shape[0]
    local_width = tokens.shape[1]
    tap_count = block_weight.shape[0]
    block_size = block_weight.shape[1]
    hidden_local = block_weight.shape[2]
    group_count = local_width // block_size
    local_bits = group_count.bit_length() - 1
    tok_blocks = tokens.reshape(tok_rows, group_count, block_size)
    tap_inputs = [tok_blocks]
    for tap_index in range(1, tap_count):
        level_bit = tap_index - 1
        if level_bit < local_bits:
            tap_inputs.append(flip_groups(tok_blocks, 1 << level_bit))
        else:
            partner = from_partner(tokens, "mp", level_bit - local_bits)
            tap_inputs.append(partner.reshape(tok_rows, group_count, block_size))
    stacked = jnp.stack(tap_inputs, axis=2)
    weight_view = block_weight.reshape(tap_count, block_size, group_count, 2 * block_size)
    butterfly = jnp.einsum("tgkc,kcgh->tgh", stacked, weight_view, preferred_element_type=f32)
    butterfly = butterfly.reshape(tok_rows, hidden_local)
    latent = lax.psum(jnp.dot(tokens, left_factor, preferred_element_type=f32), "mp")
    latent_bf = latent.astype(bf16)
    preact = butterfly + jnp.dot(latent_bf, right_factor, preferred_element_type=f32)
    value, slope = gelu_parts(preact)
    activated = value.astype(bf16)
    grad_pre = (out_cotangent.astype(f32) * slope).astype(bf16)
    latent_term = lax.dot_general(grad_pre, right_factor, NT, preferred_element_type=f32)
    latent_grad = lax.psum(latent_term, "mp").astype(bf16)
    left_part = lax.dot_general(tokens, latent_grad, TN, preferred_element_type=f32)
    right_part = lax.dot_general(latent_bf, grad_pre, TN, preferred_element_type=f32)
    left_sum, right_sum = lax.psum((left_part, right_part), "dp")
    grad_view = grad_pre.reshape(tok_rows, group_count, 2 * block_size)
    spread = jnp.einsum("tgh,kcgh->tgkc", grad_view, weight_view, preferred_element_type=f32)
    input_sum = spread[:, :, 0]
    for tap_index in range(1, tap_count):
        level_bit = tap_index - 1
        piece = spread[:, :, tap_index]
        if level_bit < local_bits:
            input_sum = input_sum + flip_groups(piece, 1 << level_bit)
        else:
            returned = from_partner(
                piece.reshape(tok_rows, local_width), "mp", level_bit - local_bits
            )
            input_sum = input_sum + returned.reshape(tok_rows, group_count, block_size)
    low_rank = lax.dot_general(latent_grad, left_factor, NT, preferred_element_type=f32)
    input_grad = (input_sum.reshape(tok_rows, local_width) + low_rank).astype(bf16)
    partial_value = jnp.einsum("tgkc,tgh->kcgh", stacked, grad_view, preferred_element_type=f32)
    partial_value = partial_value.reshape(tap_count, block_size, hidden_local)
    weight_grad = lax.psum_scatter(partial_value, "dp", scatter_dimension=1, tiled=True).astype(bf16)
    return (activated, input_grad, weight_grad, left_sum.astype(bf16), right_sum.astype(bf16))


def solution(mesh):
    pairs = mesh.shape["dp"] == 2 and mesh.shape["mp"] >= 4
    return jax.shard_map(
        on_device if pairs else on_device_general,
        mesh=mesh,
        in_specs=(P("dp", "mp"), P(None, None, "mp"), P("mp", None), P(None, "mp"), P("dp", "mp")),
        out_specs=(P("dp", "mp"), P("dp", "mp"), P(None, "dp", "mp"), P("mp", None), P(None, "mp")),
        check_vma=False,
    )
```

time: 497 us -> 217 us (0.44)
  blocking collectives: 298 us -> 0 us
  waiting for transfers between devices: 0.04 us -> 130 us
  local copies, waits for them, and re-layouts: 109 us -> 2.46 us
  matrix products: 60.1 us -> 1.8 us
  Pallas kernels: 0 us -> 40.8 us
  starting transfers between devices: 8.66 us -> 39.9 us
  between operations: 14.2 us -> 1.01 us
  other arithmetic: 5.35 us -> 0.34 us
    psum x3 -> x0, blocking collectives: 298 us -> none  [the longest x1 148 us: on_device(): latent_grad = lax.psum(latent_term, 'mp').astype(jnp.bfloat16)]
    ppermute x8 -> x39, waiting for transfers between devices: 0.02 us -> 130 us  [from_partner(): lax.ppermute(shard, axis, [(i, i ^ 1 << distance) for i in range(lax.axis...]
    dot_general x9 -> x1, matrix products: 60.1 us -> 1.8 us  [on_device(): jnp.dot(tokens, left_factor, preferred_element_type=f32)]
    pallas_call x0 -> x7, Pallas kernels: none -> 40.8 us  [the longest x2 24.3 us: forward_chunk(): pl.pallas_call(functools.partial(forward_body, local_taps, len(remote), a...]
    another operation x14 -> x0, local copies, waits for them, and re-layouts: 32.1 us -> none  [the longest x4 11.6 us: on_device(): piece.reshape(tok_rows, local_width)]
    ppermute x8 -> x39, starting transfers between devices: 8.62 us -> 39.9 us  [from_partner(): lax.ppermute(shard, axis, [(i, i ^ 1 << distance) for i in range(lax.axis...]
    reshape x5 -> x0, local copies, waits for them, and re-layouts: 20.1 us -> none  [the longest x2 8.77 us: on_device(): grad_view = grad_pre.reshape(tok_rows, group_count, 2 * block_size)]
    unnamed x23 -> x29, local copies, waits for them, and re-layouts: 20 us -> 1.02 us
  transfers between devices with their start and end apart: 9 -> 39, of which waited for: 0 -> 21; matrix products, arithmetic and copies ran while one was open for 19% -> 1% of each run, Pallas kernels for 0% -> 16%
where the time goes in v1:
time: 217 us
  waiting for transfers between devices  130 us (60%)
  Pallas kernels  40.8 us (19%)
  starting transfers between devices  39.9 us (18%)
  local copies, waits for them, and re-layouts  2.46 us (1%)
    ppermute x39, waiting for transfers between devices, from_partner(): lax.ppermute(shard, axis, [(i, i ^ 1 << distance) for i in range(lax.axis...  130 us
    ppermute x39, starting transfers between devices, from_partner(): lax.ppermute(shard, axis, [(i, i ^ 1 << distance) for i in range(lax.axis...  39.9 us
    pallas_call x2, Pallas kernels, forward_chunk(): pl.pallas_call(functools.partial(forward_body, local_taps, len(remote), a...  24.3 us
    pallas_call x1, Pallas kernels, weight_grads(): pl.pallas_call(functools.partial(weights_body, local_taps, len(remote)),...  9.9 us
    pallas_call x1, Pallas kernels, input_grads(): pl.pallas_call(functools.partial(inputs_body, len(terms)), grid_spec=pltp...  5.37 us
  transfers between devices with their start and end apart: 39, of which 21 were waited for; matrix products, arithmetic and copies ran while one was open for 1% of the time, Pallas kernels for 16%

profile of v1, /device:TPU:0, one launch (start us, length us, event | category | flops | bytes accessed | tf_op | source)
XLA Modules:
  0.0 216.7 jit_solution(2020074015692569365)
XLA Ops:
  0.6 1.8 fusion.5
  2.5 0.5 collective-permute-start.4
  3.0 1.2 collective-permute-done.4
  4.2 3.0 %collective-permute-start.5 = (f32[128,256]{1,0:T(8,128)S(1)}, f32[128,256]{1,0:T(8,128)S(1)}, u32[]{:S(2)}, u32[]{:S(2)}) collective-permute-start(f32[128,256]{1,0:T(8,128)S(1)} %constant_dynamic-slice_fusion.2), channel_id=1, source_target_pairs={{0,2},{1,3},{2,0},{3,1},{4,6},{5,7},{6,4},{7,5},{8,10},{9,11},{10,... | collective-permute-start | bytes 393224 | tf_op jit(solution)/shard_map/ppermute | solution.py:20
  7.2 3.8 %collective-permute-done.5 = f32[128,256]{1,0:T(8,128)S(1)} collective-permute-done((f32[128,256]{1,0:T(8,128)S(1)}, f32[128,256]{1,0:T(8,128)S(1)}, u32[]{:S(2)}, u32[]{:S(2)}) %collective-permute-start.5) | collective-permute-done | bytes 131104 | tf_op jit(solution)/shard_map/ppermute | solution.py:20
  11.0 1.9 collective-permute-start.6
  12.9 3.2 %collective-permute-done.6 = f32[128,256]{1,0:T(8,128)S(1)} collective-permute-done((f32[128,256]{1,0:T(8,128)S(1)}, f32[128,256]{1,0:T(8,128)S(1)}, u32[]{:S(2)}, u32[]{:S(2)}) %collective-permute-start.6) | collective-permute-done | bytes 131104 | tf_op jit(solution)/shard_map/ppermute | solution.py:20
  16.1 2.8 %collective-permute-start.7 = (f32[128,256]{1,0:T(8,128)S(1)}, f32[128,256]{1,0:T(8,128)S(1)}, u32[]{:S(2)}, u32[]{:S(2)}) collective-permute-start(f32[128,256]{1,0:T(8,128)S(1)} %add.50), channel_id=1, source_target_pairs={{0,8},{1,9},{2,10},{3,11},{4,12},{5,13},{6,14},{7,15},{8,0},{9,1},... | collective-permute-start | bytes 393224 | tf_op jit(solution)/shard_map/ppermute | solution.py:20
  18.9 1.3 fusion.2
  20.3 1.6 collective-permute-start.11
  21.9 1.6 collective-permute-start.12
  24.0 1.2 collective-permute-start.8
  25.2 10.8 %collective-permute-done.8 = bf16[1,128,256]{2,1,0:T(8,128)(2,1)S(1)} collective-permute-done((bf16[1,128,256]{2,1,0:T(8,128)(2,1)S(1)}, bf16[1,128,256]{2,1,0:T(8,128)(2,1)S(1)}, u32[]{:S(2)}, u32[]{:S(2)}) %collective-permute-start.8) | collective-permute-done | bytes 65568 | tf_op jit(solution)/shard_map/ppermute | solution.py:20
  36.7 1.5 collective-permute-start.1
  38.2 6.5 %collective-permute-done.12.refs_5_.refs_0_.refs_7_ = bf16[256,1024]{1,0:T(8,128)(2,1)S(1)} collective-permute-done((bf16[256,1024]{1,0:T(8,128)(2,1)S(1)}, bf16[256,1024]{1,0:T(8,128)(2,1)S(1)}, u32[]{:S(2)}, u32[]{:S(2)}) %collective-permute-start.12) | collective-permute-done | bytes 524320 | tf_op jit(solution)/shard_map/ppermute | solution.py:20
  44.7 5.4 %collective-permute-start.3 = (bf16[256,1024]{1,0:T(8,128)(2,1)S(1)}, bf16[256,1024]{1,0:T(8,128)(2,1)S(1)}, u32[]{:S(2)}, u32[]{:S(2)}) collective-permute-start(bf16[256,1024]{1,0:T(8,128)(2,1)S(1)} %get-tuple-element.54), channel_id=1, source_target_pairs={{0,8},{1,9},{2,10},{3,11},{4,12},{5,13},{6,14},{7,15},{8,0},{9,1},... | collective-permute-start | bytes 1572872 | tf_op jit(solution)/shard_map/ppermute | solution.py:20
  50.2 1.6 collective-permute-start.22
  51.7 12.2 %forward_chunk.2 = (bf16[512,2048]{1,0:T(8,128)(2,1)}, bf16[256,2048]{1,0:T(8,128)(2,1)S(1)}, bf16[256,1024]{1,0:T(8,128)(2,1)S(1)}, bf16[256,1024]{1,0:T(8,128)...) custom-call(s32[2]{0:T(128)S(1)} %pad_add_fusion.idx_ref, ...), custom_call_target="tpu_custom_call" | custom-call | flops 4294967296 | bytes 17825792 | tf_op jit(solution)/shard_map/forward_chunk/pallas_call | solution.py:119
  64.0 7.3 %collective-permute-done.2.refs_5_.refs_0_.refs_8_ = bf16[256,1024]{1,0:T(8,128)(2,1)S(1)} collective-permute-done((bf16[256,1024]{1,0:T(8,128)(2,1)S(1)}, bf16[256,1024]{1,0:T(8,128)(2,1)S(1)}, u32[]{:S(2)}, u32[]{:S(2)}) %collective-permute-start.2) | collective-permute-done | bytes 524320 | tf_op jit(solution)/shard_map/ppermute | solution.py:20
  71.3 2.0 collective-permute-done.3.refs_6_.refs_1_.refs_10_
  73.3 12.2 %forward_chunk.3 = (bf16[512,2048]{1,0:T(8,128)(2,1)}, bf16[256,2048]{1,0:T(8,128)(2,1)S(1)}, bf16[256,1024]{1,0:T(8,128)(2,1)S(1)}, bf16[256,1024]{1,0:T(8,128)...) custom-call(s32[2]{0:T(128)S(1)} %pad_add_fusion.idx_ref, ...), custom_call_target="tpu_custom_call", output_to_operand_aliasing={{0}: (13, {})} | custom-call | flops 4294967296 | bytes 17825792 | tf_op jit(solution)/shard_map/forward_chunk/pallas_call | solution.py:119
  86.0 1.6 collective-permute-start.32
  88.0 0.6 collective-permute-start.33
  88.6 1.5 collective-permute-start.34
  90.3 4.9 %collective-permute-done.32.refs_18_ = bf16[256,512]{1,0:T(8,128)(2,1)S(1)} collective-permute-done((bf16[256,512]{1,0:T(8,128)(2,1)S(1)}, bf16[256,512]{1,0:T(8,128)(2,1)S(1)}, u32[]{:S(2)}, u32[]{:S(2)}) %collective-permute-start.32) | collective-permute-done | bytes 262176 | tf_op jit(solution)/shard_map/ppermute | solution.py:20
  95.2 5.6 %collective-permute-done.33.refs_19_ = bf16[256,512]{1,0:T(8,128)(2,1)S(1)} collective-permute-done((bf16[256,512]{1,0:T(8,128)(2,1)S(1)}, bf16[256,512]{1,0:T(8,128)(2,1)S(1)}, u32[]{:S(2)}, u32[]{:S(2)}) %collective-permute-start.33) | collective-permute-done | bytes 262176 | tf_op jit(solution)/shard_map/ppermute | solution.py:20
  100.8 1.5 collective-permute-start.35
  102.3 4.1 %collective-permute-done.34.refs_20_ = bf16[256,512]{1,0:T(8,128)(2,1)S(1)} collective-permute-done((bf16[256,512]{1,0:T(8,128)(2,1)S(1)}, bf16[256,512]{1,0:T(8,128)(2,1)S(1)}, u32[]{:S(2)}, u32[]{:S(2)}) %collective-permute-start.34) | collective-permute-done | bytes 262176 | tf_op jit(solution)/shard_map/ppermute | solution.py:20
  106.4 1.5 collective-permute-start.38
  108.8 3.3 %collective-permute-done.35.refs_21_ = bf16[256,512]{1,0:T(8,128)(2,1)S(1)} collective-permute-done((bf16[256,512]{1,0:T(8,128)(2,1)S(1)}, bf16[256,512]{1,0:T(8,128)(2,1)S(1)}, u32[]{:S(2)}, u32[]{:S(2)}) %collective-permute-start.35) | collective-permute-done | bytes 262176 | tf_op jit(solution)/shard_map/ppermute | solution.py:20
  112.1 1.9 collective-permute-done.25
  114.0 0.5 collective-permute-start.36
  114.5 3.2 %collective-permute-done.38.refs_27_ = bf16[4,128,256]{2,1,0:T(8,128)(2,1)S(1)} collective-permute-done((bf16[4,128,256]{2,1,0:T(8,128)(2,1)S(1)}, bf16[4,128,256]{2,1,0:T(8,128)(2,1)S(1)}, u32[]{:S(2)}, u32[]{:S(2)}) %collective-permute-start.38) | collective-permute-done | bytes 262176 | tf_op jit(solution)/shard_map/ppermute | solution.py:20
  117.7 1.6 collective-permute-start.37
  119.3 6.5 %collective-permute-done.26 = f32[128,256]{1,0:T(8,128)S(1)} collective-permute-done((f32[128,256]{1,0:T(8,128)S(1)}, f32[128,256]{1,0:T(8,128)S(1)}, u32[]{:S(2)}, u32[]{:S(2)}) %collective-permute-start.26) | collective-permute-done | bytes 131104 | tf_op jit(solution)/shard_map/ppermute | solution.py:20
  125.8 2.1 collective-permute-start.27
  127.9 12.9 %collective-permute-done.27 = bf16[1,128,256]{2,1,0:T(8,128)(2,1)S(1)} collective-permute-done((bf16[1,128,256]{2,1,0:T(8,128)(2,1)S(1)}, bf16[1,128,256]{2,1,0:T(8,128)(2,1)S(1)}, u32[]{:S(2)}, u32[]{:S(2)}) %collective-permute-start.27) | collective-permute-done | bytes 65568 | tf_op jit(solution)/shard_map/ppermute | solution.py:20
  141.1 1.8 collective-permute-start.17
  143.1 12.6 %collective-permute-done.16.refs_4_ = bf16[256,1024]{1,0:T(8,128)(2,1)S(1)} collective-permute-done((bf16[256,1024]{1,0:T(8,128)(2,1)S(1)}, bf16[256,1024]{1,0:T(8,128)(2,1)S(1)}, u32[]{:S(2)}, u32[]{:S(2)}) %collective-permute-start.16) | collective-permute-done | bytes 524320 | tf_op jit(solution)/shard_map/ppermute | solution.py:20
  155.7 9.1 %collective-permute-done.17.refs_5_ = bf16[256,1024]{1,0:T(8,128)(2,1)S(1)} collective-permute-done((bf16[256,1024]{1,0:T(8,128)(2,1)S(1)}, bf16[256,1024]{1,0:T(8,128)(2,1)S(1)}, u32[]{:S(2)}, u32[]{:S(2)}) %collective-permute-start.17) | collective-permute-done | bytes 524320 | tf_op jit(solution)/shard_map/ppermute | solution.py:20
  164.8 2.4 %collective-permute-start.20 = (bf16[256,1024]{1,0:T(8,128)(2,1)S(1)}, bf16[256,1024]{1,0:T(8,128)(2,1)S(1)}, u32[]{:S(2)}, u32[]{:S(2)}) collective-permute-start(bf16[256,1024]{1,0:T(8,128)(2,1)S(1)} %get-tuple-element.39), channel_id=1, source_target_pairs={{0,8},{1,9},{2,10},{3,11},{4,12},{5,13},{6,14},{7,15},{8,0},{9,1},... | collective-permute-start | bytes 1572872 | tf_op jit(solution)/shard_map/ppermute | solution.py:20
  167.8 1.6 collective-permute-start.29
  169.4 0.9 copy-done.7
  170.3 9.9 %weight_grads.1 = (bf16[7,128,2048]{2,1,0:T(8,128)(2,1)}, bf16[256,2048]{1,0:T(8,128)(2,1)}) custom-call(s32[2]{0:T(128)S(1)} %pad_add_fusion.idx_ref, bf16[512,1024]{1,0:T(8,128)(2,1)} %refs_2_.5, bf16[512,1024]{1,0:T(8,128)(2,1)} %refs_2_.5, bf16[512,1024]{1,0:T(8,128)(2,1)} %refs_2_.5, bf16[256,1024]{1,0:T(8,128)(2,1)S(1)} %collective-permute-done.10.refs_3_, ...), custom_call_target="tpu_custom_call" | custom-call | flops 4831838208 | bytes 22544384 | tf_op jit(solution)/shard_map/weight_grads/pallas_call | solution.py:209
  180.2 7.1 %collective-permute-done.19.refs_7_ = bf16[256,1024]{1,0:T(8,128)(2,1)S(1)} collective-permute-done((bf16[256,1024]{1,0:T(8,128)(2,1)S(1)}, bf16[256,1024]{1,0:T(8,128)(2,1)S(1)}, u32[]{:S(2)}, u32[]{:S(2)}) %collective-permute-start.19) | collective-permute-done | bytes 524320 | tf_op jit(solution)/shard_map/ppermute | solution.py:20
  187.4 15.7 %collective-permute-done.20.refs_8_ = bf16[256,1024]{1,0:T(8,128)(2,1)S(1)} collective-permute-done((bf16[256,1024]{1,0:T(8,128)(2,1)S(1)}, bf16[256,1024]{1,0:T(8,128)(2,1)S(1)}, u32[]{:S(2)}, u32[]{:S(2)}) %collective-permute-start.20) | collective-permute-done | bytes 524320 | tf_op jit(solution)/shard_map/ppermute | solution.py:20
  203.0 8.2 %collective-permute-done.21.refs_9_ = bf16[256,1024]{1,0:T(8,128)(2,1)S(1)} collective-permute-done((bf16[256,1024]{1,0:T(8,128)(2,1)S(1)}, bf16[256,1024]{1,0:T(8,128)(2,1)S(1)}, u32[]{:S(2)}, u32[]{:S(2)}) %collective-permute-start.21) | collective-permute-done | bytes 524320 | tf_op jit(solution)/shard_map/ppermute | solution.py:20
  211.3 5.4 %input_grads.1 = (bf16[512,1024]{1,0:T(8,128)(2,1)}, bf16[1024,256]{1,0:T(8,128)(2,1)}) custom-call(s32[2]{0:T(128)S(1)} %pad_add_fusion.idx_ref, f32[256,1024]{1,0:T(8,128)} %get-tuple-element.31.refs_0_, f32[256,1024]{1,0:T(8,128)} %get-tuple-element.32.refs_1_, bf16[256,1024]{1,0:T(8,128)(2,1)S(1)} %collective-permute-done.14.refs_2_, ...), custom_call_target="tpu_custom_call" | custom-call | flops 805306368 | bytes 10485760 | tf_op jit(solution)/shard_map/input_grads/pallas_call | solution.py:268
  (88 shorter events, 4.5 us)
Async XLA Ops:
  2.5 1.7 collective-permute-start.4
  4.2 6.8 %collective-permute-start.5 = (f32[128,256]{1,0:T(8,128)S(1)}, f32[128,256]{1,0:T(8,128)S(1)}, u32[]{:S(2)}, u32[]{:S(2)}) collective-permute-start(f32[128,256]{1,0:T(8,128)S(1)} %constant_dynamic-slice_fusion.2), channel_id=1, source_target_pairs={{0,2},{1,3},{2,0},{3,1},{4,6},{5,7},{6,4},{7,5},{8,10},{9,11},{10,... | collective-permute-start | bytes 393224 | tf_op jit(solution)/shard_map/ppermute | solution.py:20
  11.0 5.1 %collective-permute-start.6 = (f32[128,256]{1,0:T(8,128)S(1)}, f32[128,256]{1,0:T(8,128)S(1)}, u32[]{:S(2)}, u32[]{:S(2)}) collective-permute-start(f32[128,256]{1,0:T(8,128)S(1)} %dynamic-slice_add_fusion.3), channel_id=1, source_target_pairs={{0,4},{1,5},{2,6},{3,7},{4,0},{5,1},{6,2},{7,3},{8,12},{9,13},{10,... | collective-permute-start | bytes 393224 | tf_op jit(solution)/shard_map/ppermute | solution.py:20
  16.1 7.9 %collective-permute-start.7 = (f32[128,256]{1,0:T(8,128)S(1)}, f32[128,256]{1,0:T(8,128)S(1)}, u32[]{:S(2)}, u32[]{:S(2)}) collective-permute-start(f32[128,256]{1,0:T(8,128)S(1)} %add.50), channel_id=1, source_target_pairs={{0,8},{1,9},{2,10},{3,11},{4,12},{5,13},{6,14},{7,15},{8,0},{9,1},... | collective-permute-start | bytes 393224 | tf_op jit(solution)/shard_map/ppermute | solution.py:20
  20.2 16.0 %collective-permute-start.10 = (bf16[256,1024]{1,0:T(8,128)(2,1)S(1)}, bf16[256,1024]{1,0:T(8,128)(2,1)S(1)}, u32[]{:S(2)}, u32[]{:S(2)}) collective-permute-start(bf16[256,1024]{1,0:T(8,128)(2,1)S(1)} %get-tuple-element.53), channel_id=1, source_target_pairs={{0,1},{1,0},{2,3},{3,2},{4,5},{5,4},{6,7},{7,6},{8,9},{9,8},{10,11... | collective-permute-start | bytes 1572872 | tf_op jit(solution)/shard_map/ppermute | solution.py:20
  20.3 16.4 %collective-permute-start.11 = (bf16[256,1024]{1,0:T(8,128)(2,1)S(1)}, bf16[256,1024]{1,0:T(8,128)(2,1)S(1)}, u32[]{:S(2)}, u32[]{:S(2)}) collective-permute-start(bf16[256,1024]{1,0:T(8,128)(2,1)S(1)} %get-tuple-element.53), channel_id=1, source_target_pairs={{0,2},{1,3},{2,0},{3,1},{4,6},{5,7},{6,4},{7,5},{8,10},{9,11},{10,... | collective-permute-start | bytes 1572872 | tf_op jit(solution)/shard_map/ppermute | solution.py:20
  21.9 22.9 %collective-permute-start.12 = (bf16[256,1024]{1,0:T(8,128)(2,1)S(1)}, bf16[256,1024]{1,0:T(8,128)(2,1)S(1)}, u32[]{:S(2)}, u32[]{:S(2)}) collective-permute-start(bf16[256,1024]{1,0:T(8,128)(2,1)S(1)} %get-tuple-element.53), channel_id=1, source_target_pairs={{0,4},{1,5},{2,6},{3,7},{4,0},{5,1},{6,2},{7,3},{8,12},{9,13},{10,... | collective-permute-start | bytes 1572872 | tf_op jit(solution)/shard_map/ppermute | solution.py:20
  23.4 26.7 %collective-permute-start.13 = (bf16[256,1024]{1,0:T(8,128)(2,1)S(1)}, bf16[256,1024]{1,0:T(8,128)(2,1)S(1)}, u32[]{:S(2)}, u32[]{:S(2)}) collective-permute-start(bf16[256,1024]{1,0:T(8,128)(2,1)S(1)} %get-tuple-element.53), channel_id=1, source_target_pairs={{0,8},{1,9},{2,10},{3,11},{4,12},{5,13},{6,14},{7,15},{8,0},{9,1},... | collective-permute-start | bytes 1572872 | tf_op jit(solution)/shard_map/ppermute | solution.py:20
  24.0 12.0 %collective-permute-start.8 = (bf16[1,128,256]{2,1,0:T(8,128)(2,1)S(1)}, bf16[1,128,256]{2,1,0:T(8,128)(2,1)S(1)}, u32[]{:S(2)}, u32[]{:S(2)}) collective-permute-start(bf16[1,128,256]{2,1,0:T(8,128)(2,1)S(1)} %fusion), channel_id=1, source_target_pairs={{0,2},{1,3},{2,0},{3,1},{4,6},{5,7},{6,4},{7,5},{8,10},{9,11},{10,... | collective-permute-start | bytes 196616 | tf_op jit(solution)/shard_map/ppermute | solution.py:20
  36.0 8.7 %collective-permute-start.9 = (bf16[2,128,256]{2,1,0:T(8,128)(2,1)S(1)}, bf16[2,128,256]{2,1,0:T(8,128)(2,1)S(1)}, u32[]{:S(2)}, u32[]{:S(2)}) collective-permute-start(bf16[2,128,256]{2,1,0:T(8,128)(2,1)S(1)} %pad_maximum_fusion.2), channel_id=1, source_target_pairs={{0,1},{1,0},{2,3},{3,2},{4,5},{5,4},{6,7},{7,6},{8,9},{9,8},{10,11... | collective-permute-start | bytes 393224 | tf_op jit(solution)/shard_map/ppermute | solution.py:20
  36.2 27.7 %collective-permute-start = (bf16[256,1024]{1,0:T(8,128)(2,1)S(1)}, bf16[256,1024]{1,0:T(8,128)(2,1)S(1)}, u32[]{:S(2)}, u32[]{:S(2)}) collective-permute-start(bf16[256,1024]{1,0:T(8,128)(2,1)S(1)} %get-tuple-element.54), channel_id=1, source_target_pairs={{0,1},{1,0},{2,3},{3,2},{4,5},{5,4},{6,7},{7,6},{8,9},{9,8},{10,11... | collective-permute-start | bytes 1572872 | tf_op jit(solution)/shard_map/ppermute | solution.py:20
  36.7 27.3 %collective-permute-start.1 = (bf16[256,1024]{1,0:T(8,128)(2,1)S(1)}, bf16[256,1024]{1,0:T(8,128)(2,1)S(1)}, u32[]{:S(2)}, u32[]{:S(2)}) collective-permute-start(bf16[256,1024]{1,0:T(8,128)(2,1)S(1)} %get-tuple-element.54), channel_id=1, source_target_pairs={{0,2},{1,3},{2,0},{3,1},{4,6},{5,7},{6,4},{7,5},{8,10},{9,11},{10,... | collective-permute-start | bytes 1572872 | tf_op jit(solution)/shard_map/ppermute | solution.py:20
  44.7 26.5 %collective-permute-start.2 = (bf16[256,1024]{1,0:T(8,128)(2,1)S(1)}, bf16[256,1024]{1,0:T(8,128)(2,1)S(1)}, u32[]{:S(2)}, u32[]{:S(2)}) collective-permute-start(bf16[256,1024]{1,0:T(8,128)(2,1)S(1)} %get-tuple-element.54), channel_id=1, source_target_pairs={{0,4},{1,5},{2,6},{3,7},{4,0},{5,1},{6,2},{7,3},{8,12},{9,13},{10,... | collective-permute-start | bytes 1572872 | tf_op jit(solution)/shard_map/ppermute | solution.py:20
  44.7 28.5 %collective-permute-start.3 = (bf16[256,1024]{1,0:T(8,128)(2,1)S(1)}, bf16[256,1024]{1,0:T(8,128)(2,1)S(1)}, u32[]{:S(2)}, u32[]{:S(2)}) collective-permute-start(bf16[256,1024]{1,0:T(8,128)(2,1)S(1)} %get-tuple-element.54), channel_id=1, source_target_pairs={{0,8},{1,9},{2,10},{3,11},{4,12},{5,13},{6,14},{7,15},{8,0},{9,1},... | collective-permute-start | bytes 1572872 | tf_op jit(solution)/shard_map/ppermute | solution.py:20
  50.2 35.4 %copy-start.1 = (bf16[256,1024]{1,0:T(8,128)(2,1)}, bf16[256,1024]{1,0:T(8,128)(2,1)S(1)}, u32[]{:S(2)}) copy-start(bf16[256,1024]{1,0:T(8,128)(2,1)S(1)} %collective-permute-done.13.refs_6_.refs_1_.refs_9_) | copy-start | bytes 1572868
  50.2 57.8 %collective-permute-start.22 = (bf16[512,1024]{1,0:T(8,128)(2,1)}, bf16[512,1024]{1,0:T(8,128)(2,1)S(1)}, u32[]{:S(2)}, u32[]{:S(2)}) collective-permute-start(bf16[512,1024]{1,0:T(8,128)(2,1)} %refs_2_.5), channel_id=1, source_target_pairs={{0,16},{16,0},{1,17},{17,1},{2,18},{18,2},{3,19},{19,3},{4,20},{20... | collective-permute-start | bytes 3145736 | tf_op jit(solution)/shard_map/ppermute | solution.py:20
  63.9 50.0 %copy-start.4 = (bf16[256,2048]{1,0:T(8,128)(2,1)}, bf16[256,2048]{1,0:T(8,128)(2,1)S(1)}, u32[]{:S(2)}) copy-start(bf16[256,2048]{1,0:T(8,128)(2,1)S(1)} %get-tuple-element.48.refs_22_) | copy-start | bytes 3145732
  85.4 32.3 %copy-start.5 = (bf16[256,2048]{1,0:T(8,128)(2,1)}, bf16[256,2048]{1,0:T(8,128)(2,1)S(1)}, u32[]{:S(2)}) copy-start(bf16[256,2048]{1,0:T(8,128)(2,1)S(1)} %get-tuple-element.49.refs_23_) | copy-start | bytes 3145732
  85.5 4.6 %collective-permute-start.23 = (f32[256,256]{1,0:T(8,128)S(1)}, f32[256,256]{1,0:T(8,128)S(1)}, u32[]{:S(2)}, u32[]{:S(2)}) collective-permute-start(f32[256,256]{1,0:T(8,128)S(1)} %constant_dynamic-slice_fusion.1), channel_id=1, source_target_pairs={{0,1},{1,0},{2,3},{3,2},{4,5},{5,4},{6,7},{7,6},{8,9},{9,8},{10,11... | collective-permute-start | bytes 786440 | tf_op jit(solution)/shard_map/ppermute | solution.py:20
  86.0 9.2 %collective-permute-start.32 = (bf16[256,512]{1,0:T(8,128)(2,1)S(1)}, bf16[256,512]{1,0:T(8,128)(2,1)S(1)}, u32[]{:S(2)}, u32[]{:S(2)}) collective-permute-start(bf16[256,512]{1,0:T(8,128)(2,1)S(1)} %get-tuple-element.44), channel_id=1, source_target_pairs={{0,16},{16,0},{1,17},{17,1},{2,18},{18,2},{3,19},{19,3},{4,20},{20... | collective-permute-start | bytes 786440 | tf_op jit(solution)/shard_map/ppermute | solution.py:20
  88.0 12.8 %collective-permute-start.33 = (bf16[256,512]{1,0:T(8,128)(2,1)S(1)}, bf16[256,512]{1,0:T(8,128)(2,1)S(1)}, u32[]{:S(2)}, u32[]{:S(2)}) collective-permute-start(bf16[256,512]{1,0:T(8,128)(2,1)S(1)} %get-tuple-element.45), channel_id=1, source_target_pairs={{0,16},{16,0},{1,17},{17,1},{2,18},{18,2},{3,19},{19,3},{4,20},{20... | collective-permute-start | bytes 786440 | tf_op jit(solution)/shard_map/ppermute | solution.py:20
  88.6 17.8 %collective-permute-start.34 = (bf16[256,512]{1,0:T(8,128)(2,1)S(1)}, bf16[256,512]{1,0:T(8,128)(2,1)S(1)}, u32[]{:S(2)}, u32[]{:S(2)}) collective-permute-start(bf16[256,512]{1,0:T(8,128)(2,1)S(1)} %get-tuple-element.46), channel_id=1, source_target_pairs={{0,16},{16,0},{1,17},{17,1},{2,18},{18,2},{3,19},{19,3},{4,20},{20... | collective-permute-start | bytes 786440 | tf_op jit(solution)/shard_map/ppermute | solution.py:20
  90.2 17.8 %collective-permute-start.24 = (f32[128,256]{1,0:T(8,128)S(1)}, f32[128,256]{1,0:T(8,128)S(1)}, u32[]{:S(2)}, u32[]{:S(2)}) collective-permute-start(f32[128,256]{1,0:T(8,128)S(1)} %constant_dynamic-slice_fusion), channel_id=1, source_target_pairs={{0,2},{1,3},{2,0},{3,1},{4,6},{5,7},{6,4},{7,5},{8,10},{9,11},{10,... | collective-permute-start | bytes 393224 | tf_op jit(solution)/shard_map/ppermute | solution.py:20
  95.2 22.5 %collective-permute-start.14 = (bf16[256,1024]{1,0:T(8,128)(2,1)S(1)}, bf16[256,1024]{1,0:T(8,128)(2,1)S(1)}, u32[]{:S(2)}, u32[]{:S(2)}) collective-permute-start(bf16[256,1024]{1,0:T(8,128)(2,1)S(1)} %get-tuple-element.33), channel_id=1, source_target_pairs={{0,1},{1,0},{2,3},{3,2},{4,5},{5,4},{6,7},{7,6},{8,9},{9,8},{10,11... | collective-permute-start | bytes 1572872 | tf_op jit(solution)/shard_map/ppermute | solution.py:20
  100.8 11.2 %collective-permute-start.35 = (bf16[256,512]{1,0:T(8,128)(2,1)S(1)}, bf16[256,512]{1,0:T(8,128)(2,1)S(1)}, u32[]{:S(2)}, u32[]{:S(2)}) collective-permute-start(bf16[256,512]{1,0:T(8,128)(2,1)S(1)} %get-tuple-element.47), channel_id=1, source_target_pairs={{0,16},{16,0},{1,17},{17,1},{2,18},{18,2},{3,19},{19,3},{4,20},{20... | collective-permute-start | bytes 786440 | tf_op jit(solution)/shard_map/ppermute | solution.py:20
  106.4 36.7 %copy-start.6 = (bf16[256,512]{1,0:T(8,128)(2,1)}, bf16[256,512]{1,0:T(8,128)(2,1)S(1)}, u32[]{:S(2)}) copy-start(bf16[256,512]{1,0:T(8,128)(2,1)S(1)} %collective-permute-done.34.refs_20_) | copy-start | bytes 786436
  106.4 11.2 %collective-permute-start.38 = (bf16[4,128,256]{2,1,0:T(8,128)(2,1)S(1)}, bf16[4,128,256]{2,1,0:T(8,128)(2,1)S(1)}, u32[]{:S(2)}, u32[]{:S(2)}) collective-permute-start(bf16[4,128,256]{2,1,0:T(8,128)(2,1)S(1)} %pad_maximum_fusion.refs_7_.refs_8_.refs_26_), channel_id=1, source_target_pairs={{0,16},{16,0},{1,17},{17,1},{2,18},{18,2},{3,19},{19,3},{4,20},{20... | collective-permute-start | bytes 786440 | tf_op jit(solution)/shard_map/ppermute | solution.py:20
  107.9 17.9 %collective-permute-start.15 = (bf16[256,1024]{1,0:T(8,128)(2,1)S(1)}, bf16[256,1024]{1,0:T(8,128)(2,1)S(1)}, u32[]{:S(2)}, u32[]{:S(2)}) collective-permute-start(bf16[256,1024]{1,0:T(8,128)(2,1)S(1)} %get-tuple-element.34), channel_id=1, source_target_pairs={{0,1},{1,0},{2,3},{3,2},{4,5},{5,4},{6,7},{7,6},{8,9},{9,8},{10,11... | collective-permute-start | bytes 1572872 | tf_op jit(solution)/shard_map/ppermute | solution.py:20
  108.0 35.1 %copy-start = (bf16[512,1024]{1,0:T(8,128)(2,1)}, bf16[512,1024]{1,0:T(8,128)(2,1)S(1)}, u32[]{:S(2)}) copy-start(bf16[512,1024]{1,0:T(8,128)(2,1)S(1)} %collective-permute-done.22.refs_11_.refs_0_.refs_12_.refs_13_) | copy-start | bytes 3145732
  108.0 6.0 %collective-permute-start.25 = (f32[128,256]{1,0:T(8,128)S(1)}, f32[128,256]{1,0:T(8,128)S(1)}, u32[]{:S(2)}, u32[]{:S(2)}) collective-permute-start(f32[128,256]{1,0:T(8,128)S(1)} %dynamic-slice_add_fusion.2), channel_id=1, source_target_pairs={{0,4},{1,5},{2,6},{3,7},{4,0},{5,1},{6,2},{7,3},{8,12},{9,13},{10,... | collective-permute-start | bytes 393224 | tf_op jit(solution)/shard_map/ppermute | solution.py:20
  112.1 28.8 %copy-start.8 = (bf16[256,512]{1,0:T(8,128)(2,1)}, bf16[256,512]{1,0:T(8,128)(2,1)S(1)}, u32[]{:S(2)}) copy-start(bf16[256,512]{1,0:T(8,128)(2,1)S(1)} %collective-permute-done.35.refs_21_) | copy-start | bytes 786436
  112.1 29.1 %collective-permute-start.30 = (bf16[512,512]{1,0:T(8,128)(2,1)S(1)}, bf16[512,512]{1,0:T(8,128)(2,1)S(1)}, u32[]{:S(2)}, u32[]{:S(2)}) collective-permute-start(bf16[512,512]{1,0:T(8,128)(2,1)S(1)} %column_halves.3), channel_id=1, source_target_pairs={{0,1},{1,0},{2,3},{3,2},{4,5},{5,4},{6,7},{7,6},{8,9},{9,8},{10,11... | collective-permute-start | bytes 1572872 | tf_op jit(solution)/shard_map/ppermute | solution.py:20
  114.0 53.3 %collective-permute-start.36 = (bf16[256,2048]{1,0:T(8,128)(2,1)S(1)}, bf16[256,2048]{1,0:T(8,128)(2,1)S(1)}, u32[]{:S(2)}, u32[]{:S(2)}) collective-permute-start(bf16[256,2048]{1,0:T(8,128)(2,1)S(1)} %get-tuple-element.48.refs_22_), channel_id=1, source_target_pairs={{0,16},{16,0},{1,17},{17,1},{2,18},{18,2},{3,19},{19,3},{4,20},{20... | collective-permute-start | bytes 3145736 | tf_op jit(solution)/shard_map/ppermute | solution.py:20
  117.7 8.1 %collective-permute-start.26 = (f32[128,256]{1,0:T(8,128)S(1)}, f32[128,256]{1,0:T(8,128)S(1)}, u32[]{:S(2)}, u32[]{:S(2)}) collective-permute-start(f32[128,256]{1,0:T(8,128)S(1)} %add.54), channel_id=1, source_target_pairs={{0,8},{1,9},{2,10},{3,11},{4,12},{5,13},{6,14},{7,15},{8,0},{9,1},... | collective-permute-start | bytes 393224 | tf_op jit(solution)/shard_map/ppermute | solution.py:20
  117.7 50.1 %collective-permute-start.37 = (bf16[256,2048]{1,0:T(8,128)(2,1)S(1)}, bf16[256,2048]{1,0:T(8,128)(2,1)S(1)}, u32[]{:S(2)}, u32[]{:S(2)}) collective-permute-start(bf16[256,2048]{1,0:T(8,128)(2,1)S(1)} %get-tuple-element.49.refs_23_), channel_id=1, source_target_pairs={{0,16},{16,0},{1,17},{17,1},{2,18},{18,2},{3,19},{19,3},{4,20},{20... | collective-permute-start | bytes 3145736 | tf_op jit(solution)/shard_map/ppermute | solution.py:20
  125.8 17.2 %collective-permute-start.31 = (bf16[512,512]{1,0:T(8,128)(2,1)S(1)}, bf16[512,512]{1,0:T(8,128)(2,1)S(1)}, u32[]{:S(2)}, u32[]{:S(2)}) collective-permute-start(bf16[512,512]{1,0:T(8,128)(2,1)S(1)} %column_halves.3), channel_id=1, source_target_pairs={{0,2},{1,3},{2,0},{3,1},{4,6},{5,7},{6,4},{7,5},{8,10},{9,11},{10,... | collective-permute-start | bytes 1572872 | tf_op jit(solution)/shard_map/ppermute | solution.py:20
  125.8 15.0 %collective-permute-start.27 = (bf16[1,128,256]{2,1,0:T(8,128)(2,1)S(1)}, bf16[1,128,256]{2,1,0:T(8,128)(2,1)S(1)}, u32[]{:S(2)}, u32[]{:S(2)}) collective-permute-start(bf16[1,128,256]{2,1,0:T(8,128)(2,1)S(1)} %fusion.1), channel_id=1, source_target_pairs={{0,2},{1,3},{2,0},{3,1},{4,6},{5,7},{6,4},{7,5},{8,10},{9,11},{10,... | collective-permute-start | bytes 196616 | tf_op jit(solution)/shard_map/ppermute | solution.py:20
  140.8 28.5 %copy-start.9 = (bf16[256,512]{1,0:T(8,128)(2,1)S(1)}, bf16[256,512]{1,0:T(8,128)(2,1)}, u32[]{:S(2)}) copy-start(bf16[256,512]{1,0:T(8,128)(2,1)} %copy-done.8) | copy-start | bytes 786436
  140.8 14.9 %collective-permute-start.16 = (bf16[256,1024]{1,0:T(8,128)(2,1)S(1)}, bf16[256,1024]{1,0:T(8,128)(2,1)S(1)}, u32[]{:S(2)}, u32[]{:S(2)}) collective-permute-start(bf16[256,1024]{1,0:T(8,128)(2,1)S(1)} %get-tuple-element.35), channel_id=1, source_target_pairs={{0,2},{1,3},{2,0},{3,1},{4,6},{5,7},{6,4},{7,5},{8,10},{9,11},{10,... | collective-permute-start | bytes 1572872 | tf_op jit(solution)/shard_map/ppermute | solution.py:20
  141.1 28.2 %copy-start.11 = (bf16[4,128,256]{2,1,0:T(8,128)(2,1)S(1)}, bf16[4,128,256]{2,1,0:T(8,128)(2,1)}, u32[]{:S(2)}) copy-start(bf16[4,128,256]{2,1,0:T(8,128)(2,1)} %copy-done.10) | copy-start | bytes 786436
  141.1 23.7 %collective-permute-start.17 = (bf16[256,1024]{1,0:T(8,128)(2,1)S(1)}, bf16[256,1024]{1,0:T(8,128)(2,1)S(1)}, u32[]{:S(2)}, u32[]{:S(2)}) collective-permute-start(bf16[256,1024]{1,0:T(8,128)(2,1)S(1)} %get-tuple-element.36), channel_id=1, source_target_pairs={{0,2},{1,3},{2,0},{3,1},{4,6},{5,7},{6,4},{7,5},{8,10},{9,11},{10,... | collective-permute-start | bytes 1572872 | tf_op jit(solution)/shard_map/ppermute | solution.py:20
  143.0 21.8 %collective-permute-start.28 = (bf16[2,128,256]{2,1,0:T(8,128)(2,1)S(1)}, bf16[2,128,256]{2,1,0:T(8,128)(2,1)S(1)}, u32[]{:S(2)}, u32[]{:S(2)}) collective-permute-start(bf16[2,128,256]{2,1,0:T(8,128)(2,1)S(1)} %pad_maximum_fusion.3), channel_id=1, source_target_pairs={{0,1},{1,0},{2,3},{3,2},{4,5},{5,4},{6,7},{7,6},{8,9},{9,8},{10,11... | collective-permute-start | bytes 393224 | tf_op jit(solution)/shard_map/ppermute | solution.py:20
  155.7 24.5 %collective-permute-start.18 = (bf16[256,1024]{1,0:T(8,128)(2,1)S(1)}, bf16[256,1024]{1,0:T(8,128)(2,1)S(1)}, u32[]{:S(2)}, u32[]{:S(2)}) collective-permute-start(bf16[256,1024]{1,0:T(8,128)(2,1)S(1)} %get-tuple-element.37), channel_id=1, source_target_pairs={{0,4},{1,5},{2,6},{3,7},{4,0},{5,1},{6,2},{7,3},{8,12},{9,13},{10,... | collective-permute-start | bytes 1572872 | tf_op jit(solution)/shard_map/ppermute | solution.py:20
  164.8 22.6 %collective-permute-start.19 = (bf16[256,1024]{1,0:T(8,128)(2,1)S(1)}, bf16[256,1024]{1,0:T(8,128)(2,1)S(1)}, u32[]{:S(2)}, u32[]{:S(2)}) collective-permute-start(bf16[256,1024]{1,0:T(8,128)(2,1)S(1)} %get-tuple-element.38), channel_id=1, source_target_pairs={{0,4},{1,5},{2,6},{3,7},{4,0},{5,1},{6,2},{7,3},{8,12},{9,13},{10,... | collective-permute-start | bytes 1572872 | tf_op jit(solution)/shard_map/ppermute | solution.py:20
  164.8 38.2 %collective-permute-start.20 = (bf16[256,1024]{1,0:T(8,128)(2,1)S(1)}, bf16[256,1024]{1,0:T(8,128)(2,1)S(1)}, u32[]{:S(2)}, u32[]{:S(2)}) collective-permute-start(bf16[256,1024]{1,0:T(8,128)(2,1)S(1)} %get-tuple-element.39), channel_id=1, source_target_pairs={{0,8},{1,9},{2,10},{3,11},{4,12},{5,13},{6,14},{7,15},{8,0},{9,1},... | collective-permute-start | bytes 1572872 | tf_op jit(solution)/shard_map/ppermute | solution.py:20
  167.2 44.0 %collective-permute-start.21 = (bf16[256,1024]{1,0:T(8,128)(2,1)S(1)}, bf16[256,1024]{1,0:T(8,128)(2,1)S(1)}, u32[]{:S(2)}, u32[]{:S(2)}) collective-permute-start(bf16[256,1024]{1,0:T(8,128)(2,1)S(1)} %get-tuple-element.40), channel_id=1, source_target_pairs={{0,8},{1,9},{2,10},{3,11},{4,12},{5,13},{6,14},{7,15},{8,0},{9,1},... | collective-permute-start | bytes 1572872 | tf_op jit(solution)/shard_map/ppermute | solution.py:20
  167.8 43.5 %collective-permute-start.29 = (bf16[4,128,256]{2,1,0:T(8,128)(2,1)S(1)}, bf16[4,128,256]{2,1,0:T(8,128)(2,1)S(1)}, u32[]{:S(2)}, u32[]{:S(2)}) collective-permute-start(bf16[4,128,256]{2,1,0:T(8,128)(2,1)S(1)} %pad_maximum_fusion.1.refs_13_), channel_id=1, source_target_pairs={{0,16},{16,0},{1,17},{17,1},{2,18},{18,2},{3,19},{19,3},{4,20},{20... | collective-permute-start | bytes 786440 | tf_op jit(solution)/shard_map/ppermute | solution.py:20
  170.3 41.0 %copy-start.2 = (bf16[1024,256]{1,0:T(8,128)(2,1)S(1)}, bf16[1024,256]{1,0:T(8,128)(2,1)}, u32[]{:S(2)}) copy-start(bf16[1024,256]{1,0:T(8,128)(2,1)} %refs_12_.1) | copy-start | bytes 1572868
  (5 other events, 42.4 us)

commit v2 on v1

v2 whole, which is shorter than its diff:
```python
import functools

import jax
import jax.numpy as jnp
from jax import lax
from jax.experimental import pallas as pl
from jax.experimental.pallas import tpu as pltpu
from jax.sharding import PartitionSpec as P

gelu_scale = 0.7978845608028654
gelu_cubic = 0.044715
f32 = jnp.float32
bf16 = jnp.bfloat16
NEAR_HINT = 8
FORWARD_HINTS = (4, 1 / 16)
WEIGHT_HINT = 1 / 16
INPUT_HINT = 30
LEFT_HINT = 1 / 16
NT = (((1,), (1,)), ((), ()))
TN = (((0,), (0,)), ((), ()))


def from_partner(shard, axis, distance):
    return lax.ppermute(shard, axis, [(i, i ^ 1 << distance) for i in range(lax.axis_size(axis))])


def gelu_parts(preact):
    inner = gelu_scale * (preact + gelu_cubic * preact * preact * preact)
    tangent = jnp.tanh(inner)
    value = 0.5 * preact * (1.0 + tangent)
    slope = 0.5 * (1.0 + tangent) + 0.5 * preact * (1.0 - tangent * tangent) * gelu_scale * (
        1.0 + 3.0 * gelu_cubic * preact * preact
    )
    return (value, slope)


def params(mib=60):
    return pltpu.CompilerParams(vmem_limit_bytes=mib * 1024 * 1024)


def cost(hint, flops, moved):
    return pl.CostEstimate(flops=int(hint * flops), bytes_accessed=int(hint * moved), transcendentals=0)


def rows_of(pieces):
    return pieces[0][...] if len(pieces) == 1 else jnp.concatenate([p[...] for p in pieces], axis=0)


def taken(refs):
    refs = list(refs)
    return lambda n: [refs.pop(0) for _ in range(n)]


def forward_body(local_taps, pieces, aliased, packed, idx_ref, *refs):
    take = taken(refs)
    own = [r[...] for r in take(local_taps)]
    remote_refs = [take(n) for n in pieces]
    remote = [rows_of(r) for r in remote_refs]
    remote_refs = [r[0] for r in remote_refs]
    latent = jnp.concatenate([r[0] for r in take(2)], axis=0)
    weight_ref, right_ref, cot_ref = take(3)
    take(1 if aliased else 0)
    act_ref, grad_ref = take(2)
    terms = take(len(pieces))
    local_ref, latent_term_ref = take(2)
    group = pl.program_id(0)
    taps, block, hidden = weight_ref.shape
    weights = weight_ref[...].reshape(taps * block, hidden)
    right = right_ref[...]
    preact = jnp.dot(jnp.concatenate(own + remote, axis=1), weights, preferred_element_type=f32)
    preact = preact + jnp.dot(latent, right, preferred_element_type=f32)
    value, slope = gelu_parts(preact)
    act_ref[...] = value.astype(bf16)
    grad = (cot_ref[...].astype(f32) * slope).astype(bf16)
    rows = grad.shape[0]
    grad_ref[:rows] = grad
    if packed:
        half = block // 2
        height = grad_ref.shape[0] - rows
        theirs = pl.ds(pl.multiple_of((1 - idx_ref[1]) * half, half), half)
        cells = [
            ref[row : row + height, theirs] for ref in remote_refs[-packed:] for row in range(0, rows, height)
        ]
        grad_ref[rows:] = jnp.concatenate(cells, axis=1)
    spread = lax.dot_general(grad, weights, NT, preferred_element_type=f32)
    for k, term_ref in enumerate(terms):
        lo = (local_taps + k) * block
        term_ref[...] = spread[:, lo : lo + block].astype(bf16)

    @pl.when(group == 0)
    def _():
        local_ref[...] = jnp.zeros_like(local_ref)
        latent_term_ref[...] = jnp.zeros_like(latent_term_ref)

    for k in range(local_taps):
        target = group if k == 0 else group ^ (1 << (k - 1))
        cols = pl.ds(pl.multiple_of(target * block, block), block)
        local_ref[:, cols] += spread[:, k * block : (k + 1) * block]
    latent_term_ref[...] += lax.dot_general(grad, right, NT, preferred_element_type=f32)


def forward_chunk(chunk, idx, tokens, remote, latent, weight, right, cotangent, act_before, packed):
    taps, block, hidden_local = weight.shape
    width = tokens.shape[1]
    rows = tokens.shape[0] // 2
    groups = width // block
    hidden = hidden_local // groups
    local_taps = taps - len(remote)
    quarter, rank = latent.shape[2:]
    height = packed * rows * (block // 2) // hidden
    own_spec = lambda k: pl.BlockSpec(
        (rows, block), lambda g, idx: (chunk, g if k == 0 else g ^ (1 << (k - 1)))
    )
    piece_spec = lambda piece: pl.BlockSpec((piece[2], block), lambda g, idx: (piece[1], g))
    latent_spec = lambda k: pl.BlockSpec(
        (1, None, quarter, rank), lambda g, idx: (idx[0] ^ k, 0, 0, 0)
    )
    in_specs = [own_spec(k) for k in range(local_taps)]
    in_specs += [piece_spec(p) for tap in remote for p in tap]
    in_specs += [latent_spec(2 * chunk), latent_spec(2 * chunk + 1)]
    in_specs += [
        pl.BlockSpec((taps, block, hidden), lambda g, idx: (0, 0, g)),
        pl.BlockSpec((rank, hidden), lambda g, idx: (0, g)),
        pl.BlockSpec((rows, hidden), lambda g, idx: (chunk, g)),
    ]
    args = [tokens] * local_taps + [p[0] for tap in remote for p in tap]
    args += [latent, latent, weight, right, cotangent]
    aliases = {}
    if act_before is not None:
        in_specs.append(pl.BlockSpec(memory_space=pl.ANY))
        args.append(act_before)
        aliases = {len(args): 0}
    out_specs = [
        pl.BlockSpec((rows, hidden), lambda g, idx: (chunk, g)),
        pl.BlockSpec((rows + height, hidden), lambda g, idx: (0, g)),
    ]
    out_specs += [pl.BlockSpec((rows, block), lambda g, idx: (0, g))] * len(remote)
    out_specs += [
        pl.BlockSpec((rows, width), lambda g, idx: (0, 0)),
        pl.BlockSpec((rows, rank), lambda g, idx: (0, 0)),
    ]
    shape = jax.ShapeDtypeStruct
    out_shape = [shape(cotangent.shape, bf16), shape((rows + height, hidden_local), bf16)]
    out_shape += [shape((rows, width), bf16)] * len(remote)
    out_shape += [shape((rows, width), f32), shape((rows, rank), f32)]
    outs = pl.pallas_call(
        functools.partial(
            forward_body, local_taps, [len(t) for t in remote], act_before is not None, packed
        ),
        grid_spec=pltpu.PrefetchScalarGridSpec(
            num_scalar_prefetch=1, grid=(groups,), in_specs=in_specs, out_specs=out_specs
        ),
        out_shape=out_shape,
        input_output_aliases=aliases,
        compiler_params=params(),
        cost_estimate=cost(
            FORWARD_HINTS[chunk],
            4 * rows * hidden_local * (taps * block + rank),
            2 * (weight.size + right.size + 3 * rows * hidden_local + 12 * rows * width),
        ),
        name="forward_chunk",
    )(idx, *args)
    act, grad = outs[:2]
    return act, grad, outs[2 : 2 + len(remote)], outs[-2], outs[-1]


def halves_body(idx_ref, *refs):
    row, out_ref = 0, refs[-1]
    for src in refs[:-1]:
        out_ref[row : row + src.shape[0]] = src[...]
        row += src.shape[0]


def column_halves(which, arrays, block):
    width = arrays[0].shape[1]
    half = block // 2
    rows = sum(a.shape[0] for a in arrays)
    return pl.pallas_call(
        halves_body,
        grid_spec=pltpu.PrefetchScalarGridSpec(
            num_scalar_prefetch=1,
            grid=(width // block,),
            in_specs=[
                pl.BlockSpec((a.shape[0], half), lambda j, which: (0, 2 * j + which[0])) for a in arrays
            ],
            out_specs=pl.BlockSpec((rows, half), lambda j, which: (0, j)),
        ),
        out_shape=jax.ShapeDtypeStruct((rows, width // 2), bf16),
        compiler_params=params(8),
        cost_estimate=cost(1 / 16, 0, 2 * rows * width),
        name="column_halves",
    )(which, *arrays)


def in_dp_order(idx_ref, near, far):
    first = idx_ref[1] == 0
    return jnp.concatenate([jnp.where(first, near, far), jnp.where(first, far, near)], axis=0)


def near_body(local_taps, pieces, idx_ref, *refs):
    take = taken(refs)
    own = [r[...] for r in take(local_taps)]
    remote = [rows_of(take(n)) for n in pieces]
    grad = rows_of(take(2))
    sum_ref = refs[-1]
    total = lax.dot_general(jnp.concatenate(own + remote, axis=1), grad, TN, preferred_element_type=f32)
    sum_ref[...] = total.reshape(sum_ref.shape)


def far_body(local_taps, pieces, packed, idx_ref, *refs):
    take = taken(refs)
    own = [r[...] for r in take(local_taps)]
    remote = [rows_of(take(n)) for n in pieces]
    pack_ref = take(1)[0]
    half = own[0].shape[1]
    cells = [pack_ref[:, lo : lo + half] for lo in range(0, pack_ref.shape[1], half)]
    count = len(cells) // packed
    for k in range(packed):
        tap = len(remote) - packed + k
        remote[tap] = jnp.concatenate([remote[tap]] + cells[k * count : (k + 1) * count], axis=0)
    grad, far_grad = rows_of(take(2)), rows_of(take(2))
    latent_ref, far_latent_ref, near_ref, weight_ref, right_ref = take(5)
    total = lax.dot_general(jnp.concatenate(own + remote, axis=1), far_grad, TN, preferred_element_type=f32)
    weight_ref[...] = (near_ref[...] + total.reshape(weight_ref.shape)).astype(bf16)
    order = [k ^ idx_ref[0] for k in range(latent_ref.shape[0])]
    latent = jnp.concatenate([latent_ref[k] for k in order], axis=0)
    far_latent = jnp.concatenate([far_latent_ref[k] for k in order], axis=0)
    latents, grads = in_dp_order(idx_ref, latent, far_latent), in_dp_order(idx_ref, grad, far_grad)
    right = lax.dot_general(latents, grads, TN, preferred_element_type=f32)
    right_ref[...] = right.astype(bf16)


def weight_specs(tokens, grads, taps, block):
    rows, width = tokens.shape
    chunk_rows, hidden_local = grads[0].shape
    groups = width // block
    half = block // 2
    hidden = hidden_local // groups
    own_spec = lambda k: pl.BlockSpec(
        (rows, half), lambda g, idx: (0, 2 * (g if k == 0 else g ^ (1 << (k - 1))) + idx[1])
    )
    grad_spec = pl.BlockSpec((chunk_rows, hidden), lambda g, idx: (0, g))
    sum_spec = pl.BlockSpec((taps, half, hidden), lambda g, idx: (0, 0, g))
    return rows, chunk_rows, hidden_local, groups, half, hidden, own_spec, grad_spec, sum_spec


def near_weight_grads(idx, tokens, remote, grads, taps, block):
    rows, _, hidden_local, groups, half, _, own_spec, grad_spec, sum_spec = weight_specs(
        tokens, grads, taps, block
    )
    local_taps = taps - len(remote)
    piece_spec = lambda p: pl.BlockSpec((p[2], half), lambda g, idx: (p[1], 2 * g + idx[1]))
    pieces = [p for tap in remote for p in tap]
    return pl.pallas_call(
        functools.partial(near_body, local_taps, [len(t) for t in remote]),
        grid_spec=pltpu.PrefetchScalarGridSpec(
            num_scalar_prefetch=1,
            grid=(groups,),
            in_specs=[own_spec(k) for k in range(local_taps)]
            + [piece_spec(p) for p in pieces]
            + [grad_spec] * 2,
            out_specs=sum_spec,
        ),
        out_shape=jax.ShapeDtypeStruct((taps, half, hidden_local), f32),
        compiler_params=params(),
        cost_estimate=cost(
            NEAR_HINT, 2 * rows * hidden_local * taps * half, 4 * taps * half * hidden_local
        ),
        name="near_weight_grads",
    )(idx, *([tokens] * local_taps), *[p[0] for p in pieces], *grads)


def weight_grads(idx, near, tokens, remote, grads, latent, far_latent, taps, block):
    rows, chunk_rows, hidden_local, groups, half, hidden, own_spec, grad_spec, sum_spec = weight_specs(
        tokens, grads, taps, block
    )
    local_taps = taps - len(remote)
    rank = latent[0].shape[3]
    pack = grads[-1]
    height = pack.shape[0] - chunk_rows
    packed = height * hidden // (chunk_rows * half)
    piece_spec = lambda p: pl.BlockSpec((p[2], half), lambda g, idx: (p[1], g))
    pieces = [p for tap in remote for p in tap]
    return pl.pallas_call(
        functools.partial(far_body, local_taps, [len(t) for t in remote], packed),
        grid_spec=pltpu.PrefetchScalarGridSpec(
            num_scalar_prefetch=1,
            grid=(groups,),
            in_specs=[own_spec(k) for k in range(local_taps)]
            + [piece_spec(p) for p in pieces]
            + [pl.BlockSpec((height, hidden), lambda g, idx: (chunk_rows // height, g))]
            + [grad_spec] * 4
            + [latent_spec(latent), latent_spec(far_latent), sum_spec],
            out_specs=[sum_spec, pl.BlockSpec((rank, hidden), lambda g, idx: (0, g))],
        ),
        out_shape=[
            jax.ShapeDtypeStruct((taps, half, hidden_local), bf16),
            jax.ShapeDtypeStruct((rank, hidden_local), bf16),
        ],
        compiler_params=params(),
        cost_estimate=cost(
            WEIGHT_HINT,
            2 * rows * hidden_local * (taps * half + 2 * rank),
            8 * taps * half * hidden_local,
        ),
        name="weight_grads",
    )(
        idx,
        *([tokens] * local_taps),
        *[p[0] for p in pieces],
        pack,
        *grads,
        latent[0],
        far_latent[0],
        near,
    )


def inputs_body(n_terms, idx_ref, *refs):
    take = taken(refs)
    total = rows_of(take(2))
    for _ in range(n_terms):
        total = total + rows_of(take(2)).astype(f32)
    left_ref, latent_ref, input_ref = take(3)
    latent = jnp.concatenate([latent_ref[k ^ idx_ref[0]] for k in range(latent_ref.shape[0])], axis=0)
    low_rank = lax.dot_general(latent, left_ref[...], NT, preferred_element_type=f32)
    input_ref[...] = (total + low_rank).astype(bf16)


def latent_spec(pair):
    return pl.BlockSpec(
        (pair[0].shape[0], None) + pair[0].shape[2:], lambda g, idx: (0, pair[1], 0, 0)
    )


def input_grads(idx, local, terms, left, latent, block):
    width, rank = left.shape
    chunk_rows = local[0].shape[0]
    rows = 2 * chunk_rows
    chunk_spec = pl.BlockSpec((chunk_rows, block), lambda g, idx: (0, g))
    return pl.pallas_call(
        functools.partial(inputs_body, len(terms)),
        grid_spec=pltpu.PrefetchScalarGridSpec(
            num_scalar_prefetch=1,
            grid=(width // block,),
            in_specs=[chunk_spec] * (2 + 2 * len(terms))
            + [pl.BlockSpec((block, rank), lambda g, idx: (g, 0)), latent_spec(latent)],
            out_specs=pl.BlockSpec((rows, block), lambda g, idx: (0, g)),
        ),
        out_shape=jax.ShapeDtypeStruct((rows, width), bf16),
        compiler_params=params(),
        cost_estimate=cost(INPUT_HINT, 2 * rows * width * rank, 20 * rows * width),
        name="input_grads",
    )(idx, *local, *[c for pair in terms for c in pair], left, latent[0])


def left_body(idx_ref, tokens_ref, far_tokens_ref, latent_ref, far_latent_ref, left_ref):
    order = [k ^ idx_ref[0] for k in range(latent_ref.shape[0])]
    latent = jnp.concatenate([latent_ref[k] for k in order], axis=0)
    far_latent = jnp.concatenate([far_latent_ref[k] for k in order], axis=0)
    tokens = in_dp_order(idx_ref, tokens_ref[...], far_tokens_ref[...])
    latents = in_dp_order(idx_ref, latent, far_latent)
    left = lax.dot_general(tokens, latents, TN, preferred_element_type=f32)
    left_ref[...] = left.astype(bf16)


def left_grads(idx, tokens, far_tokens, latent, far_latent, block):
    rows, width = tokens.shape
    rank = latent[0].shape[3]
    token_spec = pl.BlockSpec((rows, block), lambda g, idx: (0, g))
    return pl.pallas_call(
        left_body,
        grid_spec=pltpu.PrefetchScalarGridSpec(
            num_scalar_prefetch=1,
            grid=(width // block,),
            in_specs=[token_spec, token_spec, latent_spec(latent), latent_spec(far_latent)],
            out_specs=pl.BlockSpec((block, rank), lambda g, idx: (g, 0)),
        ),
        out_shape=jax.ShapeDtypeStruct((width, rank), bf16),
        compiler_params=params(),
        cost_estimate=cost(LEFT_HINT, 4 * rows * width * rank, 4 * rows * width),
        name="left_grads",
    )(idx, tokens, far_tokens, latent[0], far_latent[0])


def after(value, *first):
    return lax.optimization_barrier((value, first))[0]


def one_step(f, *args):
    shapes = jax.eval_shape(f, *args)
    other = lambda *_: jax.tree.map(lambda x: jnp.zeros(x.shape, x.dtype), shapes)
    return lax.cond(lax.axis_index("mp") >= 0, f, other, *args)


def halved_sum(halves, bit):
    mine = (lax.axis_index("mp") >> bit) & 1
    sent = jnp.where(mine == 0, halves[1], halves[0])
    kept = jnp.where(mine == 0, halves[0], halves[1])
    return kept + from_partner(sent, "mp", bit)


def high_sum(part):
    for bit in range(2, lax.axis_size("mp").bit_length() - 1):
        part = part + from_partner(part, "mp", bit)
    return part.astype(bf16)[None, None]


def gathered(stack):
    for bit in (1, 0):
        stack = jnp.concatenate([stack, from_partner(stack, "mp", bit)], axis=0)
    return stack


def with_places(arrays, places):
    return [[(a, *p) for a, p in zip(*tap)] for tap in zip(arrays, places)]


def over_high_terms(terms, *first):
    return [from_partner(after(t, *first), "mp", bit) for bit, t in enumerate(terms) if bit >= 2]


def on_device(tokens, block_weight, left_factor, right_factor, out_cotangent):
    rows, width = tokens.shape
    taps, block, _ = block_weight.shape
    groups = width // block
    local_bits = groups.bit_length() - 1
    high_bits = range(2, taps - 1 - local_bits)
    mp_index = lax.axis_index("mp")
    dp_index = lax.axis_index("dp")
    place = 2 * (mp_index & 1) + ((mp_index >> 1) & 1)
    idx = jnp.stack([place, dp_index]).astype(jnp.int32)
    mine = dp_index.reshape(1).astype(jnp.int32)
    theirs = 1 - mine
    half_rows = rows // 2

    over_high = lambda x: [from_partner(x, "mp", bit) for bit in high_bits]
    cut = half_rows // 2
    first = over_high(tokens[:cut])

    def low_part(tokens, left):
        part = jnp.dot(tokens, left, preferred_element_type=f32)
        part = halved_sum(jnp.split(part, 2, axis=0), 0)
        core = from_partner(after(tokens, part), "mp", 0)
        return halved_sum(jnp.split(part, 2, axis=0), 1), core

    def high_part(part, tokens):
        far_tokens = from_partner(tokens, "dp", 0)
        near_y = from_partner(tokens[:half_rows], "mp", 1)
        quarter_sum = high_sum(part)
        second = over_high(after(tokens[cut:half_rows], quarter_sum))
        far = from_partner(quarter_sum, "dp", 0)
        far_half = column_halves(mine, [far_tokens], block)
        return gathered(quarter_sum), far, far_tokens, far_half, near_y, second

    low_sum, core = one_step(low_part, tokens, left_factor)
    low_sum, first = after((low_sum, first))
    latent, far_quarter, far_tokens, far_half, near_y, second = one_step(high_part, low_sum, tokens)
    third = over_high(after(tokens[half_rows:], latent))
    far_y = from_partner(after(tokens[half_rows:], latent), "mp", 1)
    received = [
        [[(core, 0, half_rows)], [(near_y, 0, half_rows)]]
        + [[(p, 0, cut), (q, 0, half_rows - cut)] for p, q in zip(first, second)],
        [[(core, 1, half_rows)], [(far_y, 0, half_rows)]] + [[(p, 0, half_rows)] for p in third],
    ]

    halves = column_halves(theirs, [p[0] for tap in received[0][2:] for p in tap], block)
    far_halves = from_partner(halves, "dp", 0)
    latent, halves = after((latent, halves))
    forward = functools.partial(forward_chunk, idx=idx, tokens=tokens, latent=latent)
    forward = functools.partial(forward, weight=block_weight, right=right_factor, cotangent=out_cotangent)
    act, near_grad, near_out, near_local, near_latent = forward(
        0, remote=received[0], act_before=None, packed=0
    )
    far_near_grad = from_partner(after(near_grad, far_halves), "dp", 0)
    near_terms = over_high_terms(near_out, far_y)
    far_y_half = from_partner(after(far_half, far_y, third, near_grad), "mp", 1)
    act, grad, far_out, far_local, far_latent_term = forward(
        1, remote=received[1], act_before=act, packed=len(high_bits)
    )
    far_far_grad = from_partner(grad, "dp", 0)
    local = [near_local, far_local]
    grads = [near_grad, grad, far_near_grad, far_far_grad]

    def low_grad(a, b):
        return halved_sum(jnp.split(halved_sum([a, b], 0), 2, axis=0), 1)

    def high_grad(part, *terms):
        return high_sum(part), [from_partner(t, "mp", bit) for bit, t in enumerate(terms)]

    def gather_grad(quarter_sum, far_quarter, core_term, y_term, far_half, tokens, remote, grads):
        remote = with_places(remote, near_places)
        near = near_weight_grads(idx, tokens, remote, grads, taps, block)
        stack = jnp.concatenate([quarter_sum, far_quarter], axis=1)
        other = from_partner(stack, "mp", 1)
        core_term = from_partner(core_term, "mp", 0)
        far_core = from_partner(after(far_half, core_term), "mp", 0)
        y_term = from_partner(after(y_term, other, far_core), "mp", 1)
        stack = jnp.concatenate([stack, other], axis=0)
        stack = jnp.concatenate([stack, from_partner(after(stack, far_core), "mp", 0)], axis=0)
        return stack, core_term, y_term, far_core, near

    low_sum = one_step(low_grad, near_latent, far_latent_term)
    low_sum, near_terms, far_near_grad, far_y_half = after(
        (low_sum, near_terms, far_near_grad, far_y_half)
    )
    quarter_sum, low_terms = one_step(high_grad, low_sum, *near_out[:2])
    near_terms = low_terms + near_terms
    far_terms = over_high_terms(far_out, quarter_sum)
    remote = [a + b for a, b in zip(*received)]
    near_places = [[p[1:] for p in tap] for tap in remote]
    gathered_both, core_term, y_term, far_core, near = one_step(
        gather_grad,
        quarter_sum,
        far_quarter,
        *far_out[:2],
        far_half,
        tokens,
        [[p[0] for p in tap] for tap in remote],
        grads[:2],
    )
    far_terms = [core_term, y_term] + far_terms

    far_remote = [[(c, 0, rows)] for c in (far_core, far_y_half)]
    far_remote += [[(far_halves, k, half_rows)] for k in range(len(high_bits))]

    def last_part(gathered_both, far_tokens, near, grads, latent, far_remote):
        far_latent_grad = from_partner(gathered_both[:, :1], "dp", 0)
        far_remote = with_places(far_remote, far_places)
        weights = weight_grads(
            idx, near, far_tokens, far_remote, grads, (latent, 0), (gathered_both, 1), taps, block
        )
        return far_latent_grad, *weights

    far_places = [[p[1:] for p in tap] for tap in far_remote]
    input_grad = input_grads(
        idx, local, list(zip(near_terms, far_terms)), left_factor, (gathered_both, 0), block
    )
    gathered_both, input_grad = after((gathered_both, input_grad))
    far_latent_grad, weight_grad, right_grad = one_step(
        last_part,
        gathered_both,
        far_tokens,
        near,
        grads,
        latent,
        [[p[0] for p in tap] for tap in far_remote],
    )
    left_grad = left_grads(idx, tokens, far_tokens, (gathered_both, 0), (far_latent_grad, 0), block)
    return act, input_grad, weight_grad, left_grad, right_grad


def flip_groups(blocks, distance):
    full_shape = blocks.shape
    group_count = full_shape[1]
    split_view = blocks.reshape(
        (full_shape[0], group_count // (2 * distance), 2, distance) + full_shape[2:]
    )
    return jnp.flip(split_view, axis=2).reshape(full_shape)


def on_device_general(tokens, block_weight, left_factor, right_factor, out_cotangent):
    tok_rows = tokens.shape[0]
    local_width = tokens.shape[1]
    tap_count = block_weight.shape[0]
    block_size = block_weight.shape[1]
    hidden_local = block_weight.shape[2]
    group_count = local_width // block_size
    local_bits = group_count.bit_length() - 1
    tok_blocks = tokens.reshape(tok_rows, group_count, block_size)
    tap_inputs = [tok_blocks]
    for tap_index in range(1, tap_count):
        level_bit = tap_index - 1
        if level_bit < local_bits:
            tap_inputs.append(flip_groups(tok_blocks, 1 << level_bit))
        else:
            partner = from_partner(tokens, "mp", level_bit - local_bits)
            tap_inputs.append(partner.reshape(tok_rows, group_count, block_size))
    stacked = jnp.stack(tap_inputs, axis=2)
    weight_view = block_weight.reshape(tap_count, block_size, group_count, 2 * block_size)
    butterfly = jnp.einsum("tgkc,kcgh->tgh", stacked, weight_view, preferred_element_type=f32)
    butterfly = butterfly.reshape(tok_rows, hidden_local)
    latent = lax.psum(jnp.dot(tokens, left_factor, preferred_element_type=f32), "mp")
    latent_bf = latent.astype(bf16)
    preact = butterfly + jnp.dot(latent_bf, right_factor, preferred_element_type=f32)
    value, slope = gelu_parts(preact)
    activated = value.astype(bf16)
    grad_pre = (out_cotangent.astype(f32) * slope).astype(bf16)
    latent_term = lax.dot_general(grad_pre, right_factor, NT, preferred_element_type=f32)
    latent_grad = lax.psum(latent_term, "mp").astype(bf16)
    left_part = lax.dot_general(tokens, latent_grad, TN, preferred_element_type=f32)
    right_part = lax.dot_general(latent_bf, grad_pre, TN, preferred_element_type=f32)
    left_sum, right_sum = lax.psum((left_part, right_part), "dp")
    grad_view = grad_pre.reshape(tok_rows, group_count, 2 * block_size)
    spread = jnp.einsum("tgh,kcgh->tgkc", grad_view, weight_view, preferred_element_type=f32)
    input_sum = spread[:, :, 0]
    for tap_index in range(1, tap_count):
        level_bit = tap_index - 1
        piece = spread[:, :, tap_index]
        if level_bit < local_bits:
            input_sum = input_sum + flip_groups(piece, 1 << level_bit)
        else:
            returned = from_partner(
                piece.reshape(tok_rows, local_width), "mp", level_bit - local_bits
            )
            input_sum = input_sum + returned.reshape(tok_rows, group_count, block_size)
    low_rank = lax.dot_general(latent_grad, left_factor, NT, preferred_element_type=f32)
    input_grad = (input_sum.reshape(tok_rows, local_width) + low_rank).astype(bf16)
    partial_value = jnp.einsum("tgkc,tgh->kcgh", stacked, grad_view, preferred_element_type=f32)
    partial_value = partial_value.reshape(tap_count, block_size, hidden_local)
    weight_grad = lax.psum_scatter(partial_value, "dp", scatter_dimension=1, tiled=True).astype(bf16)
    return (activated, input_grad, weight_grad, left_sum.astype(bf16), right_sum.astype(bf16))


def solution(mesh):
    pairs = mesh.shape["dp"] == 2 and mesh.shape["mp"] >= 4
    return jax.shard_map(
        on_device if pairs else on_device_general,
        mesh=mesh,
        in_specs=(P("dp", "mp"), P(None, None, "mp"), P("mp", None), P(None, "mp"), P("dp", "mp")),
        out_specs=(P("dp", "mp"), P("dp", "mp"), P(None, "dp", "mp"), P("mp", None), P(None, "mp")),
        check_vma=False,
    )
```

time: 217 us -> 162 us (0.75)
  waiting for transfers between devices: 130 us -> 59.7 us
  Pallas kernels: 40.8 us -> 54.8 us
  local copies, waits for them, and re-layouts: 2.46 us -> 7.27 us
  starting transfers between devices: 39.9 us -> 35.5 us
    ppermute x39 -> x37, waiting for transfers between devices: 130 us -> 59.7 us  [from_partner(): lax.ppermute(shard, axis, [(i, i ^ 1 << distance) for i in range(lax.axis...]
    pallas_call x3 -> x5, Pallas kernels: 34.2 us -> 45.4 us  [the longest x2 23.9 us: forward_chunk(): pl.pallas_call(functools.partial(forward_body, local_taps, [len(t) for t...]
    ppermute x39 -> x37, starting transfers between devices: 39.9 us -> 35.5 us  [from_partner(): lax.ppermute(shard, axis, [(i, i ^ 1 << distance) for i in range(lax.axis...]
    slice x3 -> x5, local copies, waits for them, and re-layouts: 1.34 us -> 5.6 us  [the longest x1 1.87 us: on_device(): far_y = from_partner(after(tokens[half_rows:], latent), 'mp', 1)]
    pallas_call x3 -> x2, Pallas kernels: 1.2 us -> 3.79 us  [column_halves(): pl.pallas_call(halves_body, grid_spec=pltpu.PrefetchScalarGridSpec(num_sc...]
  transfers between devices with their start and end apart: 39 -> 37, of which waited for: 21 -> 20; matrix products, arithmetic and copies ran while one was open for 1% -> 5% of each run, Pallas kernels for 16% -> 31%
where the time goes in v2:
time: 162 us; the launch traced here: 161 us
  waiting for transfers between devices  59.7 us (37%)
  Pallas kernels  54.8 us (34%)
  starting transfers between devices  35.5 us (22%)
  local copies, waits for them, and re-layouts  7.27 us (4%)
  matrix products  1.89 us (1%)
    ppermute x37, waiting for transfers between devices, from_partner(): lax.ppermute(shard, axis, [(i, i ^ 1 << distance) for i in range(lax.axis...  59.7 us
    ppermute x37, starting transfers between devices, from_partner(): lax.ppermute(shard, axis, [(i, i ^ 1 << distance) for i in range(lax.axis...  35.5 us
    pallas_call x2, Pallas kernels, forward_chunk(): pl.pallas_call(functools.partial(forward_body, local_taps, [len(t) for t...  23.9 us
    pallas_call x1, Pallas kernels, weight_grads(): pl.pallas_call(functools.partial(far_body, local_taps, [len(t) for t in r...  9.06 us
    pallas_call x1, Pallas kernels, near_weight_grads(): pl.pallas_call(functools.partial(near_body, local_taps, [len(t) for t in...  7.81 us
    pallas_call x1, Pallas kernels, input_grads(): pl.pallas_call(functools.partial(inputs_body, len(terms)), grid_spec=pltp...  5.55 us
    pallas_call x1, Pallas kernels, left_grads(): pl.pallas_call(left_body, grid_spec=pltpu.PrefetchScalarGridSpec(num_scal...  4.69 us
    pallas_call x2, Pallas kernels, column_halves(): pl.pallas_call(halves_body, grid_spec=pltpu.PrefetchScalarGridSpec(num_sc...  3.79 us
  transfers between devices with their start and end apart: 37, of which 20 were waited for; matrix products, arithmetic and copies ran while one was open for 5% of the time, Pallas kernels for 31%

profile of v2, /device:TPU:0, one launch (start us, length us, event | category | flops | bytes accessed | tf_op | source)
XLA Modules:
  0.0 161.5 jit_solution(17335407506691601120)
XLA Ops:
  1.6 3.1 %collective-permute-start.24 = (bf16[128,1024]{1,0:T(8,128)(2,1)S(1)}, bf16[128,1024]{1,0:T(8,128)(2,1)S(1)}, u32[]{:S(2)}, u32[]{:S(2)}) collective-permute-start(bf16[128,1024]{1,0:T(8,128)(2,1)S(1)} %slice.17), channel_id=1, source_target_pairs={{0,4},{1,5},{2,6},{3,7},{4,0},{5,1},{6,2},{7,3},{8,12},{9,13},{10,... | collective-permute-start | bytes 786440 | tf_op jit(solution)/shard_map/ppermute | solution.py:24
  4.7 2.6 %collective-permute-start.25 = (bf16[128,1024]{1,0:T(8,128)(2,1)S(1)}, bf16[128,1024]{1,0:T(8,128)(2,1)S(1)}, u32[]{:S(2)}, u32[]{:S(2)}) collective-permute-start(bf16[128,1024]{1,0:T(8,128)(2,1)S(1)} %slice.17), channel_id=1, source_target_pairs={{0,8},{1,9},{2,10},{3,11},{4,12},{5,13},{6,14},{7,15},{8,0},{9,1},... | collective-permute-start | bytes 786440 | tf_op jit(solution)/shard_map/ppermute | solution.py:24
  7.3 1.9 %slice.16 = bf16[256,1024]{1,0:T(8,128)(2,1)} slice(bf16[512,1024]{1,0:T(8,128)(2,1)} %tokens_ref.1), slice={[256:512], [0:1024]} | slice | bytes 1048576 | tf_op jit(solution)/shard_map/slice | solution.py:460
  9.2 9.7 %conditional.6 = (f32[128,256]{1,0:T(8,128)S(1)}, bf16[512,1024]{1,0:T(8,128)(2,1)}) conditional(s32[]{:T(128)} %convert_element_type.8, () %tuple.70, (bf16[512,1024]{1,0:T(8,128)(2,1)}, bf16[1024,256]{1,0:T(8,128)(2,1)}) %tuple.71), branch_computations={%region_0.0_spmd, %region_1.2_spmd} | conditional | flops 268730368 | bytes 14811390 | solution.py:393
  9.2 1.9 %fusion.2 = f32[512,256]{1,0:T(8,128)S(1)} fusion(bf16[512,1024]{1,0:T(8,128)(2,1)} %get-tuple-element.85, bf16[1024,256]{1,0:T(8,128)(2,1)} %get-tuple-element.84), kind=kOutput, calls=%fused_computation.19 | convolution fusion | flops 268435456 | bytes 2097152 | tf_op jit(solution)/shard_map/cond/branch_1_fun/dot_general | solution.py:442
  11.2 1.5 collective-permute-done.21
  13.0 1.6 collective-permute-start.22
  14.6 4.2 %collective-permute-done.22 = f32[128,256]{1,0:T(8,128)S(1)} collective-permute-done((f32[128,256]{1,0:T(8,128)S(1)}, f32[128,256]{1,0:T(8,128)S(1)}, u32[]{:S(2)}, u32[]{:S(2)}) %collective-permute-start.22) | collective-permute-done | bytes 131104 | tf_op jit(solution)/shard_map/cond/branch_1_fun/ppermute | solution.py:24
  19.0 28.9 %conditional.7 = (bf16[4,1,128,256]{3,2,1,0:T(8,128)(2,1)S(1)}, bf16[1,1,128,256]{3,2,1,0:T(8,128)(2,1)}, bf16[512,1024]{1,0:T(8,128)(2,1)}, bf16[512,512]{1,0:T...) conditional(s32[]{:T(128)} %convert_element_type.8, () %tuple.72, ...), branch_computations={%region_2.3_spmd, %region_3.4_spmd} | conditional | flops 425984 | bytes 13631904 | solution.py:393
  19.0 1.5 collective-permute-start.6
  21.0 4.5 %collective-permute-done.1 = f32[128,256]{1,0:T(8,128)S(1)} collective-permute-done((f32[128,256]{1,0:T(8,128)S(1)}, f32[128,256]{1,0:T(8,128)S(1)}, u32[]{:S(2)}, u32[]{:S(2)}) %collective-permute-start.1) | collective-permute-done | bytes 131104 | tf_op jit(solution)/shard_map/cond/branch_1_fun/ppermute | solution.py:24
  27.7 1.6 collective-permute-start.7
  29.2 3.8 %collective-permute-done.2 = f32[128,256]{1,0:T(8,128)S(1)} collective-permute-done((f32[128,256]{1,0:T(8,128)S(1)}, f32[128,256]{1,0:T(8,128)S(1)}, u32[]{:S(2)}, u32[]{:S(2)}) %collective-permute-start.2) | collective-permute-done | bytes 131104 | tf_op jit(solution)/shard_map/cond/branch_1_fun/ppermute | solution.py:24
  33.1 1.6 collective-permute-start.3
  35.8 2.6 %collective-permute-start.9 = (bf16[128,1024]{1,0:T(8,128)(2,1)S(1)}, bf16[128,1024]{1,0:T(8,128)(2,1)}, u32[]{:S(2)}, u32[]{:S(2)}) collective-permute-start(bf16[128,1024]{1,0:T(8,128)(2,1)S(1)} %slice.12), channel_id=1, source_target_pairs={{0,8},{1,9},{2,10},{3,11},{4,12},{5,13},{6,14},{7,15},{8,0},{9,1},... | collective-permute-start | bytes 786440 | tf_op jit(solution)/shard_map/cond/branch_1_fun/ppermute | solution.py:24
  38.3 2.2 %collective-permute-done.3 = bf16[1,1,128,256]{3,2,1,0:T(8,128)(2,1)S(1)} collective-permute-done((bf16[1,1,128,256]{3,2,1,0:T(8,128)(2,1)S(1)}, bf16[1,1,128,256]{3,2,1,0:T(8,128)(2,1)S(1)}, u32[]{:S(2)}, u32[]{:S(2)}) %collective-permute-start.3) | collective-permute-done | bytes 65568 | tf_op jit(solution)/shard_map/cond/branch_1_fun/ppermute | solution.py:24
  40.6 1.3 collective-permute-done.4
  42.1 1.8 %collective-permute-done.6.refs_0_ = bf16[512,1024]{1,0:T(8,128)(2,1)} collective-permute-done((bf16[512,1024]{1,0:T(8,128)(2,1)}, bf16[512,1024]{1,0:T(8,128)(2,1)}, u32[]{:S(2)}, u32[]{:S(2)}) %collective-permute-start.6) | collective-permute-done | bytes 1048608 | tf_op jit(solution)/shard_map/cond/branch_1_fun/ppermute | solution.py:24
  44.0 2.0 %column_halves.2 = bf16[512,512]{1,0:T(8,128)(2,1)S(1)} custom-call(s32[1]{0:T(128)} %get-tuple-element.88.idx_ref, bf16[512,1024]{1,0:T(8,128)(2,1)} %collective-permute-done.6.refs_0_), custom_call_target="tpu_custom_call" | custom-call | bytes 65536 | tf_op jit(solution)/shard_map/cond/branch_1_fun/column_halves/pallas_call | solution.py:178
  46.3 1.6 collective-permute-done.9
  48.5 2.5 %collective-permute-start.28 = (bf16[256,1024]{1,0:T(8,128)(2,1)}, bf16[256,1024]{1,0:T(8,128)(2,1)}, u32[]{:S(2)}, u32[]{:S(2)}) collective-permute-start(bf16[256,1024]{1,0:T(8,128)(2,1)} %slice.16), channel_id=1, source_target_pairs={{0,8},{1,9},{2,10},{3,11},{4,12},{5,13},{6,14},{7,15},{8,0},{9,1},... | collective-permute-start | bytes 1572872 | tf_op jit(solution)/shard_map/ppermute | solution.py:24
  51.0 1.8 %column_halves.3 = bf16[512,512]{1,0:T(8,128)(2,1)S(1)} custom-call(s32[1]{0:T(128)S(6)} %sub.3.idx_ref, bf16[128,1024]{1,0:T(8,128)(2,1)S(1)} %collective-permute-done.24.refs_0_.refs_5_, bf16[128,1024]{1,0:T(8,128)(2,1)} %get-tuple-element.194.refs_1_.refs_6_, bf16[128,1024]{1,0:T(8,128)(2,1)S(1)} %collective-permute-done.25.refs_2_.refs_7_, ...), custom_call_target="tpu_custom_call" | custom-call | bytes 65536 | tf_op jit(solution)/shard_map/column_halves/pallas_call | solution.py:178
  53.0 11.9 %forward_chunk.2 = (bf16[512,2048]{1,0:T(8,128)(2,1)}, bf16[256,2048]{1,0:T(8,128)(2,1)}, bf16[256,1024]{1,0:T(8,128)(2,1)}, bf16[256,1024]{1,0:T(8,128)(2,1)}, ...) custom-call(s32[2]{0:T(128)S(1)} %pad_add_fusion.idx_ref, ...), custom_call_target="tpu_custom_call" | custom-call | flops 17179869184 | bytes 71303168 | tf_op jit(solution)/shard_map/forward_chunk/pallas_call | solution.py:146
  65.2 1.7 %collective-permute-start.32 = (bf16[256,2048]{1,0:T(8,128)(2,1)}, bf16[256,2048]{1,0:T(8,128)(2,1)}, u32[]{:S(2)}, u32[]{:S(2)}) collective-permute-start(bf16[256,2048]{1,0:T(8,128)(2,1)} %get-tuple-element.208), channel_id=1, source_target_pairs={{0,16},{16,0},{1,17},{17,1},{2,18},{18,2},{3,19},{19,3},{4,20},{20... | collective-permute-start | bytes 3145736 | tf_op jit(solution)/shard_map/ppermute | solution.py:24
  66.9 5.4 %collective-permute-done.27.refs_5_ = bf16[256,1024]{1,0:T(8,128)(2,1)S(1)} collective-permute-done((bf16[256,1024]{1,0:T(8,128)(2,1)}, bf16[256,1024]{1,0:T(8,128)(2,1)S(1)}, u32[]{:S(2)}, u32[]{:S(2)}) %collective-permute-start.27) | collective-permute-done | bytes 524320 | tf_op jit(solution)/shard_map/ppermute | solution.py:24
  73.0 1.2 collective-permute-start.33
  75.4 2.8 %collective-permute-start.30 = (bf16[256,1024]{1,0:T(8,128)(2,1)}, bf16[256,1024]{1,0:T(8,128)(2,1)}, u32[]{:S(2)}, u32[]{:S(2)}) collective-permute-start(bf16[256,1024]{1,0:T(8,128)(2,1)} %get-tuple-element.206), channel_id=1, source_target_pairs={{0,8},{1,9},{2,10},{3,11},{4,12},{5,13},{6,14},{7,15},{8,0},{9,1},... | collective-permute-start | bytes 1572872 | tf_op jit(solution)/shard_map/ppermute | solution.py:24
  78.2 12.0 %forward_chunk.3 = (bf16[512,2048]{1,0:T(8,128)(2,1)}, bf16[384,2048]{1,0:T(8,128)(2,1)}, bf16[256,1024]{1,0:T(8,128)(2,1)}, bf16[256,1024]{1,0:T(8,128)(2,1)}, ...) custom-call(s32[2]{0:T(128)S(1)} %pad_add_fusion.idx_ref, ...), custom_call_target="tpu_custom_call", output_to_operand_aliasing={{0}: (13, {})} | custom-call | flops 268435456 | bytes 1114112 | tf_op jit(solution)/shard_map/forward_chunk/pallas_call | solution.py:146
  90.3 7.4 %conditional.8 = (f32[128,256]{1,0:T(8,128)S(1)}) conditional(s32[]{:T(128)} %convert_element_type.8, () %tuple.79, (f32[256,256]{1,0:T(8,128)S(1)}, f32[256,256]{1,0:T(8,128)S(1)}) %tuple.80), branch_computations={%region_4.5_spmd, %region_5.6_spmd} | conditional | flops 294920 | bytes 4325554 | solution.py:393
  90.4 1.5 collective-permute-done.10
  92.0 1.3 collective-permute-start.11
  93.3 4.3 %collective-permute-done.11 = f32[128,256]{1,0:T(8,128)S(1)} collective-permute-done((f32[128,256]{1,0:T(8,128)S(1)}, f32[128,256]{1,0:T(8,128)S(1)}, u32[]{:S(2)}, u32[]{:S(2)}) %collective-permute-start.11) | collective-permute-done | bytes 131104 | tf_op jit(solution)/shard_map/cond/branch_1_fun/ppermute | solution.py:24
  98.0 1.4 collective-permute-done.30.refs_8_
  99.5 15.1 %conditional.9 = (bf16[1,1,128,256]{3,2,1,0:T(8,128)(2,1)S(1)}, bf16[256,1024]{1,0:T(8,128)(2,1)}, bf16[256,1024]{1,0:T(8,128)(2,1)}) conditional(s32[]{:T(128)} %convert_element_type.8, () %tuple.78, (f32[128,256]{1,0:T(8,128)S(1)}, bf16[256,1024]{1,0:T(8,128)(2,1)}, bf16[256,1024]{1,0:T(8,128)(2,1)}) %tuple.86), branch_computations={%region_6.7_spmd, %region_7.8_spmd} | conditional | flops 98304 | bytes 5963960 | solution.py:393
  100.2 5.6 %collective-permute-done.12 = f32[128,256]{1,0:T(8,128)S(1)} collective-permute-done((f32[128,256]{1,0:T(8,128)S(1)}, f32[128,256]{1,0:T(8,128)S(1)}, u32[]{:S(2)}, u32[]{:S(2)}) %collective-permute-start.12) | collective-permute-done | bytes 131104 | tf_op jit(solution)/shard_map/cond/branch_1_fun/ppermute | solution.py:24
  106.3 8.3 %collective-permute-done.13 = f32[128,256]{1,0:T(8,128)S(1)} collective-permute-done((f32[128,256]{1,0:T(8,128)S(1)}, f32[128,256]{1,0:T(8,128)S(1)}, u32[]{:S(2)}, u32[]{:S(2)}) %collective-permute-start.13) | collective-permute-done | bytes 131104 | tf_op jit(solution)/shard_map/cond/branch_1_fun/ppermute | solution.py:24
  114.7 1.8 %collective-permute-start.34 = (bf16[256,1024]{1,0:T(8,128)(2,1)}, bf16[256,1024]{1,0:T(8,128)(2,1)}, u32[]{:S(2)}, u32[]{:S(2)}) collective-permute-start(bf16[256,1024]{1,0:T(8,128)(2,1)} %get-tuple-element.228), channel_id=1, source_target_pairs={{0,4},{1,5},{2,6},{3,7},{4,0},{5,1},{6,2},{7,3},{8,12},{9,13},{10,... | collective-permute-start | bytes 1572872 | tf_op jit(solution)/shard_map/ppermute | solution.py:24
  116.5 23.8 %conditional.10 = (bf16[4,2,128,256]{3,2,1,0:T(8,128)(2,1)S(1)}, bf16[256,1024]{1,0:T(8,128)(2,1)}, bf16[256,1024]{1,0:T(8,128)(2,1)}, bf16[512,512]{1,0:T(8,128)(2,1)}, f32[7,128,2048]{2,1,0:T(8,128)}) conditional(s32[]{:T(128)} %convert_element_type.8, () %tuple.77, (bf16[1,1,128,256]{3,2,1,0:T(8,128)(2,1)S(1)}, ...), branch_computations={%region_8.9_spmd, %region_9.10_spmd} | conditional | flops 15033040896 | bytes 68419824 | solution.py:393
  116.5 2.2 %collective-permute-done.17 = bf16[256,1024]{1,0:T(8,128)(2,1)} collective-permute-done((bf16[256,1024]{1,0:T(8,128)(2,1)}, bf16[256,1024]{1,0:T(8,128)(2,1)}, u32[]{:S(2)}, u32[]{:S(2)}) %collective-permute-start.17) | collective-permute-done | bytes 524320 | tf_op jit(solution)/shard_map/cond/branch_1_fun/ppermute | solution.py:24
  119.7 1.3 collective-permute-start.16
  121.0 4.5 %collective-permute-done.16 = bf16[1,2,128,256]{3,2,1,0:T(8,128)(2,1)S(1)} collective-permute-done((bf16[1,2,128,256]{3,2,1,0:T(8,128)(2,1)S(1)}, bf16[1,2,128,256]{3,2,1,0:T(8,128)(2,1)S(1)}, u32[]{:S(2)}, u32[]{:S(2)}) %collective-permute-start.16) | collective-permute-done | bytes 131104 | tf_op jit(solution)/shard_map/cond/branch_1_fun/ppermute | solution.py:24
  125.6 1.3 collective-permute-start.20
  126.9 7.8 %near_weight_grads.1 = f32[7,128,2048]{2,1,0:T(8,128)} custom-call(s32[2]{0:T(128)S(1)} %get-tuple-element.103.idx_ref, bf16[512,1024]{1,0:T(8,128)(2,1)S(1)} %get-tuple-element.104.refs_0_.refs_1_.refs_2_, bf16[512,1024]{1,0:T(8,128)(2,1)S(1)} %get-tuple-element.104.refs_0_.refs_1_.refs_2_, ...), custom_call_target="tpu_custom_call" | custom-call | flops 15032385536 | bytes 58720256 | tf_op jit(solution)/shard_map/cond/branch_1_fun/near_weight_grads/pallas_call | solution.py:254
  135.8 4.5 %collective-permute-done.20 = bf16[256,1024]{1,0:T(8,128)(2,1)} collective-permute-done((bf16[256,1024]{1,0:T(8,128)(2,1)}, bf16[256,1024]{1,0:T(8,128)(2,1)}, u32[]{:S(2)}, u32[]{:S(2)}) %collective-permute-start.20) | collective-permute-done | bytes 524320 | tf_op jit(solution)/shard_map/cond/branch_1_fun/ppermute | solution.py:24
  140.3 5.6 %input_grads.1 = bf16[512,1024]{1,0:T(8,128)(2,1)} custom-call(s32[2]{0:T(128)S(1)} %pad_add_fusion.idx_ref, f32[256,1024]{1,0:T(8,128)} %get-tuple-element.220.refs_0_, f32[256,1024]{1,0:T(8,128)} %get-tuple-element.221.refs_1_, bf16[256,1024]{1,0:T(8,128)(2,1)} %get-tuple-element.222.refs_2_, bf16[256,1024]{1,0:T(8,128)(2,1)} %get-tuple-element.223.refs_3_, ...), custom_call_target="tpu_custom_call" | custom-call | flops 8053063680 | bytes 314572800 | tf_op jit(solution)/shard_map/input_grads/pallas_call | solution.py:341
  145.9 10.9 %conditional.11 = (bf16[4,1,128,256]{3,2,1,0:T(8,128)(2,1)}, bf16[7,128,2048]{2,1,0:T(8,128)(2,1)}, bf16[256,2048]{1,0:T(8,128)(2,1)}) conditional(s32[]{:T(128)} %convert_element_type.8, () %tuple.91, (bf16[4,2,128,256]{3,2,1,0:T(8,128)(2,1)S(1)}, s32[2]{0:T(128)S(1)}, bf16[512,1024]{1,0:T(8,128)(2,1)}, bf16[512,512]{1,0:T(8,128)(2,1)}, ...), branch_computations={%region_10.11_spmd, %region_11.12_spmd} | conditional | flops 184549376 | bytes 4980766 | solution.py:393
  147.7 9.1 %weight_grads.1 = (bf16[7,128,2048]{2,1,0:T(8,128)(2,1)}, bf16[256,2048]{1,0:T(8,128)(2,1)}) custom-call(s32[2]{0:T(128)S(1)} %get-tuple-element.117.idx_ref, bf16[512,1024]{1,0:T(8,128)(2,1)} %get-tuple-element.118.refs_0_.refs_1_.refs_2_, bf16[512,1024]{1,0:T(8,128)(2,1)} %get-tuple-element.118.refs_0_.refs_1_.refs_2_, ...), custom_call_target="tpu_custom_call" | custom-call | flops 184549376 | bytes 917504 | tf_op jit(solution)/shard_map/cond/branch_1_fun/weight_grads/pallas_call | solution.py:284
  156.8 4.7 %left_grads.1 = bf16[1024,256]{1,0:T(8,128)(2,1)} custom-call(s32[2]{0:T(128)S(1)} %pad_add_fusion.idx_ref, bf16[512,1024]{1,0:T(8,128)(2,1)S(1)} %copy-done, bf16[512,1024]{1,0:T(8,128)(2,1)} %get-tuple-element.234.far_tokens_ref, bf16[4,2,128,256]{3,2,1,0:T(8,128)(2,1)S(1)} %get-tuple-element.233.refs_11_.latent_ref, ...), custom_call_target="tpu_custom_call" | custom-call | flops 33554432 | bytes 131072 | tf_op jit(solution)/shard_map/left_grads/pallas_call | solution.py:371
  (85 shorter events, 14.7 us)
Async XLA Ops:
  1.6 17.3 %collective-permute-start.24 = (bf16[128,1024]{1,0:T(8,128)(2,1)S(1)}, bf16[128,1024]{1,0:T(8,128)(2,1)S(1)}, u32[]{:S(2)}, u32[]{:S(2)}) collective-permute-start(bf16[128,1024]{1,0:T(8,128)(2,1)S(1)} %slice.17), channel_id=1, source_target_pairs={{0,4},{1,5},{2,6},{3,7},{4,0},{5,1},{6,2},{7,3},{8,12},{9,13},{10,... | collective-permute-start | bytes 786440 | tf_op jit(solution)/shard_map/ppermute | solution.py:24
  4.7 14.3 %collective-permute-start.25 = (bf16[128,1024]{1,0:T(8,128)(2,1)S(1)}, bf16[128,1024]{1,0:T(8,128)(2,1)S(1)}, u32[]{:S(2)}, u32[]{:S(2)}) collective-permute-start(bf16[128,1024]{1,0:T(8,128)(2,1)S(1)} %slice.17), channel_id=1, source_target_pairs={{0,8},{1,9},{2,10},{3,11},{4,12},{5,13},{6,14},{7,15},{8,0},{9,1},... | collective-permute-start | bytes 786440 | tf_op jit(solution)/shard_map/ppermute | solution.py:24
  9.2 3.6 %copy-start.1 = (bf16[512,1024]{1,0:T(8,128)(2,1)S(1)}, bf16[512,1024]{1,0:T(8,128)(2,1)}, u32[]{:S(2)}) copy-start(bf16[512,1024]{1,0:T(8,128)(2,1)} %get-tuple-element.85) | copy-start | bytes 3145732 | tf_op jit(solution)/shard_map/cond
  11.1 1.6 collective-permute-start.21
  12.8 6.1 %collective-permute-start.23 = (bf16[512,1024]{1,0:T(8,128)(2,1)S(1)}, bf16[512,1024]{1,0:T(8,128)(2,1)}, u32[]{:S(2)}, u32[]{:S(2)}) collective-permute-start(bf16[512,1024]{1,0:T(8,128)(2,1)S(1)} %copy-done.1), channel_id=1, source_target_pairs={{0,1},{1,0},{2,3},{3,2},{4,5},{5,4},{6,7},{7,6},{8,9},{9,8},{10,11... | collective-permute-start | bytes 3145736 | tf_op jit(solution)/shard_map/cond/branch_1_fun/ppermute | solution.py:24
  13.0 5.8 %collective-permute-start.22 = (f32[128,256]{1,0:T(8,128)S(1)}, f32[128,256]{1,0:T(8,128)S(1)}, u32[]{:S(2)}, u32[]{:S(2)}) collective-permute-start(f32[128,256]{1,0:T(8,128)S(1)} %slice_select_fusion.1), channel_id=1, source_target_pairs={{0,2},{1,3},{2,0},{3,1},{4,6},{5,7},{6,4},{7,5},{8,10},{9,11},{10,... | collective-permute-start | bytes 393224 | tf_op jit(solution)/shard_map/cond/branch_1_fun/ppermute | solution.py:24
  18.9 32.0 %copy-start.8 = (bf16[128,1024]{1,0:T(8,128)(2,1)}, bf16[128,1024]{1,0:T(8,128)(2,1)S(1)}, u32[]{:S(2)}) copy-start(bf16[128,1024]{1,0:T(8,128)(2,1)S(1)} %collective-permute-done.24.refs_0_.refs_5_) | copy-start | bytes 786436
  19.0 32.0 %copy-start.9 = (bf16[128,1024]{1,0:T(8,128)(2,1)}, bf16[128,1024]{1,0:T(8,128)(2,1)S(1)}, u32[]{:S(2)}) copy-start(bf16[128,1024]{1,0:T(8,128)(2,1)S(1)} %collective-permute-done.25.refs_2_.refs_7_) | copy-start | bytes 786436
  19.0 24.9 %collective-permute-start.6 = (bf16[512,1024]{1,0:T(8,128)(2,1)}, bf16[512,1024]{1,0:T(8,128)(2,1)}, u32[]{:S(2)}, u32[]{:S(2)}) collective-permute-start(bf16[512,1024]{1,0:T(8,128)(2,1)} %get-tuple-element.87), channel_id=1, source_target_pairs={{0,16},{16,0},{1,17},{17,1},{2,18},{18,2},{3,19},{19,3},{4,20},{20... | collective-permute-start | bytes 3145736 | tf_op jit(solution)/shard_map/cond/branch_1_fun/ppermute | solution.py:24
  20.5 5.0 %collective-permute-start.1 = (f32[128,256]{1,0:T(8,128)S(1)}, f32[128,256]{1,0:T(8,128)S(1)}, u32[]{:S(2)}, u32[]{:S(2)}) collective-permute-start(f32[128,256]{1,0:T(8,128)S(1)} %get-tuple-element.86), channel_id=1, source_target_pairs={{0,4},{1,5},{2,6},{3,7},{4,0},{5,1},{6,2},{7,3},{8,12},{9,13},{10,... | collective-permute-start | bytes 393224 | tf_op jit(solution)/shard_map/cond/branch_1_fun/ppermute | solution.py:24
  25.5 7.6 %collective-permute-start.2 = (f32[128,256]{1,0:T(8,128)S(1)}, f32[128,256]{1,0:T(8,128)S(1)}, u32[]{:S(2)}, u32[]{:S(2)}) collective-permute-start(f32[128,256]{1,0:T(8,128)S(1)} %add.20), channel_id=1, source_target_pairs={{0,8},{1,9},{2,10},{3,11},{4,12},{5,13},{6,14},{7,15},{8,0},{9,1},... | collective-permute-start | bytes 393224 | tf_op jit(solution)/shard_map/cond/branch_1_fun/ppermute | solution.py:24
  27.7 20.3 %collective-permute-start.7 = (bf16[256,1024]{1,0:T(8,128)(2,1)S(1)}, bf16[256,1024]{1,0:T(8,128)(2,1)}, u32[]{:S(2)}, u32[]{:S(2)}) collective-permute-start(bf16[256,1024]{1,0:T(8,128)(2,1)S(1)} %slice.6), channel_id=1, source_target_pairs={{0,2},{1,3},{2,0},{3,1},{4,6},{5,7},{6,4},{7,5},{8,10},{9,11},{10,... | collective-permute-start | bytes 1572872 | tf_op jit(solution)/shard_map/cond/branch_1_fun/ppermute | solution.py:24
  33.1 7.4 %collective-permute-start.3 = (bf16[1,1,128,256]{3,2,1,0:T(8,128)(2,1)S(1)}, bf16[1,1,128,256]{3,2,1,0:T(8,128)(2,1)S(1)}, u32[]{:S(2)}, u32[]{:S(2)}) collective-permute-start(bf16[1,1,128,256]{3,2,1,0:T(8,128)(2,1)S(1)} %fusion), channel_id=1, source_target_pairs={{0,2},{1,3},{2,0},{3,1},{4,6},{5,7},{6,4},{7,5},{8,10},{9,11},{10,... | collective-permute-start | bytes 196616 | tf_op jit(solution)/shard_map/cond/branch_1_fun/ppermute | solution.py:24
  35.7 10.7 %collective-permute-start.8 = (bf16[128,1024]{1,0:T(8,128)(2,1)S(1)}, bf16[128,1024]{1,0:T(8,128)(2,1)}, u32[]{:S(2)}, u32[]{:S(2)}) collective-permute-start(bf16[128,1024]{1,0:T(8,128)(2,1)S(1)} %slice.12), channel_id=1, source_target_pairs={{0,4},{1,5},{2,6},{3,7},{4,0},{5,1},{6,2},{7,3},{8,12},{9,13},{10,... | collective-permute-start | bytes 786440 | tf_op jit(solution)/shard_map/cond/branch_1_fun/ppermute | solution.py:24
  35.8 12.2 %collective-permute-start.9 = (bf16[128,1024]{1,0:T(8,128)(2,1)S(1)}, bf16[128,1024]{1,0:T(8,128)(2,1)}, u32[]{:S(2)}, u32[]{:S(2)}) collective-permute-start(bf16[128,1024]{1,0:T(8,128)(2,1)S(1)} %slice.12), channel_id=1, source_target_pairs={{0,8},{1,9},{2,10},{3,11},{4,12},{5,13},{6,14},{7,15},{8,0},{9,1},... | collective-permute-start | bytes 786440 | tf_op jit(solution)/shard_map/cond/branch_1_fun/ppermute | solution.py:24
  40.6 1.4 collective-permute-start.4
  42.0 4.4 %collective-permute-start.5 = (bf16[1,1,128,256]{3,2,1,0:T(8,128)(2,1)S(1)}, bf16[1,1,128,256]{3,2,1,0:T(8,128)(2,1)}, u32[]{:S(2)}, u32[]{:S(2)}) collective-permute-start(bf16[1,1,128,256]{3,2,1,0:T(8,128)(2,1)S(1)} %fusion), channel_id=1, source_target_pairs={{0,16},{16,0},{1,17},{17,1},{2,18},{18,2},{3,19},{19,3},{4,20},{20... | collective-permute-start | bytes 196616 | tf_op jit(solution)/shard_map/cond/branch_1_fun/ppermute | solution.py:24
  48.0 5.1 %copy-start.7 = (bf16[512,512]{1,0:T(8,128)(2,1)}, bf16[512,512]{1,0:T(8,128)(2,1)S(1)}, u32[]{:S(2)}) copy-start(bf16[512,512]{1,0:T(8,128)(2,1)S(1)} %get-tuple-element.210) | copy-start | bytes 1572868
  48.0 18.9 %collective-permute-start.26 = (bf16[256,1024]{1,0:T(8,128)(2,1)}, bf16[256,1024]{1,0:T(8,128)(2,1)S(1)}, u32[]{:S(2)}, u32[]{:S(2)}) collective-permute-start(bf16[256,1024]{1,0:T(8,128)(2,1)} %slice.16), channel_id=1, source_target_pairs={{0,2},{1,3},{2,0},{3,1},{4,6},{5,7},{6,4},{7,5},{8,10},{9,11},{10,... | collective-permute-start | bytes 1572872 | tf_op jit(solution)/shard_map/ppermute | solution.py:24
  48.5 23.8 %collective-permute-start.27 = (bf16[256,1024]{1,0:T(8,128)(2,1)}, bf16[256,1024]{1,0:T(8,128)(2,1)S(1)}, u32[]{:S(2)}, u32[]{:S(2)}) collective-permute-start(bf16[256,1024]{1,0:T(8,128)(2,1)} %slice.16), channel_id=1, source_target_pairs={{0,4},{1,5},{2,6},{3,7},{4,0},{5,1},{6,2},{7,3},{8,12},{9,13},{10,... | collective-permute-start | bytes 1572872 | tf_op jit(solution)/shard_map/ppermute | solution.py:24
  48.5 23.8 %collective-permute-start.28 = (bf16[256,1024]{1,0:T(8,128)(2,1)}, bf16[256,1024]{1,0:T(8,128)(2,1)}, u32[]{:S(2)}, u32[]{:S(2)}) collective-permute-start(bf16[256,1024]{1,0:T(8,128)(2,1)} %slice.16), channel_id=1, source_target_pairs={{0,8},{1,9},{2,10},{3,11},{4,12},{5,13},{6,14},{7,15},{8,0},{9,1},... | collective-permute-start | bytes 1572872 | tf_op jit(solution)/shard_map/ppermute | solution.py:24
  52.8 12.3 %collective-permute-start.31 = (bf16[512,512]{1,0:T(8,128)(2,1)S(1)}, bf16[512,512]{1,0:T(8,128)(2,1)S(1)}, u32[]{:S(2)}, u32[]{:S(2)}) collective-permute-start(bf16[512,512]{1,0:T(8,128)(2,1)S(1)} %column_halves.3), channel_id=1, source_target_pairs={{0,16},{16,0},{1,17},{17,1},{2,18},{18,2},{3,19},{19,3},{4,20},{20... | collective-permute-start | bytes 1572872 | tf_op jit(solution)/shard_map/ppermute | solution.py:24
  53.0 25.2 %copy-start = (bf16[512,1024]{1,0:T(8,128)(2,1)S(1)}, bf16[512,1024]{1,0:T(8,128)(2,1)}, u32[]{:S(2)}) copy-start(bf16[512,1024]{1,0:T(8,128)(2,1)} %tokens_ref.1) | copy-start | bytes 3145732
  65.2 25.1 %copy-start.2 = (bf16[512,512]{1,0:T(8,128)(2,1)}, bf16[512,512]{1,0:T(8,128)(2,1)S(1)}, u32[]{:S(2)}) copy-start(bf16[512,512]{1,0:T(8,128)(2,1)S(1)} %collective-permute-done.31) | copy-start | bytes 1572868
  65.2 34.3 %collective-permute-start.32 = (bf16[256,2048]{1,0:T(8,128)(2,1)}, bf16[256,2048]{1,0:T(8,128)(2,1)}, u32[]{:S(2)}, u32[]{:S(2)}) collective-permute-start(bf16[256,2048]{1,0:T(8,128)(2,1)} %get-tuple-element.208), channel_id=1, source_target_pairs={{0,16},{16,0},{1,17},{17,1},{2,18},{18,2},{3,19},{19,3},{4,20},{20... | collective-permute-start | bytes 3145736 | tf_op jit(solution)/shard_map/ppermute | solution.py:24
  66.9 23.4 %copy-start.5 = (bf16[256,1024]{1,0:T(8,128)(2,1)}, bf16[256,1024]{1,0:T(8,128)(2,1)S(1)}, u32[]{:S(2)}) copy-start(bf16[256,1024]{1,0:T(8,128)(2,1)S(1)} %collective-permute-done.26.refs_4_) | copy-start | bytes 1572868
  72.2 0.8 copy-start.6
  73.0 25.0 %collective-permute-start.33 = (bf16[512,512]{1,0:T(8,128)(2,1)}, bf16[512,512]{1,0:T(8,128)(2,1)S(1)}, u32[]{:S(2)}, u32[]{:S(2)}) collective-permute-start(bf16[512,512]{1,0:T(8,128)(2,1)} %copy-done.7), channel_id=1, source_target_pairs={{0,2},{1,3},{2,0},{3,1},{4,6},{5,7},{6,4},{7,5},{8,10},{9,11},{10,... | collective-permute-start | bytes 1572872 | tf_op jit(solution)/shard_map/ppermute | solution.py:24
  74.3 23.8 %collective-permute-start.29 = (bf16[256,1024]{1,0:T(8,128)(2,1)}, bf16[256,1024]{1,0:T(8,128)(2,1)}, u32[]{:S(2)}, u32[]{:S(2)}) collective-permute-start(bf16[256,1024]{1,0:T(8,128)(2,1)} %get-tuple-element.204), channel_id=1, source_target_pairs={{0,4},{1,5},{2,6},{3,7},{4,0},{5,1},{6,2},{7,3},{8,12},{9,13},{10,... | collective-permute-start | bytes 1572872 | tf_op jit(solution)/shard_map/ppermute | solution.py:24
  75.4 24.0 %collective-permute-start.30 = (bf16[256,1024]{1,0:T(8,128)(2,1)}, bf16[256,1024]{1,0:T(8,128)(2,1)}, u32[]{:S(2)}, u32[]{:S(2)}) collective-permute-start(bf16[256,1024]{1,0:T(8,128)(2,1)} %get-tuple-element.206), channel_id=1, source_target_pairs={{0,8},{1,9},{2,10},{3,11},{4,12},{5,13},{6,14},{7,15},{8,0},{9,1},... | collective-permute-start | bytes 1572872 | tf_op jit(solution)/shard_map/ppermute | solution.py:24
  90.3 1.6 collective-permute-start.10
  92.0 5.6 %collective-permute-start.11 = (f32[128,256]{1,0:T(8,128)S(1)}, f32[128,256]{1,0:T(8,128)S(1)}, u32[]{:S(2)}, u32[]{:S(2)}) collective-permute-start(f32[128,256]{1,0:T(8,128)S(1)} %slice_select_fusion.2), channel_id=1, source_target_pairs={{0,2},{1,3},{2,0},{3,1},{4,6},{5,7},{6,4},{7,5},{8,10},{9,11},{10,... | collective-permute-start | bytes 393224 | tf_op jit(solution)/shard_map/cond/branch_1_fun/ppermute | solution.py:24
  97.6 48.2 %collective-permute-start.36 = (bf16[384,2048]{1,0:T(8,128)(2,1)}, bf16[384,2048]{1,0:T(8,128)(2,1)S(1)}, u32[]{:S(2)}, u32[]{:S(2)}) collective-permute-start(bf16[384,2048]{1,0:T(8,128)(2,1)} %get-tuple-element.218), channel_id=1, source_target_pairs={{0,16},{16,0},{1,17},{17,1},{2,18},{18,2},{3,19},{19,3},{4,20},{20... | collective-permute-start | bytes 4718600 | tf_op jit(solution)/shard_map/ppermute | solution.py:24
  98.0 18.5 %copy-start.4 = (bf16[512,512]{1,0:T(8,128)(2,1)}, bf16[512,512]{1,0:T(8,128)(2,1)S(1)}, u32[]{:S(2)}) copy-start(bf16[512,512]{1,0:T(8,128)(2,1)S(1)} %collective-permute-done.33) | copy-start | bytes 1572868
  99.5 15.1 %collective-permute-start.14 = (bf16[256,1024]{1,0:T(8,128)(2,1)}, bf16[256,1024]{1,0:T(8,128)(2,1)}, u32[]{:S(2)}, u32[]{:S(2)}) collective-permute-start(bf16[256,1024]{1,0:T(8,128)(2,1)} %get-tuple-element.93), channel_id=1, source_target_pairs={{0,1},{1,0},{2,3},{3,2},{4,5},{5,4},{6,7},{7,6},{8,9},{9,8},{10,11... | collective-permute-start | bytes 1572872 | tf_op jit(solution)/shard_map/cond/branch_1_fun/ppermute | solution.py:24
  99.5 15.1 %collective-permute-start.15 = (bf16[256,1024]{1,0:T(8,128)(2,1)}, bf16[256,1024]{1,0:T(8,128)(2,1)}, u32[]{:S(2)}, u32[]{:S(2)}) collective-permute-start(bf16[256,1024]{1,0:T(8,128)(2,1)} %get-tuple-element.94), channel_id=1, source_target_pairs={{0,2},{1,3},{2,0},{3,1},{4,6},{5,7},{6,4},{7,5},{8,10},{9,11},{10,... | collective-permute-start | bytes 1572872 | tf_op jit(solution)/shard_map/cond/branch_1_fun/ppermute | solution.py:24
  100.2 5.6 %collective-permute-start.12 = (f32[128,256]{1,0:T(8,128)S(1)}, f32[128,256]{1,0:T(8,128)S(1)}, u32[]{:S(2)}, u32[]{:S(2)}) collective-permute-start(f32[128,256]{1,0:T(8,128)S(1)} %get-tuple-element.92), channel_id=1, source_target_pairs={{0,4},{1,5},{2,6},{3,7},{4,0},{5,1},{6,2},{7,3},{8,12},{9,13},{10,... | collective-permute-start | bytes 393224 | tf_op jit(solution)/shard_map/cond/branch_1_fun/ppermute | solution.py:24
  105.9 8.7 %collective-permute-start.13 = (f32[128,256]{1,0:T(8,128)S(1)}, f32[128,256]{1,0:T(8,128)S(1)}, u32[]{:S(2)}, u32[]{:S(2)}) collective-permute-start(f32[128,256]{1,0:T(8,128)S(1)} %add.24), channel_id=1, source_target_pairs={{0,8},{1,9},{2,10},{3,11},{4,12},{5,13},{6,14},{7,15},{8,0},{9,1},... | collective-permute-start | bytes 393224 | tf_op jit(solution)/shard_map/cond/branch_1_fun/ppermute | solution.py:24
  114.6 25.7 %collective-permute-start.35 = (bf16[256,1024]{1,0:T(8,128)(2,1)}, bf16[256,1024]{1,0:T(8,128)(2,1)}, u32[]{:S(2)}, u32[]{:S(2)}) collective-permute-start(bf16[256,1024]{1,0:T(8,128)(2,1)} %get-tuple-element.231), channel_id=1, source_target_pairs={{0,8},{1,9},{2,10},{3,11},{4,12},{5,13},{6,14},{7,15},{8,0},{9,1},... | collective-permute-start | bytes 1572872 | tf_op jit(solution)/shard_map/ppermute | solution.py:24
  114.7 25.6 %collective-permute-start.34 = (bf16[256,1024]{1,0:T(8,128)(2,1)}, bf16[256,1024]{1,0:T(8,128)(2,1)}, u32[]{:S(2)}, u32[]{:S(2)}) collective-permute-start(bf16[256,1024]{1,0:T(8,128)(2,1)} %get-tuple-element.228), channel_id=1, source_target_pairs={{0,4},{1,5},{2,6},{3,7},{4,0},{5,1},{6,2},{7,3},{8,12},{9,13},{10,... | collective-permute-start | bytes 1572872 | tf_op jit(solution)/shard_map/ppermute | solution.py:24
  116.5 2.3 %collective-permute-start.17 = (bf16[256,1024]{1,0:T(8,128)(2,1)}, bf16[256,1024]{1,0:T(8,128)(2,1)}, u32[]{:S(2)}, u32[]{:S(2)}) collective-permute-start(bf16[256,1024]{1,0:T(8,128)(2,1)} %get-tuple-element.98), channel_id=1, source_target_pairs={{0,1},{1,0},{2,3},{3,2},{4,5},{5,4},{6,7},{7,6},{8,9},{9,8},{10,11... | collective-permute-start | bytes 1572872 | tf_op jit(solution)/shard_map/cond/branch_1_fun/ppermute | solution.py:24
  118.7 6.8 %collective-permute-start.18 = (bf16[512,512]{1,0:T(8,128)(2,1)}, bf16[512,512]{1,0:T(8,128)(2,1)}, u32[]{:S(2)}, u32[]{:S(2)}) collective-permute-start(bf16[512,512]{1,0:T(8,128)(2,1)} %get-tuple-element.99), channel_id=1, source_target_pairs={{0,1},{1,0},{2,3},{3,2},{4,5},{5,4},{6,7},{7,6},{8,9},{9,8},{10,11... | collective-permute-start | bytes 1572872 | tf_op jit(solution)/shard_map/cond/branch_1_fun/ppermute | solution.py:24
  119.7 5.8 %collective-permute-start.16 = (bf16[1,2,128,256]{3,2,1,0:T(8,128)(2,1)S(1)}, bf16[1,2,128,256]{3,2,1,0:T(8,128)(2,1)S(1)}, u32[]{:S(2)}, u32[]{:S(2)}) collective-permute-start(bf16[1,2,128,256]{3,2,1,0:T(8,128)(2,1)S(1)} %constant_dynamic-update-slice_fusion), channel_id=1, source_target_pairs={{0,2},{1,3},{2,0},{3,1},{4,6},{5,7},{6,4},{7,5},{8,10},{9,11},{10,... | collective-permute-start | bytes 393224 | tf_op jit(solution)/shard_map/cond/branch_1_fun/ppermute | solution.py:24
  125.5 9.2 %collective-permute-start.19 = (bf16[2,2,128,256]{3,2,1,0:T(8,128)(2,1)S(1)}, bf16[2,2,128,256]{3,2,1,0:T(8,128)(2,1)}, u32[]{:S(2)}, u32[]{:S(2)}) collective-permute-start(bf16[2,2,128,256]{3,2,1,0:T(8,128)(2,1)S(1)} %pad_maximum_fusion.3), channel_id=1, source_target_pairs={{0,1},{1,0},{2,3},{3,2},{4,5},{5,4},{6,7},{7,6},{8,9},{9,8},{10,11... | collective-permute-start | bytes 786440 | tf_op jit(solution)/shard_map/cond/branch_1_fun/ppermute | solution.py:24
  125.6 14.7 %collective-permute-start.20 = (bf16[256,1024]{1,0:T(8,128)(2,1)}, bf16[256,1024]{1,0:T(8,128)(2,1)}, u32[]{:S(2)}, u32[]{:S(2)}) collective-permute-start(bf16[256,1024]{1,0:T(8,128)(2,1)} %get-tuple-element.102), channel_id=1, source_target_pairs={{0,2},{1,3},{2,0},{3,1},{4,6},{5,7},{6,4},{7,5},{8,10},{9,11},{10,... | collective-permute-start | bytes 1572872 | tf_op jit(solution)/shard_map/cond/branch_1_fun/ppermute | solution.py:24
  140.3 5.6 %copy-start.3 = (bf16[512,512]{1,0:T(8,128)(2,1)S(1)}, bf16[512,512]{1,0:T(8,128)(2,1)}, u32[]{:S(2)}) copy-start(bf16[512,512]{1,0:T(8,128)(2,1)} %copy-done.2) | copy-start | bytes 1572868
  146.6 10.2 %collective-permute-start = (bf16[4,1,128,256]{3,2,1,0:T(8,128)(2,1)}, bf16[4,1,128,256]{3,2,1,0:T(8,128)(2,1)}, u32[]{:S(2)}, u32[]{:S(2)}) collective-permute-start(bf16[4,1,128,256]{3,2,1,0:T(8,128)(2,1)} %slice.13), channel_id=1, source_target_pairs={{0,16},{16,0},{1,17},{17,1},{2,18},{18,2},{3,19},{19,3},{4,20},{20... | collective-permute-start | bytes 786440 | tf_op jit(solution)/shard_map/cond/branch_1_fun/ppermute | solution.py:24

commit v3 on v2

--- a/solution.py
+++ b/solution.py
@@ -11,11 +11,10 @@
 gelu_cubic = 0.044715
 f32 = jnp.float32
 bf16 = jnp.bfloat16
-NEAR_HINT = 8
 FORWARD_HINTS = (4, 1 / 16)
 WEIGHT_HINT = 1 / 16
-INPUT_HINT = 30
-LEFT_HINT = 1 / 16
+INPUT_HINT = 1 / 16
+STACK_HINT = 458752
 NT = (((1,), (1,)), ((), ()))
 TN = (((0,), (0,)), ((), ()))
 
@@ -197,31 +196,26 @@
     return jnp.concatenate([jnp.where(first, near, far), jnp.where(first, far, near)], axis=0)
 
 
-def near_body(local_taps, pieces, idx_ref, *refs):
+def weights_body(local_taps, pieces, far_pieces, packed, idx_ref, *refs):
     take = taken(refs)
     own = [r[...] for r in take(local_taps)]
     remote = [rows_of(take(n)) for n in pieces]
-    grad = rows_of(take(2))
-    sum_ref = refs[-1]
-    total = lax.dot_general(jnp.concatenate(own + remote, axis=1), grad, TN, preferred_element_type=f32)
-    sum_ref[...] = total.reshape(sum_ref.shape)
-
-
-def far_body(local_taps, pieces, packed, idx_ref, *refs):
-    take = taken(refs)
-    own = [r[...] for r in take(local_taps)]
-    remote = [rows_of(take(n)) for n in pieces]
+    far_own = [r[...] for r in take(local_taps)]
+    far_remote = [rows_of(take(n)) for n in far_pieces]
     pack_ref = take(1)[0]
-    half = own[0].shape[1]
+    half = far_own[0].shape[1]
     cells = [pack_ref[:, lo : lo + half] for lo in range(0, pack_ref.shape[1], half)]
     count = len(cells) // packed
     for k in range(packed):
-        tap = len(remote) - packed + k
-        remote[tap] = jnp.concatenate([remote[tap]] + cells[k * count : (k + 1) * count], axis=0)
+        tap = len(far_remote) - packed + k
+        far_remote[tap] = jnp.concatenate([far_remote[tap]] + cells[k * count : (k + 1) * count], axis=0)
     grad, far_grad = rows_of(take(2)), rows_of(take(2))
-    latent_ref, far_latent_ref, near_ref, weight_ref, right_ref = take(5)
-    total = lax.dot_general(jnp.concatenate(own + remote, axis=1), far_grad, TN, preferred_element_type=f32)
-    weight_ref[...] = (near_ref[...] + total.reshape(weight_ref.shape)).astype(bf16)
+    latent_ref, far_latent_ref, weight_ref, right_ref = take(4)
+    total = lax.dot_general(jnp.concatenate(own + remote, axis=1), grad, TN, preferred_element_type=f32)
+    total = total + lax.dot_general(
+        jnp.concatenate(far_own + far_remote, axis=1), far_grad, TN, preferred_element_type=f32
+    )
+    weight_ref[...] = total.reshape(weight_ref.shape).astype(bf16)
     order = [k ^ idx_ref[0] for k in range(latent_ref.shape[0])]
     latent = jnp.concatenate([latent_ref[k] for k in order], axis=0)
     far_latent = jnp.concatenate([far_latent_ref[k] for k in order], axis=0)
@@ -230,68 +224,43 @@
     right_ref[...] = right.astype(bf16)
 
 
-def weight_specs(tokens, grads, taps, block):
+def weight_grads(idx, tokens, remote, far_tokens, far_remote, grads, latent, far_latent, taps, block):
     rows, width = tokens.shape
     chunk_rows, hidden_local = grads[0].shape
     groups = width // block
     half = block // 2
     hidden = hidden_local // groups
-    own_spec = lambda k: pl.BlockSpec(
-        (rows, half), lambda g, idx: (0, 2 * (g if k == 0 else g ^ (1 << (k - 1))) + idx[1])
-    )
-    grad_spec = pl.BlockSpec((chunk_rows, hidden), lambda g, idx: (0, g))
-    sum_spec = pl.BlockSpec((taps, half, hidden), lambda g, idx: (0, 0, g))
-    return rows, chunk_rows, hidden_local, groups, half, hidden, own_spec, grad_spec, sum_spec
-
-
-def near_weight_grads(idx, tokens, remote, grads, taps, block):
-    rows, _, hidden_local, groups, half, _, own_spec, grad_spec, sum_spec = weight_specs(
-        tokens, grads, taps, block
-    )
-    local_taps = taps - len(remote)
-    piece_spec = lambda p: pl.BlockSpec((p[2], half), lambda g, idx: (p[1], 2 * g + idx[1]))
-    pieces = [p for tap in remote for p in tap]
-    return pl.pallas_call(
-        functools.partial(near_body, local_taps, [len(t) for t in remote]),
-        grid_spec=pltpu.PrefetchScalarGridSpec(
-            num_scalar_prefetch=1,
-            grid=(groups,),
-            in_specs=[own_spec(k) for k in range(local_taps)]
-            + [piece_spec(p) for p in pieces]
-            + [grad_spec] * 2,
-            out_specs=sum_spec,
-        ),
-        out_shape=jax.ShapeDtypeStruct((taps, half, hidden_local), f32),
-        compiler_params=params(),
-        cost_estimate=cost(
-            NEAR_HINT, 2 * rows * hidden_local * taps * half, 4 * taps * half * hidden_local
-        ),
-        name="near_weight_grads",
-    )(idx, *([tokens] * local_taps), *[p[0] for p in pieces], *grads)
-
-
-def weight_grads(idx, near, tokens, remote, grads, latent, far_latent, taps, block):
-    rows, chunk_rows, hidden_local, groups, half, hidden, own_spec, grad_spec, sum_spec = weight_specs(
-        tokens, grads, taps, block
-    )
     local_taps = taps - len(remote)
     rank = latent[0].shape[3]
     pack = grads[-1]
     height = pack.shape[0] - chunk_rows
     packed = height * hidden // (chunk_rows * half)
-    piece_spec = lambda p: pl.BlockSpec((p[2], half), lambda g, idx: (p[1], g))
+    own_spec = lambda k: pl.BlockSpec(
+        (rows, half), lambda g, idx: (0, 2 * (g if k == 0 else g ^ (1 << (k - 1))) + idx[1])
+    )
+    own_specs = [own_spec(k) for k in range(local_taps)]
+    near_spec = lambda p: pl.BlockSpec((p[2], half), lambda g, idx: (p[1], 2 * g + idx[1]))
+    far_spec = lambda p: pl.BlockSpec((p[2], half), lambda g, idx: (p[1], g))
     pieces = [p for tap in remote for p in tap]
+    far_pieces = [p for tap in far_remote for p in tap]
     return pl.pallas_call(
-        functools.partial(far_body, local_taps, [len(t) for t in remote], packed),
+        functools.partial(
+            weights_body, local_taps, [len(t) for t in remote], [len(t) for t in far_remote], packed
+        ),
         grid_spec=pltpu.PrefetchScalarGridSpec(
             num_scalar_prefetch=1,
             grid=(groups,),
-            in_specs=[own_spec(k) for k in range(local_taps)]
-            + [piece_spec(p) for p in pieces]
+            in_specs=own_specs
+            + [near_spec(p) for p in pieces]
+            + own_specs
+            + [far_spec(p) for p in far_pieces]
             + [pl.BlockSpec((height, hidden), lambda g, idx: (chunk_rows // height, g))]
-            + [grad_spec] * 4
-            + [latent_spec(latent), latent_spec(far_latent), sum_spec],
-            out_specs=[sum_spec, pl.BlockSpec((rank, hidden), lambda g, idx: (0, g))],
+            + [pl.BlockSpec((chunk_rows, hidden), lambda g, idx: (0, g))] * 4
+            + [latent_spec(latent), latent_spec(far_latent)],
+            out_specs=[
+                pl.BlockSpec((taps, half, hidden), lambda g, idx: (0, 0, g)),
+                pl.BlockSpec((rank, hidden), lambda g, idx: (0, g)),
+            ],
         ),
         out_shape=[
             jax.ShapeDtypeStruct((taps, half, hidden_local), bf16),
@@ -299,21 +268,34 @@
         ],
         compiler_params=params(),
         cost_estimate=cost(
-            WEIGHT_HINT,
-            2 * rows * hidden_local * (taps * half + 2 * rank),
-            8 * taps * half * hidden_local,
+            WEIGHT_HINT, 4 * rows * hidden_local * (taps * half + rank), 8 * taps * half * hidden_local
         ),
         name="weight_grads",
     )(
         idx,
         *([tokens] * local_taps),
         *[p[0] for p in pieces],
+        *([far_tokens] * local_taps),
+        *[p[0] for p in far_pieces],
         pack,
         *grads,
         latent[0],
         far_latent[0],
-        near,
-    )
+    )
+
+
+def stack_body(first_ref, second_ref, out_ref):
+    out_ref[:, :1] = first_ref[...]
+    out_ref[:, 1:] = second_ref[...]
+
+
+def stacked(first, second):
+    return pl.pallas_call(
+        stack_body,
+        out_shape=jax.ShapeDtypeStruct((first.shape[0], 2) + first.shape[2:], bf16),
+        cost_estimate=cost(STACK_HINT, first.size, 4 * first.size),
+        name="stacked",
+    )(first, second)
 
 
 def inputs_body(n_terms, idx_ref, *refs):
@@ -321,10 +303,16 @@
     total = rows_of(take(2))
     for _ in range(n_terms):
         total = total + rows_of(take(2)).astype(f32)
-    left_ref, latent_ref, input_ref = take(3)
-    latent = jnp.concatenate([latent_ref[k ^ idx_ref[0]] for k in range(latent_ref.shape[0])], axis=0)
+    left_ref, latent_ref, far_latent_ref, tokens_ref, far_tokens_ref, input_ref, left_grad_ref = take(7)
+    order = [k ^ idx_ref[0] for k in range(latent_ref.shape[0])]
+    latent = jnp.concatenate([latent_ref[k] for k in order], axis=0)
+    far_latent = jnp.concatenate([far_latent_ref[k] for k in order], axis=0)
     low_rank = lax.dot_general(latent, left_ref[...], NT, preferred_element_type=f32)
     input_ref[...] = (total + low_rank).astype(bf16)
+    tokens = in_dp_order(idx_ref, tokens_ref[...], far_tokens_ref[...])
+    latents = in_dp_order(idx_ref, latent, far_latent)
+    left = lax.dot_general(tokens, latents, TN, preferred_element_type=f32)
+    left_grad_ref[...] = left.astype(bf16)
 
 
 def latent_spec(pair):
@@ -333,54 +321,39 @@
     )
 
 
-def input_grads(idx, local, terms, left, latent, block):
+def input_grads(idx, local, terms, left, latent, far_latent, tokens, far_tokens, block):
     width, rank = left.shape
     chunk_rows = local[0].shape[0]
     rows = 2 * chunk_rows
     chunk_spec = pl.BlockSpec((chunk_rows, block), lambda g, idx: (0, g))
+    token_spec = pl.BlockSpec((rows, block), lambda g, idx: (0, g))
+    left_spec = pl.BlockSpec((block, rank), lambda g, idx: (g, 0))
     return pl.pallas_call(
         functools.partial(inputs_body, len(terms)),
         grid_spec=pltpu.PrefetchScalarGridSpec(
             num_scalar_prefetch=1,
             grid=(width // block,),
             in_specs=[chunk_spec] * (2 + 2 * len(terms))
-            + [pl.BlockSpec((block, rank), lambda g, idx: (g, 0)), latent_spec(latent)],
-            out_specs=pl.BlockSpec((rows, block), lambda g, idx: (0, g)),
-        ),
-        out_shape=jax.ShapeDtypeStruct((rows, width), bf16),
+            + [left_spec, latent_spec(latent), latent_spec(far_latent), token_spec, token_spec],
+            out_specs=[token_spec, left_spec],
+        ),
+        out_shape=[
+            jax.ShapeDtypeStruct((rows, width), bf16),
+            jax.ShapeDtypeStruct((width, rank), bf16),
+        ],
         compiler_params=params(),
-        cost_estimate=cost(INPUT_HINT, 2 * rows * width * rank, 20 * rows * width),
+        cost_estimate=cost(INPUT_HINT, 6 * rows * width * rank, 20 * rows * width),
         name="input_grads",
-    )(idx, *local, *[c for pair in terms for c in pair], left, latent[0])
-
-
-def left_body(idx_ref, tokens_ref, far_tokens_ref, latent_ref, far_latent_ref, left_ref):
-    order = [k ^ idx_ref[0] for k in range(latent_ref.shape[0])]
-    latent = jnp.concatenate([latent_ref[k] for k in order], axis=0)
-    far_latent = jnp.concatenate([far_latent_ref[k] for k in order], axis=0)
-    tokens = in_dp_order(idx_ref, tokens_ref[...], far_tokens_ref[...])
-    latents = in_dp_order(idx_ref, latent, far_latent)
-    left = lax.dot_general(tokens, latents, TN, preferred_element_type=f32)
-    left_ref[...] = left.astype(bf16)
-
-
-def left_grads(idx, tokens, far_tokens, latent, far_latent, block):
-    rows, width = tokens.shape
-    rank = latent[0].shape[3]
-    token_spec = pl.BlockSpec((rows, block), lambda g, idx: (0, g))
-    return pl.pallas_call(
-        left_body,
-        grid_spec=pltpu.PrefetchScalarGridSpec(
-            num_scalar_prefetch=1,
-            grid=(width // block,),
-            in_specs=[token_spec, token_spec, latent_spec(latent), latent_spec(far_latent)],
-            out_specs=pl.BlockSpec((block, rank), lambda g, idx: (g, 0)),
-        ),
-        out_shape=jax.ShapeDtypeStruct((width, rank), bf16),
-        compiler_params=params(),
-        cost_estimate=cost(LEFT_HINT, 4 * rows * width * rank, 4 * rows * width),
-        name="left_grads",
-    )(idx, tokens, far_tokens, latent[0], far_latent[0])
+    )(
+        idx,
+        *local,
+        *[c for pair in terms for c in pair],
+        left,
+        latent[0],
+        far_latent[0],
+        tokens,
+        far_tokens,
+    )
 
 
 def after(value, *first):
@@ -451,13 +424,16 @@
         second = over_high(after(tokens[cut:half_rows], quarter_sum))
         far = from_partner(quarter_sum, "dp", 0)
         far_half = column_halves(mine, [far_tokens], block)
-        return gathered(quarter_sum), far, far_tokens, far_half, near_y, second
+        rest = after(tokens, quarter_sum)[half_rows:]
+        return gathered(quarter_sum), far, far_tokens, far_half, near_y, second, rest
 
     low_sum, core = one_step(low_part, tokens, left_factor)
     low_sum, first = after((low_sum, first))
-    latent, far_quarter, far_tokens, far_half, near_y, second = one_step(high_part, low_sum, tokens)
-    third = over_high(after(tokens[half_rows:], latent))
-    far_y = from_partner(after(tokens[half_rows:], latent), "mp", 1)
+    latent, far_quarter, far_tokens, far_half, near_y, second, rest = one_step(
+        high_part, low_sum, tokens
+    )
+    third = over_high(rest)
+    far_y = from_partner(rest, "mp", 1)
     received = [
         [[(core, 0, half_rows)], [(near_y, 0, half_rows)]]
         + [[(p, 0, cut), (q, 0, half_rows - cut)] for p, q in zip(first, second)],
@@ -488,17 +464,12 @@
     def high_grad(part, *terms):
         return high_sum(part), [from_partner(t, "mp", bit) for bit, t in enumerate(terms)]
 
-    def gather_grad(quarter_sum, far_quarter, core_term, y_term, far_half, tokens, remote, grads):
-        remote = with_places(remote, near_places)
-        near = near_weight_grads(idx, tokens, remote, grads, taps, block)
-        stack = jnp.concatenate([quarter_sum, far_quarter], axis=1)
-        other = from_partner(stack, "mp", 1)
+    def gather_grad(stack, core_term, far_half):
         core_term = from_partner(core_term, "mp", 0)
         far_core = from_partner(after(far_half, core_term), "mp", 0)
-        y_term = from_partner(after(y_term, other, far_core), "mp", 1)
-        stack = jnp.concatenate([stack, other], axis=0)
+        stack = jnp.concatenate([stack, from_partner(stack, "mp", 1)], axis=0)
         stack = jnp.concatenate([stack, from_partner(after(stack, far_core), "mp", 0)], axis=0)
-        return stack, core_term, y_term, far_core, near
+        return stack, core_term, far_core
 
     low_sum = one_step(low_grad, near_latent, far_latent_term)
     low_sum, near_terms, far_near_grad, far_y_half = after(
@@ -507,46 +478,47 @@
     quarter_sum, low_terms = one_step(high_grad, low_sum, *near_out[:2])
     near_terms = low_terms + near_terms
     far_terms = over_high_terms(far_out, quarter_sum)
+    gathered_both, core_term, far_core = one_step(
+        gather_grad, stacked(quarter_sum, far_quarter), far_out[0], far_half
+    )
+
+    def last_part(gathered_both, y_term, tokens, remote, far_tokens, far_remote, grads, latent):
+        far_latent_grad = from_partner(gathered_both[:, :1], "dp", 0)
+        y_term = from_partner(y_term, "mp", 1)
+        weights = weight_grads(
+            idx,
+            tokens,
+            with_places(remote, near_places),
+            far_tokens,
+            with_places(far_remote, far_places),
+            grads,
+            (latent, 0),
+            (gathered_both, 1),
+            taps,
+            block,
+        )
+        return far_latent_grad, y_term, *weights
+
     remote = [a + b for a, b in zip(*received)]
-    near_places = [[p[1:] for p in tap] for tap in remote]
-    gathered_both, core_term, y_term, far_core, near = one_step(
-        gather_grad,
-        quarter_sum,
-        far_quarter,
-        *far_out[:2],
-        far_half,
-        tokens,
-        [[p[0] for p in tap] for tap in remote],
-        grads[:2],
-    )
-    far_terms = [core_term, y_term] + far_terms
-
     far_remote = [[(c, 0, rows)] for c in (far_core, far_y_half)]
     far_remote += [[(far_halves, k, half_rows)] for k in range(len(high_bits))]
-
-    def last_part(gathered_both, far_tokens, near, grads, latent, far_remote):
-        far_latent_grad = from_partner(gathered_both[:, :1], "dp", 0)
-        far_remote = with_places(far_remote, far_places)
-        weights = weight_grads(
-            idx, near, far_tokens, far_remote, grads, (latent, 0), (gathered_both, 1), taps, block
-        )
-        return far_latent_grad, *weights
-
-    far_places = [[p[1:] for p in tap] for tap in far_remote]
-    input_grad = input_grads(
-        idx, local, list(zip(near_terms, far_terms)), left_factor, (gathered_both, 0), block
-    )
-    gathered_both, input_grad = after((gathered_both, input_grad))
-    far_latent_grad, weight_grad, right_grad = one_step(
-        last_part,
-        gathered_both,
+    near_places, far_places = [[[p[1:] for p in tap] for tap in r] for r in (remote, far_remote)]
+    remote, far_remote = [[[p[0] for p in tap] for tap in r] for r in (remote, far_remote)]
+    far_latent_grad, y_term, weight_grad, right_grad = one_step(
+        last_part, gathered_both, far_out[1], tokens, remote, far_tokens, far_remote, grads, latent
+    )
+    far_terms = [core_term, y_term] + far_terms
+    input_grad, left_grad = input_grads(
+        idx,
+        local,
+        list(zip(near_terms, far_terms)),
+        left_factor,
+        (gathered_both, 0),
+        (far_latent_grad, 0),
+        tokens,
         far_tokens,
-        near,
-        grads,
-        latent,
-        [[p[0] for p in tap] for tap in far_remote],
-    )
-    left_grad = left_grads(idx, tokens, far_tokens, (gathered_both, 0), (far_latent_grad, 0), block)
+        block,
+    )
     return act, input_grad, weight_grad, left_grad, right_grad
 
 

time: 162 us -> 153 us (0.944)
  Pallas kernels: 54.8 us -> 44.8 us
  starting transfers between devices: 35.5 us -> 42.6 us
  local copies, waits for them, and re-layouts: 7.27 us -> 3.9 us
  waiting for transfers between devices: 59.7 us -> 57.7 us
    pallas_call x3 -> x2, Pallas kernels: 21.6 us -> 10.8 us  [the longest x1 9.98 us: weight_grads(): pl.pallas_call(functools.partial(weights_body, local_taps, [len(t) for t...]
    ppermute x37, starting transfers between devices: 35.5 us -> 42.6 us  [from_partner(): lax.ppermute(shard, axis, [(i, i ^ 1 << distance) for i in range(lax.axis...]
    ppermute x37, waiting for transfers between devices: 59.7 us -> 57.7 us  [from_partner(): lax.ppermute(shard, axis, [(i, i ^ 1 << distance) for i in range(lax.axis...]
  transfers between devices with their start and end apart: 37 -> 37, of which waited for: 20 -> 24; matrix products, arithmetic and copies ran while one was open for 5% -> 3% of each run, Pallas kernels for 31% -> 25%
where the time goes in v3:
time: 153 us; the launch traced here: 152 us
  waiting for transfers between devices  57.7 us (38%)
  Pallas kernels  44.8 us (29%)
  starting transfers between devices  42.6 us (28%)
  local copies, waits for them, and re-layouts  3.9 us (3%)
  matrix products  1.88 us (1%)
    ppermute x37, waiting for transfers between devices, from_partner(): lax.ppermute(shard, axis, [(i, i ^ 1 << distance) for i in range(lax.axis...  57.7 us
    ppermute x37, starting transfers between devices, from_partner(): lax.ppermute(shard, axis, [(i, i ^ 1 << distance) for i in range(lax.axis...  42.6 us
    pallas_call x2, Pallas kernels, forward_chunk(): pl.pallas_call(functools.partial(forward_body, local_taps, [len(t) for t...  24 us
    pallas_call x1, Pallas kernels, weight_grads(): pl.pallas_call(functools.partial(weights_body, local_taps, [len(t) for t...  9.98 us
    pallas_call x1, Pallas kernels, input_grads(): pl.pallas_call(functools.partial(inputs_body, len(terms)), grid_spec=pltp...  6.16 us
    pallas_call x2, Pallas kernels, column_halves(): pl.pallas_call(halves_body, grid_spec=pltpu.PrefetchScalarGridSpec(num_sc...  3.82 us
  transfers between devices with their start and end apart: 37, of which 24 were waited for; matrix products, arithmetic and copies ran while one was open for 3% of the time, Pallas kernels for 25%

profile of v3, /device:TPU:0, one launch (start us, length us, event | category | flops | bytes accessed | tf_op | source)
XLA Modules:
  0.0 152.4 jit_solution(13997916470842128916)
XLA Ops:
  1.6 4.1 %collective-permute-start.25 = (bf16[128,1024]{1,0:T(8,128)(2,1)S(1)}, bf16[128,1024]{1,0:T(8,128)(2,1)S(1)}, u32[]{:S(2)}, u32[]{:S(2)}) collective-permute-start(bf16[128,1024]{1,0:T(8,128)(2,1)S(1)} %slice.15), channel_id=1, source_target_pairs={{0,8},{1,9},{2,10},{3,11},{4,12},{5,13},{6,14},{7,15},{8,0},{9,1},... | collective-permute-start | bytes 786440 | tf_op jit(solution)/shard_map/ppermute | solution.py:23
  5.7 1.6 %collective-permute-start.24 = (bf16[128,1024]{1,0:T(8,128)(2,1)S(1)}, bf16[128,1024]{1,0:T(8,128)(2,1)S(1)}, u32[]{:S(2)}, u32[]{:S(2)}) collective-permute-start(bf16[128,1024]{1,0:T(8,128)(2,1)S(1)} %slice.15), channel_id=1, source_target_pairs={{0,4},{1,5},{2,6},{3,7},{4,0},{5,1},{6,2},{7,3},{8,12},{9,13},{10,... | collective-permute-start | bytes 786440 | tf_op jit(solution)/shard_map/ppermute | solution.py:23
  7.3 9.7 %conditional.6 = (f32[128,256]{1,0:T(8,128)S(1)}, bf16[512,1024]{1,0:T(8,128)(2,1)}) conditional(s32[]{:T(128)} %convert_element_type.8, () %tuple.68, (bf16[512,1024]{1,0:T(8,128)(2,1)}, bf16[1024,256]{1,0:T(8,128)(2,1)}) %tuple.69), branch_computations={%region_0.0_spmd, %region_1.2_spmd} | conditional | flops 268730368 | bytes 14811390 | solution.py:366
  7.3 1.9 %fusion.2 = f32[512,256]{1,0:T(8,128)S(1)} fusion(bf16[512,1024]{1,0:T(8,128)(2,1)} %get-tuple-element.75, bf16[1024,256]{1,0:T(8,128)(2,1)} %get-tuple-element.74), kind=kOutput, calls=%fused_computation.17 | convolution fusion | flops 268435456 | bytes 2097152 | tf_op jit(solution)/shard_map/cond/branch_1_fun/dot_general | solution.py:415
  9.3 1.5 collective-permute-done.21
  11.1 1.6 %collective-permute-start.22 = (f32[128,256]{1,0:T(8,128)S(1)}, f32[128,256]{1,0:T(8,128)S(1)}, u32[]{:S(2)}, u32[]{:S(2)}) collective-permute-start(f32[128,256]{1,0:T(8,128)S(1)} %slice_select_fusion.1), channel_id=1, source_target_pairs={{0,2},{1,3},{2,0},{3,1},{4,6},{5,7},{6,4},{7,5},{8,10},{9,11},{10,... | collective-permute-start | bytes 393224 | tf_op jit(solution)/shard_map/cond/branch_1_fun/ppermute | solution.py:23
  12.7 4.2 %collective-permute-done.22 = f32[128,256]{1,0:T(8,128)S(1)} collective-permute-done((f32[128,256]{1,0:T(8,128)S(1)}, f32[128,256]{1,0:T(8,128)S(1)}, u32[]{:S(2)}, u32[]{:S(2)}) %collective-permute-start.22) | collective-permute-done | bytes 131104 | tf_op jit(solution)/shard_map/cond/branch_1_fun/ppermute | solution.py:23
  17.9 31.1 %conditional.7 = (bf16[4,1,128,256]{3,2,1,0:T(8,128)(2,1)S(1)}, bf16[1,1,128,256]{3,2,1,0:T(8,128)(2,1)}, bf16[512,1024]{1,0:T(8,128)(2,1)}, bf16[512,512]{1,0:T...) conditional(s32[]{:T(128)} %convert_element_type.8, () %tuple.70, ...), branch_computations={%region_2.3_spmd, %region_3.4_spmd} | conditional | flops 425984 | bytes 18874820 | solution.py:366
  17.9 1.5 %collective-permute-start.7 = (bf16[512,1024]{1,0:T(8,128)(2,1)}, bf16[512,1024]{1,0:T(8,128)(2,1)}, u32[]{:S(2)}, u32[]{:S(2)}) collective-permute-start(bf16[512,1024]{1,0:T(8,128)(2,1)} %get-tuple-element.80), channel_id=1, source_target_pairs={{0,16},{16,0},{1,17},{17,1},{2,18},{18,2},{3,19},{19,3},{4,20},{20... | collective-permute-start | bytes 3145736 | tf_op jit(solution)/shard_map/cond/branch_1_fun/ppermute | solution.py:23
  19.5 1.4 collective-permute-start.2
  20.9 3.5 %collective-permute-done.2 = f32[128,256]{1,0:T(8,128)S(1)} collective-permute-done((f32[128,256]{1,0:T(8,128)S(1)}, f32[128,256]{1,0:T(8,128)S(1)}, u32[]{:S(2)}, u32[]{:S(2)}) %collective-permute-start.2) | collective-permute-done | bytes 131104 | tf_op jit(solution)/shard_map/cond/branch_1_fun/ppermute | solution.py:23
  24.5 2.3 %collective-permute-start.3 = (f32[128,256]{1,0:T(8,128)S(1)}, f32[128,256]{1,0:T(8,128)S(1)}, u32[]{:S(2)}, u32[]{:S(2)}) collective-permute-start(f32[128,256]{1,0:T(8,128)S(1)} %add.20), channel_id=1, source_target_pairs={{0,8},{1,9},{2,10},{3,11},{4,12},{5,13},{6,14},{7,15},{8,0},{9,1},... | collective-permute-start | bytes 393224 | tf_op jit(solution)/shard_map/cond/branch_1_fun/ppermute | solution.py:23
  27.9 1.6 %collective-permute-start.8 = (bf16[256,1024]{1,0:T(8,128)(2,1)S(1)}, bf16[256,1024]{1,0:T(8,128)(2,1)}, u32[]{:S(2)}, u32[]{:S(2)}) collective-permute-start(bf16[256,1024]{1,0:T(8,128)(2,1)S(1)} %slice.10), channel_id=1, source_target_pairs={{0,2},{1,3},{2,0},{3,1},{4,6},{5,7},{6,4},{7,5},{8,10},{9,11},{10,... | collective-permute-start | bytes 1572872 | tf_op jit(solution)/shard_map/cond/branch_1_fun/ppermute | solution.py:23
  29.5 3.1 %collective-permute-done.3 = f32[128,256]{1,0:T(8,128)S(1)} collective-permute-done((f32[128,256]{1,0:T(8,128)S(1)}, f32[128,256]{1,0:T(8,128)S(1)}, u32[]{:S(2)}, u32[]{:S(2)}) %collective-permute-start.3) | collective-permute-done | bytes 131104 | tf_op jit(solution)/shard_map/cond/branch_1_fun/ppermute | solution.py:23
  32.6 1.6 %collective-permute-start.4 = (bf16[1,1,128,256]{3,2,1,0:T(8,128)(2,1)S(1)}, bf16[1,1,128,256]{3,2,1,0:T(8,128)(2,1)S(1)}, u32[]{:S(2)}, u32[]{:S(2)}) collective-permute-start(bf16[1,1,128,256]{3,2,1,0:T(8,128)(2,1)S(1)} %fusion), channel_id=1, source_target_pairs={{0,2},{1,3},{2,0},{3,1},{4,6},{5,7},{6,4},{7,5},{8,10},{9,11},{10,... | collective-permute-start | bytes 196616 | tf_op jit(solution)/shard_map/cond/branch_1_fun/ppermute | solution.py:23
  35.3 3.9 %collective-permute-start.9 = (bf16[128,1024]{1,0:T(8,128)(2,1)S(1)}, bf16[128,1024]{1,0:T(8,128)(2,1)}, u32[]{:S(2)}, u32[]{:S(2)}) collective-permute-start(bf16[128,1024]{1,0:T(8,128)(2,1)S(1)} %slice.11), channel_id=1, source_target_pairs={{0,4},{1,5},{2,6},{3,7},{4,0},{5,1},{6,2},{7,3},{8,12},{9,13},{10,... | collective-permute-start | bytes 786440 | tf_op jit(solution)/shard_map/cond/branch_1_fun/ppermute | solution.py:23
  39.2 2.9 %collective-permute-done.4 = bf16[1,1,128,256]{3,2,1,0:T(8,128)(2,1)S(1)} collective-permute-done((bf16[1,1,128,256]{3,2,1,0:T(8,128)(2,1)S(1)}, bf16[1,1,128,256]{3,2,1,0:T(8,128)(2,1)S(1)}, u32[]{:S(2)}, u32[]{:S(2)}) %collective-permute-start.4) | collective-permute-done | bytes 65568 | tf_op jit(solution)/shard_map/cond/branch_1_fun/ppermute | solution.py:23
  44.2 2.0 %column_halves.2 = bf16[512,512]{1,0:T(8,128)(2,1)S(1)} custom-call(s32[1]{0:T(128)} %get-tuple-element.78.idx_ref, bf16[512,1024]{1,0:T(8,128)(2,1)} %collective-permute-done.7.refs_0_), custom_call_target="tpu_custom_call" | custom-call | bytes 65536 | tf_op jit(solution)/shard_map/cond/branch_1_fun/column_halves/pallas_call | solution.py:177
  46.2 1.8 %collective-permute-done.6 = bf16[1,1,128,256]{3,2,1,0:T(8,128)(2,1)} collective-permute-done((bf16[1,1,128,256]{3,2,1,0:T(8,128)(2,1)S(1)}, bf16[1,1,128,256]{3,2,1,0:T(8,128)(2,1)}, u32[]{:S(2)}, u32[]{:S(2)}) %collective-permute-start.6) | collective-permute-done | bytes 65568 | tf_op jit(solution)/shard_map/cond/branch_1_fun/ppermute | solution.py:23
  49.0 2.0 %collective-permute-start.28 = (bf16[256,1024]{1,0:T(8,128)(2,1)}, bf16[256,1024]{1,0:T(8,128)(2,1)S(1)}, u32[]{:S(2)}, u32[]{:S(2)}) collective-permute-start(bf16[256,1024]{1,0:T(8,128)(2,1)} %get-tuple-element.175), channel_id=1, source_target_pairs={{0,8},{1,9},{2,10},{3,11},{4,12},{5,13},{6,14},{7,15},{8,0},{9,1},... | collective-permute-start | bytes 1572872 | tf_op jit(solution)/shard_map/ppermute | solution.py:23
  51.0 1.8 %collective-permute-start.27 = (bf16[256,1024]{1,0:T(8,128)(2,1)}, bf16[256,1024]{1,0:T(8,128)(2,1)S(1)}, u32[]{:S(2)}, u32[]{:S(2)}) collective-permute-start(bf16[256,1024]{1,0:T(8,128)(2,1)} %get-tuple-element.175), channel_id=1, source_target_pairs={{0,4},{1,5},{2,6},{3,7},{4,0},{5,1},{6,2},{7,3},{8,12},{9,13},{10,... | collective-permute-start | bytes 1572872 | tf_op jit(solution)/shard_map/ppermute | solution.py:23
  53.3 1.8 %column_halves.3 = bf16[512,512]{1,0:T(8,128)(2,1)S(1)} custom-call(s32[1]{0:T(128)S(6)} %sub.3.idx_ref, bf16[128,1024]{1,0:T(8,128)(2,1)S(1)} %collective-permute-done.24.refs_0_.refs_5_, bf16[128,1024]{1,0:T(8,128)(2,1)} %get-tuple-element.178.refs_1_.refs_6_, bf16[128,1024]{1,0:T(8,128)(2,1)S(1)} %collective-permute-done.25.refs_2_.refs_7_, ...), custom_call_target="tpu_custom_call" | custom-call | bytes 65536 | tf_op jit(solution)/shard_map/column_halves/pallas_call | solution.py:177
  55.7 12.1 %forward_chunk.2 = (bf16[512,2048]{1,0:T(8,128)(2,1)}, bf16[256,2048]{1,0:T(8,128)(2,1)}, bf16[256,1024]{1,0:T(8,128)(2,1)}, bf16[256,1024]{1,0:T(8,128)(2,1)}, ...) custom-call(s32[2]{0:T(128)S(1)} %pad_add_fusion.idx_ref, ...), custom_call_target="tpu_custom_call" | custom-call | flops 17179869184 | bytes 71303168 | tf_op jit(solution)/shard_map/forward_chunk/pallas_call | solution.py:145
  67.8 1.5 %collective-permute-start.32 = (bf16[256,2048]{1,0:T(8,128)(2,1)}, bf16[256,2048]{1,0:T(8,128)(2,1)}, u32[]{:S(2)}, u32[]{:S(2)}) collective-permute-start(bf16[256,2048]{1,0:T(8,128)(2,1)} %get-tuple-element.194), channel_id=1, source_target_pairs={{0,16},{16,0},{1,17},{17,1},{2,18},{18,2},{3,19},{19,3},{4,20},{20... | collective-permute-start | bytes 3145736 | tf_op jit(solution)/shard_map/ppermute | solution.py:23
  69.3 4.3 %collective-permute-done.28.refs_6_ = bf16[256,1024]{1,0:T(8,128)(2,1)S(1)} collective-permute-done((bf16[256,1024]{1,0:T(8,128)(2,1)}, bf16[256,1024]{1,0:T(8,128)(2,1)S(1)}, u32[]{:S(2)}, u32[]{:S(2)}) %collective-permute-start.28) | collective-permute-done | bytes 524320 | tf_op jit(solution)/shard_map/ppermute | solution.py:23
  74.0 1.1 collective-permute-start.33
  75.1 1.1 collective-permute-start.30
  76.2 1.9 %collective-permute-start.29 = (bf16[256,1024]{1,0:T(8,128)(2,1)}, bf16[256,1024]{1,0:T(8,128)(2,1)}, u32[]{:S(2)}, u32[]{:S(2)}) collective-permute-start(bf16[256,1024]{1,0:T(8,128)(2,1)} %get-tuple-element.190), channel_id=1, source_target_pairs={{0,4},{1,5},{2,6},{3,7},{4,0},{5,1},{6,2},{7,3},{8,12},{9,13},{10,... | collective-permute-start | bytes 1572872 | tf_op jit(solution)/shard_map/ppermute | solution.py:23
  78.2 11.9 %forward_chunk.3 = (bf16[512,2048]{1,0:T(8,128)(2,1)}, bf16[384,2048]{1,0:T(8,128)(2,1)}, bf16[256,1024]{1,0:T(8,128)(2,1)}, bf16[256,1024]{1,0:T(8,128)(2,1)}, ...) custom-call(s32[2]{0:T(128)S(1)} %pad_add_fusion.idx_ref, ...), custom_call_target="tpu_custom_call", output_to_operand_aliasing={{0}: (13, {})} | custom-call | flops 268435456 | bytes 1114112 | tf_op jit(solution)/shard_map/forward_chunk/pallas_call | solution.py:145
  90.1 7.4 %conditional.8 = (f32[128,256]{1,0:T(8,128)S(1)}) conditional(s32[]{:T(128)} %convert_element_type.8, () %tuple.75, (f32[256,256]{1,0:T(8,128)S(1)}, f32[256,256]{1,0:T(8,128)S(1)}) %tuple.109), branch_computations={%region_4.5_spmd, %region_5.6_spmd} | conditional | flops 294920 | bytes 4325554 | solution.py:366
  90.3 1.5 collective-permute-done.11
  91.9 1.6 %collective-permute-start.12 = (f32[128,256]{1,0:T(8,128)S(1)}, f32[128,256]{1,0:T(8,128)S(1)}, u32[]{:S(2)}, u32[]{:S(2)}) collective-permute-start(f32[128,256]{1,0:T(8,128)S(1)} %slice_select_fusion.2), channel_id=1, source_target_pairs={{0,2},{1,3},{2,0},{3,1},{4,6},{5,7},{6,4},{7,5},{8,10},{9,11},{10,... | collective-permute-start | bytes 393224 | tf_op jit(solution)/shard_map/cond/branch_1_fun/ppermute | solution.py:23
  93.5 4.0 %collective-permute-done.12 = f32[128,256]{1,0:T(8,128)S(1)} collective-permute-done((f32[128,256]{1,0:T(8,128)S(1)}, f32[128,256]{1,0:T(8,128)S(1)}, u32[]{:S(2)}, u32[]{:S(2)}) %collective-permute-start.12) | collective-permute-done | bytes 131104 | tf_op jit(solution)/shard_map/cond/branch_1_fun/ppermute | solution.py:23
  98.1 2.5 %collective-permute-done.30.refs_8_ = bf16[256,1024]{1,0:T(8,128)(2,1)} collective-permute-done((bf16[256,1024]{1,0:T(8,128)(2,1)}, bf16[256,1024]{1,0:T(8,128)(2,1)}, u32[]{:S(2)}, u32[]{:S(2)}) %collective-permute-start.30) | collective-permute-done | bytes 524320 | tf_op jit(solution)/shard_map/ppermute | solution.py:23
  100.7 14.7 %conditional.9 = (bf16[1,1,128,256]{3,2,1,0:T(8,128)(2,1)S(1)}, bf16[256,1024]{1,0:T(8,128)(2,1)}, bf16[256,1024]{1,0:T(8,128)(2,1)}) conditional(s32[]{:T(128)} %convert_element_type.8, () %tuple.74, (f32[128,256]{1,0:T(8,128)S(1)}, bf16[256,1024]{1,0:T(8,128)(2,1)}, bf16[256,1024]{1,0:T(8,128)(2,1)}) %tuple.82), branch_computations={%region_6.7_spmd, %region_7.8_spmd} | conditional | flops 98304 | bytes 5963960 | solution.py:366
  101.1 5.6 %collective-permute-done.13 = f32[128,256]{1,0:T(8,128)S(1)} collective-permute-done((f32[128,256]{1,0:T(8,128)S(1)}, f32[128,256]{1,0:T(8,128)S(1)}, u32[]{:S(2)}, u32[]{:S(2)}) %collective-permute-start.13) | collective-permute-done | bytes 131104 | tf_op jit(solution)/shard_map/cond/branch_1_fun/ppermute | solution.py:23
  106.7 2.1 %collective-permute-start.14 = (f32[128,256]{1,0:T(8,128)S(1)}, f32[128,256]{1,0:T(8,128)S(1)}, u32[]{:S(2)}, u32[]{:S(2)}) collective-permute-start(f32[128,256]{1,0:T(8,128)S(1)} %add.24), channel_id=1, source_target_pairs={{0,8},{1,9},{2,10},{3,11},{4,12},{5,13},{6,14},{7,15},{8,0},{9,1},... | collective-permute-start | bytes 393224 | tf_op jit(solution)/shard_map/cond/branch_1_fun/ppermute | solution.py:23
  108.8 6.5 %collective-permute-done.14 = f32[128,256]{1,0:T(8,128)S(1)} collective-permute-done((f32[128,256]{1,0:T(8,128)S(1)}, f32[128,256]{1,0:T(8,128)S(1)}, u32[]{:S(2)}, u32[]{:S(2)}) %collective-permute-start.14) | collective-permute-done | bytes 131104 | tf_op jit(solution)/shard_map/cond/branch_1_fun/ppermute | solution.py:23
  115.6 3.4 %collective-permute-start.36 = (bf16[256,1024]{1,0:T(8,128)(2,1)}, bf16[256,1024]{1,0:T(8,128)(2,1)}, u32[]{:S(2)}, u32[]{:S(2)}) collective-permute-start(bf16[256,1024]{1,0:T(8,128)(2,1)} %get-tuple-element.218), channel_id=1, source_target_pairs={{0,8},{1,9},{2,10},{3,11},{4,12},{5,13},{6,14},{7,15},{8,0},{9,1},... | collective-permute-start | bytes 1572872 | tf_op jit(solution)/shard_map/ppermute | solution.py:23
  119.9 9.9 %conditional.10 = (bf16[4,2,128,256]{3,2,1,0:T(8,128)(2,1)S(1)}, bf16[256,1024]{1,0:T(8,128)(2,1)}, bf16[512,512]{1,0:T(8,128)(2,1)}) conditional(s32[]{:T(128)} %convert_element_type.8, () %tuple.83, (bf16[1,2,128,256]{3,2,1,0:T(8,128)(2,1)S(1)}, bf16[256,1024]{1,0:T(8,128)(2,1)}, bf16[512,512]{1,0:T(8,128)(2,1)}) %tuple.110), branch_computations={%region_8.9_spmd, %region_9.10_spmd} | conditional | flops 655360 | bytes 7340216 | solution.py:366
  119.9 2.2 %collective-permute-done.18 = bf16[256,1024]{1,0:T(8,128)(2,1)} collective-permute-done((bf16[256,1024]{1,0:T(8,128)(2,1)}, bf16[256,1024]{1,0:T(8,128)(2,1)}, u32[]{:S(2)}, u32[]{:S(2)}) %collective-permute-start.18) | collective-permute-done | bytes 524320 | tf_op jit(solution)/shard_map/cond/branch_1_fun/ppermute | solution.py:23
  122.8 5.3 %collective-permute-done.17 = bf16[1,2,128,256]{3,2,1,0:T(8,128)(2,1)S(1)} collective-permute-done((bf16[1,2,128,256]{3,2,1,0:T(8,128)(2,1)S(1)}, bf16[1,2,128,256]{3,2,1,0:T(8,128)(2,1)S(1)}, u32[]{:S(2)}, u32[]{:S(2)}) %collective-permute-start.17) | collective-permute-done | bytes 131104 | tf_op jit(solution)/shard_map/cond/branch_1_fun/ppermute | solution.py:23
  128.2 1.5 collective-permute-done.20
  129.8 3.7 %collective-permute-done.34 = bf16[384,2048]{1,0:T(8,128)(2,1)S(1)} collective-permute-done((bf16[384,2048]{1,0:T(8,128)(2,1)}, bf16[384,2048]{1,0:T(8,128)(2,1)S(1)}, u32[]{:S(2)}, u32[]{:S(2)}) %collective-permute-start.34) | collective-permute-done | bytes 1572896 | tf_op jit(solution)/shard_map/ppermute | solution.py:23
  133.5 12.7 %conditional.11 = (bf16[4,1,128,256]{3,2,1,0:T(8,128)(2,1)}, bf16[256,1024]{1,0:T(8,128)(2,1)}, bf16[7,128,2048]{2,1,0:T(8,128)(2,1)}, bf16[256,2048]{1,0:T(8,128)(2,1)}) conditional(s32[]{:T(128)} %convert_element_type.8, () %tuple.85, (bf16[4,2,128,256]{3,2,1,0:T(8,128)(2,1)S(1)}, bf16[256,1024]{1,0:T(8,128)(2,1)}, s32[2]{0:T(128)S(1)}, ...), branch_computations={%region_10.11_spmd, %region_11.12_spmd} | conditional | flops 301989888 | bytes 5505064 | solution.py:366
  133.5 1.5 collective-permute-start.1
  135.7 10.0 %weight_grads.1 = (bf16[7,128,2048]{2,1,0:T(8,128)(2,1)}, bf16[256,2048]{1,0:T(8,128)(2,1)}) custom-call(s32[2]{0:T(128)S(1)} %get-tuple-element.93.idx_ref, bf16[512,1024]{1,0:T(8,128)(2,1)S(1)} %get-tuple-element.94.refs_0_.refs_1_.refs_2_, bf16[512,1024]{1,0:T(8,128)(2,1)S(1)} %get-tuple-element.94.refs_0_.refs_1_.refs_2_, ...), custom_call_target="tpu_custom_call" | custom-call | flops 301989888 | bytes 917504 | tf_op jit(solution)/shard_map/cond/branch_1_fun/weight_grads/pallas_call | solution.py:246
  146.3 6.2 %input_grads.1 = (bf16[512,1024]{1,0:T(8,128)(2,1)}, bf16[1024,256]{1,0:T(8,128)(2,1)}) custom-call(s32[2]{0:T(128)S(1)} %pad_add_fusion.idx_ref, f32[256,1024]{1,0:T(8,128)} %get-tuple-element.185.refs_0_, f32[256,1024]{1,0:T(8,128)} %get-tuple-element.186.refs_1_, bf16[256,1024]{1,0:T(8,128)(2,1)} %get-tuple-element.200.refs_2_, ...), custom_call_target="tpu_custom_call" | custom-call | flops 50331648 | bytes 655360 | tf_op jit(solution)/shard_map/input_grads/pallas_call | solution.py:331
  (84 shorter events, 13.6 us)
Async XLA Ops:
  1.6 16.1 %collective-permute-start.25 = (bf16[128,1024]{1,0:T(8,128)(2,1)S(1)}, bf16[128,1024]{1,0:T(8,128)(2,1)S(1)}, u32[]{:S(2)}, u32[]{:S(2)}) collective-permute-start(bf16[128,1024]{1,0:T(8,128)(2,1)S(1)} %slice.15), channel_id=1, source_target_pairs={{0,8},{1,9},{2,10},{3,11},{4,12},{5,13},{6,14},{7,15},{8,0},{9,1},... | collective-permute-start | bytes 786440 | tf_op jit(solution)/shard_map/ppermute | solution.py:23
  5.7 12.2 %collective-permute-start.24 = (bf16[128,1024]{1,0:T(8,128)(2,1)S(1)}, bf16[128,1024]{1,0:T(8,128)(2,1)S(1)}, u32[]{:S(2)}, u32[]{:S(2)}) collective-permute-start(bf16[128,1024]{1,0:T(8,128)(2,1)S(1)} %slice.15), channel_id=1, source_target_pairs={{0,4},{1,5},{2,6},{3,7},{4,0},{5,1},{6,2},{7,3},{8,12},{9,13},{10,... | collective-permute-start | bytes 786440 | tf_op jit(solution)/shard_map/ppermute | solution.py:23
  7.3 3.6 %copy-start.1 = (bf16[512,1024]{1,0:T(8,128)(2,1)S(1)}, bf16[512,1024]{1,0:T(8,128)(2,1)}, u32[]{:S(2)}) copy-start(bf16[512,1024]{1,0:T(8,128)(2,1)} %get-tuple-element.75) | copy-start | bytes 3145732 | tf_op jit(solution)/shard_map/cond
  9.2 1.6 %collective-permute-start.21 = (f32[256,256]{1,0:T(8,128)S(1)}, f32[256,256]{1,0:T(8,128)S(1)}, u32[]{:S(2)}, u32[]{:S(2)}) collective-permute-start(f32[256,256]{1,0:T(8,128)S(1)} %slice_select_fusion), channel_id=1, source_target_pairs={{0,1},{1,0},{2,3},{3,2},{4,5},{5,4},{6,7},{7,6},{8,9},{9,8},{10,11... | collective-permute-start | bytes 786440 | tf_op jit(solution)/shard_map/cond/branch_1_fun/ppermute | solution.py:23
  10.9 6.1 %collective-permute-start.23 = (bf16[512,1024]{1,0:T(8,128)(2,1)S(1)}, bf16[512,1024]{1,0:T(8,128)(2,1)}, u32[]{:S(2)}, u32[]{:S(2)}) collective-permute-start(bf16[512,1024]{1,0:T(8,128)(2,1)S(1)} %copy-done.1), channel_id=1, source_target_pairs={{0,1},{1,0},{2,3},{3,2},{4,5},{5,4},{6,7},{7,6},{8,9},{9,8},{10,11... | collective-permute-start | bytes 3145736 | tf_op jit(solution)/shard_map/cond/branch_1_fun/ppermute | solution.py:23
  11.1 5.8 %collective-permute-start.22 = (f32[128,256]{1,0:T(8,128)S(1)}, f32[128,256]{1,0:T(8,128)S(1)}, u32[]{:S(2)}, u32[]{:S(2)}) collective-permute-start(f32[128,256]{1,0:T(8,128)S(1)} %slice_select_fusion.1), channel_id=1, source_target_pairs={{0,2},{1,3},{2,0},{3,1},{4,6},{5,7},{6,4},{7,5},{8,10},{9,11},{10,... | collective-permute-start | bytes 393224 | tf_op jit(solution)/shard_map/cond/branch_1_fun/ppermute | solution.py:23
  17.7 35.5 %copy-start.7 = (bf16[128,1024]{1,0:T(8,128)(2,1)}, bf16[128,1024]{1,0:T(8,128)(2,1)S(1)}, u32[]{:S(2)}) copy-start(bf16[128,1024]{1,0:T(8,128)(2,1)S(1)} %collective-permute-done.25.refs_2_.refs_7_) | copy-start | bytes 786436
  17.9 35.3 %copy-start.8 = (bf16[128,1024]{1,0:T(8,128)(2,1)}, bf16[128,1024]{1,0:T(8,128)(2,1)S(1)}, u32[]{:S(2)}) copy-start(bf16[128,1024]{1,0:T(8,128)(2,1)S(1)} %collective-permute-done.24.refs_0_.refs_5_) | copy-start | bytes 786436
  17.9 24.3 %copy-start.2 = (bf16[512,1024]{1,0:T(8,128)(2,1)S(1)}, bf16[512,1024]{1,0:T(8,128)(2,1)}, u32[]{:S(2)}) copy-start(bf16[512,1024]{1,0:T(8,128)(2,1)} %get-tuple-element.80) | copy-start | bytes 3145732 | tf_op jit(solution)/shard_map/cond
  17.9 26.2 %collective-permute-start.7 = (bf16[512,1024]{1,0:T(8,128)(2,1)}, bf16[512,1024]{1,0:T(8,128)(2,1)}, u32[]{:S(2)}, u32[]{:S(2)}) collective-permute-start(bf16[512,1024]{1,0:T(8,128)(2,1)} %get-tuple-element.80), channel_id=1, source_target_pairs={{0,16},{16,0},{1,17},{17,1},{2,18},{18,2},{3,19},{19,3},{4,20},{20... | collective-permute-start | bytes 3145736 | tf_op jit(solution)/shard_map/cond/branch_1_fun/ppermute | solution.py:23
  19.5 5.0 %collective-permute-start.2 = (f32[128,256]{1,0:T(8,128)S(1)}, f32[128,256]{1,0:T(8,128)S(1)}, u32[]{:S(2)}, u32[]{:S(2)}) collective-permute-start(f32[128,256]{1,0:T(8,128)S(1)} %get-tuple-element.76), channel_id=1, source_target_pairs={{0,4},{1,5},{2,6},{3,7},{4,0},{5,1},{6,2},{7,3},{8,12},{9,13},{10,... | collective-permute-start | bytes 393224 | tf_op jit(solution)/shard_map/cond/branch_1_fun/ppermute | solution.py:23
  24.5 8.1 %collective-permute-start.3 = (f32[128,256]{1,0:T(8,128)S(1)}, f32[128,256]{1,0:T(8,128)S(1)}, u32[]{:S(2)}, u32[]{:S(2)}) collective-permute-start(f32[128,256]{1,0:T(8,128)S(1)} %add.20), channel_id=1, source_target_pairs={{0,8},{1,9},{2,10},{3,11},{4,12},{5,13},{6,14},{7,15},{8,0},{9,1},... | collective-permute-start | bytes 393224 | tf_op jit(solution)/shard_map/cond/branch_1_fun/ppermute | solution.py:23
  27.9 21.1 %collective-permute-start.8 = (bf16[256,1024]{1,0:T(8,128)(2,1)S(1)}, bf16[256,1024]{1,0:T(8,128)(2,1)}, u32[]{:S(2)}, u32[]{:S(2)}) collective-permute-start(bf16[256,1024]{1,0:T(8,128)(2,1)S(1)} %slice.10), channel_id=1, source_target_pairs={{0,2},{1,3},{2,0},{3,1},{4,6},{5,7},{6,4},{7,5},{8,10},{9,11},{10,... | collective-permute-start | bytes 1572872 | tf_op jit(solution)/shard_map/cond/branch_1_fun/ppermute | solution.py:23
  32.6 9.6 %collective-permute-start.4 = (bf16[1,1,128,256]{3,2,1,0:T(8,128)(2,1)S(1)}, bf16[1,1,128,256]{3,2,1,0:T(8,128)(2,1)S(1)}, u32[]{:S(2)}, u32[]{:S(2)}) collective-permute-start(bf16[1,1,128,256]{3,2,1,0:T(8,128)(2,1)S(1)} %fusion), channel_id=1, source_target_pairs={{0,2},{1,3},{2,0},{3,1},{4,6},{5,7},{6,4},{7,5},{8,10},{9,11},{10,... | collective-permute-start | bytes 196616 | tf_op jit(solution)/shard_map/cond/branch_1_fun/ppermute | solution.py:23
  35.1 13.8 %collective-permute-start.10 = (bf16[128,1024]{1,0:T(8,128)(2,1)S(1)}, bf16[128,1024]{1,0:T(8,128)(2,1)}, u32[]{:S(2)}, u32[]{:S(2)}) collective-permute-start(bf16[128,1024]{1,0:T(8,128)(2,1)S(1)} %slice.11), channel_id=1, source_target_pairs={{0,8},{1,9},{2,10},{3,11},{4,12},{5,13},{6,14},{7,15},{8,0},{9,1},... | collective-permute-start | bytes 786440 | tf_op jit(solution)/shard_map/cond/branch_1_fun/ppermute | solution.py:23
  35.3 13.7 %collective-permute-start.9 = (bf16[128,1024]{1,0:T(8,128)(2,1)S(1)}, bf16[128,1024]{1,0:T(8,128)(2,1)}, u32[]{:S(2)}, u32[]{:S(2)}) collective-permute-start(bf16[128,1024]{1,0:T(8,128)(2,1)S(1)} %slice.11), channel_id=1, source_target_pairs={{0,4},{1,5},{2,6},{3,7},{4,0},{5,1},{6,2},{7,3},{8,12},{9,13},{10,... | collective-permute-start | bytes 786440 | tf_op jit(solution)/shard_map/cond/branch_1_fun/ppermute | solution.py:23
  42.2 1.4 collective-permute-start.5
  43.6 4.4 %collective-permute-start.6 = (bf16[1,1,128,256]{3,2,1,0:T(8,128)(2,1)S(1)}, bf16[1,1,128,256]{3,2,1,0:T(8,128)(2,1)}, u32[]{:S(2)}, u32[]{:S(2)}) collective-permute-start(bf16[1,1,128,256]{3,2,1,0:T(8,128)(2,1)S(1)} %fusion), channel_id=1, source_target_pairs={{0,16},{16,0},{1,17},{17,1},{2,18},{18,2},{3,19},{19,3},{4,20},{20... | collective-permute-start | bytes 196616 | tf_op jit(solution)/shard_map/cond/branch_1_fun/ppermute | solution.py:23
  49.0 6.7 %copy-start.10 = (bf16[512,512]{1,0:T(8,128)(2,1)}, bf16[512,512]{1,0:T(8,128)(2,1)S(1)}, u32[]{:S(2)}) copy-start(bf16[512,512]{1,0:T(8,128)(2,1)S(1)} %get-tuple-element.196) | copy-start | bytes 1572868
  49.0 24.6 %collective-permute-start.28 = (bf16[256,1024]{1,0:T(8,128)(2,1)}, bf16[256,1024]{1,0:T(8,128)(2,1)S(1)}, u32[]{:S(2)}, u32[]{:S(2)}) collective-permute-start(bf16[256,1024]{1,0:T(8,128)(2,1)} %get-tuple-element.175), channel_id=1, source_target_pairs={{0,8},{1,9},{2,10},{3,11},{4,12},{5,13},{6,14},{7,15},{8,0},{9,1},... | collective-permute-start | bytes 1572872 | tf_op jit(solution)/shard_map/ppermute | solution.py:23
  51.0 23.0 %collective-permute-start.27 = (bf16[256,1024]{1,0:T(8,128)(2,1)}, bf16[256,1024]{1,0:T(8,128)(2,1)S(1)}, u32[]{:S(2)}, u32[]{:S(2)}) collective-permute-start(bf16[256,1024]{1,0:T(8,128)(2,1)} %get-tuple-element.175), channel_id=1, source_target_pairs={{0,4},{1,5},{2,6},{3,7},{4,0},{5,1},{6,2},{7,3},{8,12},{9,13},{10,... | collective-permute-start | bytes 1572872 | tf_op jit(solution)/shard_map/ppermute | solution.py:23
  52.8 16.6 %collective-permute-start.26 = (bf16[256,1024]{1,0:T(8,128)(2,1)}, bf16[256,1024]{1,0:T(8,128)(2,1)S(1)}, u32[]{:S(2)}, u32[]{:S(2)}) collective-permute-start(bf16[256,1024]{1,0:T(8,128)(2,1)} %get-tuple-element.175), channel_id=1, source_target_pairs={{0,2},{1,3},{2,0},{3,1},{4,6},{5,7},{6,4},{7,5},{8,10},{9,11},{10,... | collective-permute-start | bytes 1572872 | tf_op jit(solution)/shard_map/ppermute | solution.py:23
  55.1 12.7 %collective-permute-start.31 = (bf16[512,512]{1,0:T(8,128)(2,1)S(1)}, bf16[512,512]{1,0:T(8,128)(2,1)S(1)}, u32[]{:S(2)}, u32[]{:S(2)}) collective-permute-start(bf16[512,512]{1,0:T(8,128)(2,1)S(1)} %column_halves.3), channel_id=1, source_target_pairs={{0,16},{16,0},{1,17},{17,1},{2,18},{18,2},{3,19},{19,3},{4,20},{20... | collective-permute-start | bytes 1572872 | tf_op jit(solution)/shard_map/ppermute | solution.py:23
  55.7 22.5 %copy-start = (bf16[512,1024]{1,0:T(8,128)(2,1)S(1)}, bf16[512,1024]{1,0:T(8,128)(2,1)}, u32[]{:S(2)}) copy-start(bf16[512,1024]{1,0:T(8,128)(2,1)} %refs_13_.3) | copy-start | bytes 3145732
  67.8 22.3 %copy-start.6 = (bf16[512,512]{1,0:T(8,128)(2,1)}, bf16[512,512]{1,0:T(8,128)(2,1)S(1)}, u32[]{:S(2)}) copy-start(bf16[512,512]{1,0:T(8,128)(2,1)S(1)} %collective-permute-done.31) | copy-start | bytes 1572868
  67.8 32.9 %collective-permute-start.32 = (bf16[256,2048]{1,0:T(8,128)(2,1)}, bf16[256,2048]{1,0:T(8,128)(2,1)}, u32[]{:S(2)}, u32[]{:S(2)}) collective-permute-start(bf16[256,2048]{1,0:T(8,128)(2,1)} %get-tuple-element.194), channel_id=1, source_target_pairs={{0,16},{16,0},{1,17},{17,1},{2,18},{18,2},{3,19},{19,3},{4,20},{20... | collective-permute-start | bytes 3145736 | tf_op jit(solution)/shard_map/ppermute | solution.py:23
  69.3 20.8 %copy-start.5 = (bf16[256,1024]{1,0:T(8,128)(2,1)}, bf16[256,1024]{1,0:T(8,128)(2,1)S(1)}, u32[]{:S(2)}) copy-start(bf16[256,1024]{1,0:T(8,128)(2,1)S(1)} %collective-permute-done.26.refs_4_) | copy-start | bytes 1572868
  73.6 16.5 %copy-start.3 = (bf16[256,1024]{1,0:T(8,128)(2,1)}, bf16[256,1024]{1,0:T(8,128)(2,1)S(1)}, u32[]{:S(2)}) copy-start(bf16[256,1024]{1,0:T(8,128)(2,1)S(1)} %collective-permute-done.28.refs_6_) | copy-start | bytes 1572868
  74.0 16.1 %copy-start.4 = (bf16[256,1024]{1,0:T(8,128)(2,1)}, bf16[256,1024]{1,0:T(8,128)(2,1)S(1)}, u32[]{:S(2)}) copy-start(bf16[256,1024]{1,0:T(8,128)(2,1)S(1)} %collective-permute-done.27.refs_5_) | copy-start | bytes 1572868
  74.0 24.1 %collective-permute-start.33 = (bf16[512,512]{1,0:T(8,128)(2,1)}, bf16[512,512]{1,0:T(8,128)(2,1)}, u32[]{:S(2)}, u32[]{:S(2)}) collective-permute-start(bf16[512,512]{1,0:T(8,128)(2,1)} %copy-done.10), channel_id=1, source_target_pairs={{0,2},{1,3},{2,0},{3,1},{4,6},{5,7},{6,4},{7,5},{8,10},{9,11},{10,... | collective-permute-start | bytes 1572872 | tf_op jit(solution)/shard_map/ppermute | solution.py:23
  75.1 25.5 %collective-permute-start.30 = (bf16[256,1024]{1,0:T(8,128)(2,1)}, bf16[256,1024]{1,0:T(8,128)(2,1)}, u32[]{:S(2)}, u32[]{:S(2)}) collective-permute-start(bf16[256,1024]{1,0:T(8,128)(2,1)} %get-tuple-element.192), channel_id=1, source_target_pairs={{0,8},{1,9},{2,10},{3,11},{4,12},{5,13},{6,14},{7,15},{8,0},{9,1},... | collective-permute-start | bytes 1572872 | tf_op jit(solution)/shard_map/ppermute | solution.py:23
  76.2 24.5 %collective-permute-start.29 = (bf16[256,1024]{1,0:T(8,128)(2,1)}, bf16[256,1024]{1,0:T(8,128)(2,1)}, u32[]{:S(2)}, u32[]{:S(2)}) collective-permute-start(bf16[256,1024]{1,0:T(8,128)(2,1)} %get-tuple-element.190), channel_id=1, source_target_pairs={{0,4},{1,5},{2,6},{3,7},{4,0},{5,1},{6,2},{7,3},{8,12},{9,13},{10,... | collective-permute-start | bytes 1572872 | tf_op jit(solution)/shard_map/ppermute | solution.py:23
  78.2 12.0 %copy-start.9 = (f32[256,256]{1,0:T(8,128)S(1)}, f32[256,256]{1,0:T(8,128)}, u32[]{:S(2)}) copy-start(f32[256,256]{1,0:T(8,128)} %get-tuple-element.187) | copy-start | bytes 786436
  90.2 1.6 %collective-permute-start.11 = (f32[256,256]{1,0:T(8,128)S(1)}, f32[256,256]{1,0:T(8,128)S(1)}, u32[]{:S(2)}, u32[]{:S(2)}) collective-permute-start(f32[256,256]{1,0:T(8,128)S(1)} %broadcast_select_fusion), channel_id=1, source_target_pairs={{0,1},{1,0},{2,3},{3,2},{4,5},{5,4},{6,7},{7,6},{8,9},{9,8},{10,11... | collective-permute-start | bytes 786440 | tf_op jit(solution)/shard_map/cond/branch_1_fun/ppermute | solution.py:23
  91.9 5.6 %collective-permute-start.12 = (f32[128,256]{1,0:T(8,128)S(1)}, f32[128,256]{1,0:T(8,128)S(1)}, u32[]{:S(2)}, u32[]{:S(2)}) collective-permute-start(f32[128,256]{1,0:T(8,128)S(1)} %slice_select_fusion.2), channel_id=1, source_target_pairs={{0,2},{1,3},{2,0},{3,1},{4,6},{5,7},{6,4},{7,5},{8,10},{9,11},{10,... | collective-permute-start | bytes 393224 | tf_op jit(solution)/shard_map/cond/branch_1_fun/ppermute | solution.py:23
  97.5 36.0 %collective-permute-start.34 = (bf16[384,2048]{1,0:T(8,128)(2,1)}, bf16[384,2048]{1,0:T(8,128)(2,1)S(1)}, u32[]{:S(2)}, u32[]{:S(2)}) collective-permute-start(bf16[384,2048]{1,0:T(8,128)(2,1)} %get-tuple-element.211), channel_id=1, source_target_pairs={{0,16},{16,0},{1,17},{17,1},{2,18},{18,2},{3,19},{19,3},{4,20},{20... | collective-permute-start | bytes 4718600 | tf_op jit(solution)/shard_map/ppermute | solution.py:23
  100.7 14.7 %collective-permute-start.15 = (bf16[256,1024]{1,0:T(8,128)(2,1)}, bf16[256,1024]{1,0:T(8,128)(2,1)}, u32[]{:S(2)}, u32[]{:S(2)}) collective-permute-start(bf16[256,1024]{1,0:T(8,128)(2,1)} %get-tuple-element.84), channel_id=1, source_target_pairs={{0,1},{1,0},{2,3},{3,2},{4,5},{5,4},{6,7},{7,6},{8,9},{9,8},{10,11... | collective-permute-start | bytes 1572872 | tf_op jit(solution)/shard_map/cond/branch_1_fun/ppermute | solution.py:23
  100.7 14.7 %collective-permute-start.16 = (bf16[256,1024]{1,0:T(8,128)(2,1)}, bf16[256,1024]{1,0:T(8,128)(2,1)}, u32[]{:S(2)}, u32[]{:S(2)}) collective-permute-start(bf16[256,1024]{1,0:T(8,128)(2,1)} %get-tuple-element.85), channel_id=1, source_target_pairs={{0,2},{1,3},{2,0},{3,1},{4,6},{5,7},{6,4},{7,5},{8,10},{9,11},{10,... | collective-permute-start | bytes 1572872 | tf_op jit(solution)/shard_map/cond/branch_1_fun/ppermute | solution.py:23
  101.1 5.6 %collective-permute-start.13 = (f32[128,256]{1,0:T(8,128)S(1)}, f32[128,256]{1,0:T(8,128)S(1)}, u32[]{:S(2)}, u32[]{:S(2)}) collective-permute-start(f32[128,256]{1,0:T(8,128)S(1)} %get-tuple-element.83), channel_id=1, source_target_pairs={{0,4},{1,5},{2,6},{3,7},{4,0},{5,1},{6,2},{7,3},{8,12},{9,13},{10,... | collective-permute-start | bytes 393224 | tf_op jit(solution)/shard_map/cond/branch_1_fun/ppermute | solution.py:23
  106.7 8.6 %collective-permute-start.14 = (f32[128,256]{1,0:T(8,128)S(1)}, f32[128,256]{1,0:T(8,128)S(1)}, u32[]{:S(2)}, u32[]{:S(2)}) collective-permute-start(f32[128,256]{1,0:T(8,128)S(1)} %add.24), channel_id=1, source_target_pairs={{0,8},{1,9},{2,10},{3,11},{4,12},{5,13},{6,14},{7,15},{8,0},{9,1},... | collective-permute-start | bytes 393224 | tf_op jit(solution)/shard_map/cond/branch_1_fun/ppermute | solution.py:23
  115.4 30.9 %collective-permute-start.35 = (bf16[256,1024]{1,0:T(8,128)(2,1)}, bf16[256,1024]{1,0:T(8,128)(2,1)}, u32[]{:S(2)}, u32[]{:S(2)}) collective-permute-start(bf16[256,1024]{1,0:T(8,128)(2,1)} %get-tuple-element.215), channel_id=1, source_target_pairs={{0,4},{1,5},{2,6},{3,7},{4,0},{5,1},{6,2},{7,3},{8,12},{9,13},{10,... | collective-permute-start | bytes 1572872 | tf_op jit(solution)/shard_map/ppermute | solution.py:23
  115.6 30.6 %collective-permute-start.36 = (bf16[256,1024]{1,0:T(8,128)(2,1)}, bf16[256,1024]{1,0:T(8,128)(2,1)}, u32[]{:S(2)}, u32[]{:S(2)}) collective-permute-start(bf16[256,1024]{1,0:T(8,128)(2,1)} %get-tuple-element.218), channel_id=1, source_target_pairs={{0,8},{1,9},{2,10},{3,11},{4,12},{5,13},{6,14},{7,15},{8,0},{9,1},... | collective-permute-start | bytes 1572872 | tf_op jit(solution)/shard_map/ppermute | solution.py:23
  119.9 2.3 %collective-permute-start.18 = (bf16[256,1024]{1,0:T(8,128)(2,1)}, bf16[256,1024]{1,0:T(8,128)(2,1)}, u32[]{:S(2)}, u32[]{:S(2)}) collective-permute-start(bf16[256,1024]{1,0:T(8,128)(2,1)} %get-tuple-element.88), channel_id=1, source_target_pairs={{0,1},{1,0},{2,3},{3,2},{4,5},{5,4},{6,7},{7,6},{8,9},{9,8},{10,11... | collective-permute-start | bytes 1572872 | tf_op jit(solution)/shard_map/cond/branch_1_fun/ppermute | solution.py:23
  122.2 5.9 %collective-permute-start.19 = (bf16[512,512]{1,0:T(8,128)(2,1)}, bf16[512,512]{1,0:T(8,128)(2,1)}, u32[]{:S(2)}, u32[]{:S(2)}) collective-permute-start(bf16[512,512]{1,0:T(8,128)(2,1)} %get-tuple-element.89), channel_id=1, source_target_pairs={{0,1},{1,0},{2,3},{3,2},{4,5},{5,4},{6,7},{7,6},{8,9},{9,8},{10,11... | collective-permute-start | bytes 1572872 | tf_op jit(solution)/shard_map/cond/branch_1_fun/ppermute | solution.py:23
  122.3 5.8 %collective-permute-start.17 = (bf16[1,2,128,256]{3,2,1,0:T(8,128)(2,1)S(1)}, bf16[1,2,128,256]{3,2,1,0:T(8,128)(2,1)S(1)}, u32[]{:S(2)}, u32[]{:S(2)}) collective-permute-start(bf16[1,2,128,256]{3,2,1,0:T(8,128)(2,1)S(1)} %get-tuple-element.86), channel_id=1, source_target_pairs={{0,2},{1,3},{2,0},{3,1},{4,6},{5,7},{6,4},{7,5},{8,10},{9,11},{10,... | collective-permute-start | bytes 393224 | tf_op jit(solution)/shard_map/cond/branch_1_fun/ppermute | solution.py:23
  128.1 1.6 %collective-permute-start.20 = (bf16[2,2,128,256]{3,2,1,0:T(8,128)(2,1)S(1)}, bf16[2,2,128,256]{3,2,1,0:T(8,128)(2,1)S(1)}, u32[]{:S(2)}, u32[]{:S(2)}) collective-permute-start(bf16[2,2,128,256]{3,2,1,0:T(8,128)(2,1)S(1)} %pad_maximum_fusion.3), channel_id=1, source_target_pairs={{0,1},{1,0},{2,3},{3,2},{4,5},{5,4},{6,7},{7,6},{8,9},{9,8},{10,11... | collective-permute-start | bytes 786440 | tf_op jit(solution)/shard_map/cond/branch_1_fun/ppermute | solution.py:23
  133.5 12.7 %collective-permute-start.1 = (bf16[256,1024]{1,0:T(8,128)(2,1)}, bf16[256,1024]{1,0:T(8,128)(2,1)}, u32[]{:S(2)}, u32[]{:S(2)}) collective-permute-start(bf16[256,1024]{1,0:T(8,128)(2,1)} %get-tuple-element.92), channel_id=1, source_target_pairs={{0,2},{1,3},{2,0},{3,1},{4,6},{5,7},{6,4},{7,5},{8,10},{9,11},{10,... | collective-permute-start | bytes 1572872 | tf_op jit(solution)/shard_map/cond/branch_1_fun/ppermute | solution.py:23
  135.0 10.6 %collective-permute-start = (bf16[4,1,128,256]{3,2,1,0:T(8,128)(2,1)S(1)}, bf16[4,1,128,256]{3,2,1,0:T(8,128)(2,1)}, u32[]{:S(2)}, u32[]{:S(2)}) collective-permute-start(bf16[4,1,128,256]{3,2,1,0:T(8,128)(2,1)S(1)} %slice.13), channel_id=1, source_target_pairs={{0,16},{16,0},{1,17},{17,1},{2,18},{18,2},{3,19},{19,3},{4,20},{20... | collective-permute-start | bytes 786440 | tf_op jit(solution)/shard_map/cond/branch_1_fun/ppermute | solution.py:23

commit v4 on v3

--- a/solution.py
+++ b/solution.py
@@ -11,7 +11,7 @@
 gelu_cubic = 0.044715
 f32 = jnp.float32
 bf16 = jnp.bfloat16
-FORWARD_HINTS = (4, 1 / 16)
+FORWARD_HINTS = (4, 1)
 WEIGHT_HINT = 1 / 16
 INPUT_HINT = 1 / 16
 STACK_HINT = 458752
@@ -163,27 +163,24 @@
     return act, grad, outs[2 : 2 + len(remote)], outs[-2], outs[-1]
 
 
-def halves_body(idx_ref, *refs):
+def halves_body(block, which, *refs):
     row, out_ref = 0, refs[-1]
+    half = block // 2
     for src in refs[:-1]:
-        out_ref[row : row + src.shape[0]] = src[...]
-        row += src.shape[0]
+        rows, width = src.shape
+        for j in range(width // block):
+            cols = pl.ds(pl.multiple_of(j * block + which[0] * half, half), half)
+            out_ref[row : row + rows, j * half : (j + 1) * half] = src[:, cols]
+        row += rows
 
 
 def column_halves(which, arrays, block):
     width = arrays[0].shape[1]
-    half = block // 2
     rows = sum(a.shape[0] for a in arrays)
     return pl.pallas_call(
-        halves_body,
-        grid_spec=pltpu.PrefetchScalarGridSpec(
-            num_scalar_prefetch=1,
-            grid=(width // block,),
-            in_specs=[
-                pl.BlockSpec((a.shape[0], half), lambda j, which: (0, 2 * j + which[0])) for a in arrays
-            ],
-            out_specs=pl.BlockSpec((rows, half), lambda j, which: (0, j)),
-        ),
+        functools.partial(halves_body, block),
+        in_specs=[pl.BlockSpec(memory_space=pltpu.SMEM)]
+        + [pl.BlockSpec(a.shape, lambda: (0, 0)) for a in arrays],
         out_shape=jax.ShapeDtypeStruct((rows, width // 2), bf16),
         compiler_params=params(8),
         cost_estimate=cost(1 / 16, 0, 2 * rows * width),
@@ -303,7 +300,8 @@
     total = rows_of(take(2))
     for _ in range(n_terms):
         total = total + rows_of(take(2)).astype(f32)
-    left_ref, latent_ref, far_latent_ref, tokens_ref, far_tokens_ref, input_ref, left_grad_ref = take(7)
+    left_ref, latent_ref, far_latent_ref, tokens_ref, far_tokens_ref = take(5)
+    input_ref, left_grad_ref = take(2)
     order = [k ^ idx_ref[0] for k in range(latent_ref.shape[0])]
     latent = jnp.concatenate([latent_ref[k] for k in order], axis=0)
     far_latent = jnp.concatenate([far_latent_ref[k] for k in order], axis=0)
@@ -322,6 +320,7 @@
 
 
 def input_grads(idx, local, terms, left, latent, far_latent, tokens, far_tokens, block):
+    block = 2 * block
     width, rank = left.shape
     chunk_rows = local[0].shape[0]
     rows = 2 * chunk_rows
@@ -334,7 +333,8 @@
             num_scalar_prefetch=1,
             grid=(width // block,),
             in_specs=[chunk_spec] * (2 + 2 * len(terms))
-            + [left_spec, latent_spec(latent), latent_spec(far_latent), token_spec, token_spec],
+            + [left_spec, latent_spec(latent), latent_spec(far_latent)]
+            + [token_spec, token_spec],
             out_specs=[token_spec, left_spec],
         ),
         out_shape=[
@@ -373,8 +373,8 @@
     return kept + from_partner(sent, "mp", bit)
 
 
-def high_sum(part):
-    for bit in range(2, lax.axis_size("mp").bit_length() - 1):
+def high_sum(part, first_bit=2):
+    for bit in range(first_bit, lax.axis_size("mp").bit_length() - 1):
         part = part + from_partner(part, "mp", bit)
     return part.astype(bf16)[None, None]
 
@@ -415,23 +415,28 @@
         part = jnp.dot(tokens, left, preferred_element_type=f32)
         part = halved_sum(jnp.split(part, 2, axis=0), 0)
         core = from_partner(after(tokens, part), "mp", 0)
-        return halved_sum(jnp.split(part, 2, axis=0), 1), core
-
-    def high_part(part, tokens):
+        tokens = after(tokens, part)
+        slices = [tokens[:half_rows], tokens[cut:half_rows], tokens[half_rows:]]
+        return halved_sum(jnp.split(part, 2, axis=0), 1), core, slices
+
+    def high_part(part, tokens, y_rows, rest, first):
         far_tokens = from_partner(tokens, "dp", 0)
-        near_y = from_partner(tokens[:half_rows], "mp", 1)
-        quarter_sum = high_sum(part)
-        second = over_high(after(tokens[cut:half_rows], quarter_sum))
-        far = from_partner(quarter_sum, "dp", 0)
+        near_y = from_partner(y_rows, "mp", 1)
+        stack = high_sum(part)
+        second = over_high(after(rest, stack))
+        far = from_partner(stack, "dp", 0)
+        stack = jnp.concatenate([stack, from_partner(after(stack, near_y), "mp", 1)], axis=0)
         far_half = column_halves(mine, [far_tokens], block)
-        rest = after(tokens, quarter_sum)[half_rows:]
-        return gathered(quarter_sum), far, far_tokens, far_half, near_y, second, rest
-
-    low_sum, core = one_step(low_part, tokens, left_factor)
+        stack = jnp.concatenate([stack, from_partner(after(stack, far, far_half), "mp", 0)], axis=0)
+        high = [p for pair in zip(first, second) for p in pair]
+        return stack, far, far_tokens, far_half, near_y, second, column_halves(theirs, high, block)
+
+    low_sum, core, slices = one_step(low_part, tokens, left_factor)
     low_sum, first = after((low_sum, first))
-    latent, far_quarter, far_tokens, far_half, near_y, second, rest = one_step(
-        high_part, low_sum, tokens
-    )
+    latent, far_quarter, far_tokens, far_half, near_y, second, halves = one_step(
+        high_part, low_sum, tokens, *slices[:2], first
+    )
+    rest = after(slices[2], latent)
     third = over_high(rest)
     far_y = from_partner(rest, "mp", 1)
     received = [
@@ -440,9 +445,7 @@
         [[(core, 1, half_rows)], [(far_y, 0, half_rows)]] + [[(p, 0, half_rows)] for p in third],
     ]
 
-    halves = column_halves(theirs, [p[0] for tap in received[0][2:] for p in tap], block)
     far_halves = from_partner(halves, "dp", 0)
-    latent, halves = after((latent, halves))
     forward = functools.partial(forward_chunk, idx=idx, tokens=tokens, latent=latent)
     forward = functools.partial(forward, weight=block_weight, right=right_factor, cotangent=out_cotangent)
     act, near_grad, near_out, near_local, near_latent = forward(
@@ -450,7 +453,7 @@
     )
     far_near_grad = from_partner(after(near_grad, far_halves), "dp", 0)
     near_terms = over_high_terms(near_out, far_y)
-    far_y_half = from_partner(after(far_half, far_y, third, near_grad), "mp", 1)
+    far_y_half = from_partner(after(far_half, near_grad, third), "mp", 1)
     act, grad, far_out, far_local, far_latent_term = forward(
         1, remote=received[1], act_before=act, packed=len(high_bits)
     )
@@ -465,19 +468,18 @@
         return high_sum(part), [from_partner(t, "mp", bit) for bit, t in enumerate(terms)]
 
     def gather_grad(stack, core_term, far_half):
+        stack = jnp.concatenate([stack, from_partner(stack, "mp", 1)], axis=0)
         core_term = from_partner(core_term, "mp", 0)
-        far_core = from_partner(after(far_half, core_term), "mp", 0)
-        stack = jnp.concatenate([stack, from_partner(stack, "mp", 1)], axis=0)
-        stack = jnp.concatenate([stack, from_partner(after(stack, far_core), "mp", 0)], axis=0)
-        return stack, core_term, far_core
-
+        stack, core_term = after((stack, core_term))
+        far_core = from_partner(after(far_half, stack), "mp", 0)
+        return jnp.concatenate([stack, from_partner(stack, "mp", 0)], axis=0), core_term, far_core
+
+    near_latent, far_near_grad = after((near_latent, far_near_grad))
     low_sum = one_step(low_grad, near_latent, far_latent_term)
-    low_sum, near_terms, far_near_grad, far_y_half = after(
-        (low_sum, near_terms, far_near_grad, far_y_half)
-    )
+    low_sum, far_y_half, near_terms = after((low_sum, far_y_half, near_terms))
     quarter_sum, low_terms = one_step(high_grad, low_sum, *near_out[:2])
+    far_terms = over_high_terms(far_out, quarter_sum)
     near_terms = low_terms + near_terms
-    far_terms = over_high_terms(far_out, quarter_sum)
     gathered_both, core_term, far_core = one_step(
         gather_grad, stacked(quarter_sum, far_quarter), far_out[0], far_half
     )

time: 153 us -> 149 us (0.974)
  waiting for transfers between devices: 57.7 us -> 52.2 us
  starting transfers between devices: 42.6 us -> 44.8 us
  other arithmetic: 0.52 us -> 2.17 us
    ppermute x37, waiting for transfers between devices: 57.7 us -> 52.2 us  [from_partner(): lax.ppermute(shard, axis, [(i, i ^ 1 << distance) for i in range(lax.axis...]
    ppermute x37, starting transfers between devices: 42.6 us -> 44.8 us  [from_partner(): lax.ppermute(shard, axis, [(i, i ^ 1 << distance) for i in range(lax.axis...]
  transfers between devices with their start and end apart: 37 -> 37, of which waited for: 24 -> 19; matrix products, arithmetic and copies ran while one was open for 3% -> 4% of each run, Pallas kernels for 25% -> 26%
where the time goes in v4:
time: 149 us
  waiting for transfers between devices  52.2 us (35%)
  starting transfers between devices  44.8 us (30%)
  Pallas kernels  43.5 us (29%)
  local copies, waits for them, and re-layouts  3.39 us (2%)
  other arithmetic  2.17 us (1%)
  matrix products  1.88 us (1%)
    ppermute x37, waiting for transfers between devices, from_partner(): lax.ppermute(shard, axis, [(i, i ^ 1 << distance) for i in range(lax.axis...  52.2 us
    ppermute x37, starting transfers between devices, from_partner(): lax.ppermute(shard, axis, [(i, i ^ 1 << distance) for i in range(lax.axis...  44.8 us
    pallas_call x2, Pallas kernels, forward_chunk(): pl.pallas_call(functools.partial(forward_body, local_taps, [len(t) for t...  24 us
    pallas_call x1, Pallas kernels, weight_grads(): pl.pallas_call(functools.partial(weights_body, local_taps, [len(t) for t...  9.97 us
    pallas_call x1, Pallas kernels, input_grads(): pl.pallas_call(functools.partial(inputs_body, len(terms)), grid_spec=pltp...  5.37 us
    pallas_call x2, Pallas kernels, column_halves(): pl.pallas_call(functools.partial(halves_body, block), in_specs=[pl.BlockS...  3.32 us
  transfers between devices with their start and end apart: 37, of which 19 were waited for; matrix products, arithmetic and copies ran while one was open for 4% of the time, Pallas kernels for 26%

profile of v4, /device:TPU:0, one launch (start us, length us, event | category | flops | bytes accessed | tf_op | source)
XLA Modules:
  0.0 148.9 jit_solution(9857137165944658448)
XLA Ops:
  0.6 1.0 slice.15
  1.6 4.1 %collective-permute-start.25 = (bf16[128,1024]{1,0:T(8,128)(2,1)S(1)}, bf16[128,1024]{1,0:T(8,128)(2,1)S(1)}, u32[]{:S(2)}, u32[]{:S(2)}) collective-permute-start(bf16[128,1024]{1,0:T(8,128)(2,1)S(1)} %slice.15), channel_id=1, source_target_pairs={{0,8},{1,9},{2,10},{3,11},{4,12},{5,13},{6,14},{7,15},{8,0},{9,1},... | collective-permute-start | bytes 786440 | tf_op jit(solution)/shard_map/ppermute | solution.py:23
  5.7 1.6 %collective-permute-start.24 = (bf16[128,1024]{1,0:T(8,128)(2,1)S(1)}, bf16[128,1024]{1,0:T(8,128)(2,1)S(1)}, u32[]{:S(2)}, u32[]{:S(2)}) collective-permute-start(bf16[128,1024]{1,0:T(8,128)(2,1)S(1)} %slice.15), channel_id=1, source_target_pairs={{0,4},{1,5},{2,6},{3,7},{4,0},{5,1},{6,2},{7,3},{8,12},{9,13},{10,... | collective-permute-start | bytes 786440 | tf_op jit(solution)/shard_map/ppermute | solution.py:23
  7.3 9.7 %conditional.6 = (f32[128,256]{1,0:T(8,128)S(1)}, bf16[512,1024]{1,0:T(8,128)(2,1)}, bf16[256,1024]{1,0:T(8,128)(2,1)S(1)}, bf16[128,1024]{1,0:T(8,128)(2,1)}, bf16[256,1024]{1,0:T(8,128)(2,1)}) conditional(s32[]{:T(128)} %convert_element_type.8, () %tuple.70, (bf16[512,1024]{1,0:T(8,128)(2,1)}, bf16[1024,256]{1,0:T(8,128)(2,1)}) %tuple.71), branch_computations={%region_0.0_spmd, %region_1.2_spmd} | conditional | flops 268730368 | bytes 17432854 | solution.py:366
  7.3 1.9 %fusion.3 = f32[512,256]{1,0:T(8,128)S(1)} fusion(bf16[512,1024]{1,0:T(8,128)(2,1)} %get-tuple-element.85, bf16[1024,256]{1,0:T(8,128)(2,1)} %get-tuple-element.84), kind=kOutput, calls=%fused_computation.18 | convolution fusion | flops 268435456 | bytes 2097152 | tf_op jit(solution)/shard_map/cond/branch_1_fun/dot_general | solution.py:415
  9.3 1.5 %collective-permute-done.21 = f32[256,256]{1,0:T(8,128)S(1)} collective-permute-done((f32[256,256]{1,0:T(8,128)S(1)}, f32[256,256]{1,0:T(8,128)S(1)}, u32[]{:S(2)}, u32[]{:S(2)}) %collective-permute-start.21) | collective-permute-done | bytes 262176 | tf_op jit(solution)/shard_map/cond/branch_1_fun/ppermute | solution.py:23
  11.1 1.6 %collective-permute-start.22 = (f32[128,256]{1,0:T(8,128)S(1)}, f32[128,256]{1,0:T(8,128)S(1)}, u32[]{:S(2)}, u32[]{:S(2)}) collective-permute-start(f32[128,256]{1,0:T(8,128)S(1)} %slice_select_fusion.1), channel_id=1, source_target_pairs={{0,2},{1,3},{2,0},{3,1},{4,6},{5,7},{6,4},{7,5},{8,10},{9,11},{10,... | collective-permute-start | bytes 393224 | tf_op jit(solution)/shard_map/cond/branch_1_fun/ppermute | solution.py:23
  14.3 2.7 %collective-permute-done.22 = f32[128,256]{1,0:T(8,128)S(1)} collective-permute-done((f32[128,256]{1,0:T(8,128)S(1)}, f32[128,256]{1,0:T(8,128)S(1)}, u32[]{:S(2)}, u32[]{:S(2)}) %collective-permute-start.22) | collective-permute-done | bytes 131104 | tf_op jit(solution)/shard_map/cond/branch_1_fun/ppermute | solution.py:23
  17.9 30.6 %conditional.7 = (bf16[4,1,128,256]{3,2,1,0:T(8,128)(2,1)S(1)}, bf16[1,1,128,256]{3,2,1,0:T(8,128)(2,1)}, bf16[512,1024]{1,0:T(8,128)(2,1)}, bf16[512,512]{1,0:T...) conditional(s32[]{:T(128)} %convert_element_type.8, () %tuple.72, ...), branch_computations={%region_2.3_spmd, %region_3.4_spmd} | conditional | flops 425985 | bytes 12124596 | solution.py:366
  17.9 1.5 %collective-permute-start.7 = (bf16[512,1024]{1,0:T(8,128)(2,1)}, bf16[512,1024]{1,0:T(8,128)(2,1)}, u32[]{:S(2)}, u32[]{:S(2)}) collective-permute-start(bf16[512,1024]{1,0:T(8,128)(2,1)} %get-tuple-element.90), channel_id=1, source_target_pairs={{0,16},{16,0},{1,17},{17,1},{2,18},{18,2},{3,19},{19,3},{4,20},{20... | collective-permute-start | bytes 3145736 | tf_op jit(solution)/shard_map/cond/branch_1_fun/ppermute | solution.py:23
  19.5 1.5 %collective-permute-start.4 = (bf16[256,1024]{1,0:T(8,128)(2,1)S(1)}, bf16[256,1024]{1,0:T(8,128)(2,1)}, u32[]{:S(2)}, u32[]{:S(2)}) collective-permute-start(bf16[256,1024]{1,0:T(8,128)(2,1)S(1)} %get-tuple-element.87), channel_id=1, source_target_pairs={{0,2},{1,3},{2,0},{3,1},{4,6},{5,7},{6,4},{7,5},{8,10},{9,11},{10,... | collective-permute-start | bytes 1572872 | tf_op jit(solution)/shard_map/cond/branch_1_fun/ppermute | solution.py:23
  21.0 1.4 collective-permute-start.2
  22.4 3.5 %collective-permute-done.2 = f32[128,256]{1,0:T(8,128)S(1)} collective-permute-done((f32[128,256]{1,0:T(8,128)S(1)}, f32[128,256]{1,0:T(8,128)S(1)}, u32[]{:S(2)}, u32[]{:S(2)}) %collective-permute-start.2) | collective-permute-done | bytes 131104 | tf_op jit(solution)/shard_map/cond/branch_1_fun/ppermute | solution.py:23
  26.0 2.0 %collective-permute-start.3 = (f32[128,256]{1,0:T(8,128)S(1)}, f32[128,256]{1,0:T(8,128)S(1)}, u32[]{:S(2)}, u32[]{:S(2)}) collective-permute-start(f32[128,256]{1,0:T(8,128)S(1)} %add.20), channel_id=1, source_target_pairs={{0,8},{1,9},{2,10},{3,11},{4,12},{5,13},{6,14},{7,15},{8,0},{9,1},... | collective-permute-start | bytes 393224 | tf_op jit(solution)/shard_map/cond/branch_1_fun/ppermute | solution.py:23
  28.0 5.4 %collective-permute-done.3 = f32[128,256]{1,0:T(8,128)S(1)} collective-permute-done((f32[128,256]{1,0:T(8,128)S(1)}, f32[128,256]{1,0:T(8,128)S(1)}, u32[]{:S(2)}, u32[]{:S(2)}) %collective-permute-start.3) | collective-permute-done | bytes 131104 | tf_op jit(solution)/shard_map/cond/branch_1_fun/ppermute | solution.py:23
  35.0 3.5 %collective-permute-start.9 = (bf16[128,1024]{1,0:T(8,128)(2,1)}, bf16[128,1024]{1,0:T(8,128)(2,1)}, u32[]{:S(2)}, u32[]{:S(2)}) collective-permute-start(bf16[128,1024]{1,0:T(8,128)(2,1)} %get-tuple-element.93), channel_id=1, source_target_pairs={{0,4},{1,5},{2,6},{3,7},{4,0},{5,1},{6,2},{7,3},{8,12},{9,13},{10,... | collective-permute-start | bytes 786440 | tf_op jit(solution)/shard_map/cond/branch_1_fun/ppermute | solution.py:23
  39.0 4.1 %collective-permute-done.7.refs_0_ = bf16[512,1024]{1,0:T(8,128)(2,1)} collective-permute-done((bf16[512,1024]{1,0:T(8,128)(2,1)}, bf16[512,1024]{1,0:T(8,128)(2,1)}, u32[]{:S(2)}, u32[]{:S(2)}) %collective-permute-start.7) | collective-permute-done | bytes 1048608 | tf_op jit(solution)/shard_map/cond/branch_1_fun/ppermute | solution.py:23
  43.1 1.4 column_halves.2
  44.6 1.8 %collective-permute-done.10.refs_3_ = bf16[128,1024]{1,0:T(8,128)(2,1)} collective-permute-done((bf16[128,1024]{1,0:T(8,128)(2,1)}, bf16[128,1024]{1,0:T(8,128)(2,1)}, u32[]{:S(2)}, u32[]{:S(2)}) %collective-permute-start.10) | collective-permute-done | bytes 262176 | tf_op jit(solution)/shard_map/cond/branch_1_fun/ppermute | solution.py:23
  46.5 2.0 %column_halves.3 = bf16[512,512]{1,0:T(8,128)(2,1)} custom-call(s32[1]{0:T(128)S(6)} %sub.4.which, bf16[128,1024]{1,0:T(8,128)(2,1)S(1)} %get-tuple-element.95.refs_0_, bf16[128,1024]{1,0:T(8,128)(2,1)} %collective-permute-done.9.refs_1_, bf16[128,1024]{1,0:T(8,128)(2,1)S(1)} %get-tuple-element.96.refs_2_, bf16[128,1024]{1,0:T(8,128)(2,1)} %collective-permute-done.10.refs_3_), custom_call_target="tpu_custom_call" | custom-call | bytes 65536 | tf_op jit(solution)/shard_map/cond/branch_1_fun/column_halves/pallas_call | solution.py:180
  49.3 3.1 %collective-permute-start.28 = (bf16[256,1024]{1,0:T(8,128)(2,1)}, bf16[256,1024]{1,0:T(8,128)(2,1)S(1)}, u32[]{:S(2)}, u32[]{:S(2)}) collective-permute-start(bf16[256,1024]{1,0:T(8,128)(2,1)} %get-tuple-element.202), channel_id=1, source_target_pairs={{0,8},{1,9},{2,10},{3,11},{4,12},{5,13},{6,14},{7,15},{8,0},{9,1},... | collective-permute-start | bytes 1572872 | tf_op jit(solution)/shard_map/ppermute | solution.py:23
  52.4 1.7 %collective-permute-start.27 = (bf16[256,1024]{1,0:T(8,128)(2,1)}, bf16[256,1024]{1,0:T(8,128)(2,1)S(1)}, u32[]{:S(2)}, u32[]{:S(2)}) collective-permute-start(bf16[256,1024]{1,0:T(8,128)(2,1)} %get-tuple-element.202), channel_id=1, source_target_pairs={{0,4},{1,5},{2,6},{3,7},{4,0},{5,1},{6,2},{7,3},{8,12},{9,13},{10,... | collective-permute-start | bytes 1572872 | tf_op jit(solution)/shard_map/ppermute | solution.py:23
  54.1 1.5 %collective-permute-start.26 = (bf16[256,1024]{1,0:T(8,128)(2,1)}, bf16[256,1024]{1,0:T(8,128)(2,1)S(1)}, u32[]{:S(2)}, u32[]{:S(2)}) collective-permute-start(bf16[256,1024]{1,0:T(8,128)(2,1)} %get-tuple-element.202), channel_id=1, source_target_pairs={{0,2},{1,3},{2,0},{3,1},{4,6},{5,7},{6,4},{7,5},{8,10},{9,11},{10,... | collective-permute-start | bytes 1572872 | tf_op jit(solution)/shard_map/ppermute | solution.py:23
  56.2 12.1 %forward_chunk.2 = (bf16[512,2048]{1,0:T(8,128)(2,1)}, bf16[256,2048]{1,0:T(8,128)(2,1)}, bf16[256,1024]{1,0:T(8,128)(2,1)}, bf16[256,1024]{1,0:T(8,128)(2,1)}, ...) custom-call(s32[2]{0:T(128)S(1)} %pad_add_fusion.idx_ref, ...), custom_call_target="tpu_custom_call" | custom-call | flops 17179869184 | bytes 71303168 | tf_op jit(solution)/shard_map/forward_chunk/pallas_call | solution.py:145
  68.3 1.5 %collective-permute-start.30 = (bf16[256,2048]{1,0:T(8,128)(2,1)}, bf16[256,2048]{1,0:T(8,128)(2,1)}, u32[]{:S(2)}, u32[]{:S(2)}) collective-permute-start(bf16[256,2048]{1,0:T(8,128)(2,1)} %get-tuple-element.213), channel_id=1, source_target_pairs={{0,16},{16,0},{1,17},{17,1},{2,18},{18,2},{3,19},{19,3},{4,20},{20... | collective-permute-start | bytes 3145736 | tf_op jit(solution)/shard_map/ppermute | solution.py:23
  69.9 4.3 %collective-permute-done.28.refs_6_ = bf16[256,1024]{1,0:T(8,128)(2,1)S(1)} collective-permute-done((bf16[256,1024]{1,0:T(8,128)(2,1)}, bf16[256,1024]{1,0:T(8,128)(2,1)S(1)}, u32[]{:S(2)}, u32[]{:S(2)}) %collective-permute-start.28) | collective-permute-done | bytes 524320 | tf_op jit(solution)/shard_map/ppermute | solution.py:23
  74.3 1.9 %collective-permute-start.31 = (bf16[512,512]{1,0:T(8,128)(2,1)}, bf16[512,512]{1,0:T(8,128)(2,1)}, u32[]{:S(2)}, u32[]{:S(2)}) collective-permute-start(bf16[512,512]{1,0:T(8,128)(2,1)} %copy-done.9), channel_id=1, source_target_pairs={{0,2},{1,3},{2,0},{3,1},{4,6},{5,7},{6,4},{7,5},{8,10},{9,11},{10,... | collective-permute-start | bytes 1572872 | tf_op jit(solution)/shard_map/ppermute | solution.py:23
  76.1 1.6 %collective-permute-start.33 = (bf16[256,1024]{1,0:T(8,128)(2,1)}, bf16[256,1024]{1,0:T(8,128)(2,1)}, u32[]{:S(2)}, u32[]{:S(2)}) collective-permute-start(bf16[256,1024]{1,0:T(8,128)(2,1)} %get-tuple-element.221), channel_id=1, source_target_pairs={{0,8},{1,9},{2,10},{3,11},{4,12},{5,13},{6,14},{7,15},{8,0},{9,1},... | collective-permute-start | bytes 1572872 | tf_op jit(solution)/shard_map/ppermute | solution.py:23
  77.8 2.3 %collective-permute-start.32 = (bf16[256,1024]{1,0:T(8,128)(2,1)}, bf16[256,1024]{1,0:T(8,128)(2,1)}, u32[]{:S(2)}, u32[]{:S(2)}) collective-permute-start(bf16[256,1024]{1,0:T(8,128)(2,1)} %get-tuple-element.219), channel_id=1, source_target_pairs={{0,4},{1,5},{2,6},{3,7},{4,0},{5,1},{6,2},{7,3},{8,12},{9,13},{10,... | collective-permute-start | bytes 1572872 | tf_op jit(solution)/shard_map/ppermute | solution.py:23
  80.1 11.9 %forward_chunk.3 = (bf16[512,2048]{1,0:T(8,128)(2,1)}, bf16[384,2048]{1,0:T(8,128)(2,1)}, bf16[256,1024]{1,0:T(8,128)(2,1)}, bf16[256,1024]{1,0:T(8,128)(2,1)}, ...) custom-call(s32[2]{0:T(128)S(1)} %pad_add_fusion.idx_ref, ...), custom_call_target="tpu_custom_call", output_to_operand_aliasing={{0}: (13, {})} | custom-call | flops 4294967296 | bytes 17825792 | tf_op jit(solution)/shard_map/forward_chunk/pallas_call | solution.py:145
  93.0 9.3 %conditional.8 = (f32[128,256]{1,0:T(8,128)S(1)}) conditional(s32[]{:T(128)} %convert_element_type.8, () %tuple.77, (f32[256,256]{1,0:T(8,128)S(1)}, f32[256,256]{1,0:T(8,128)S(1)}) %tuple.114), branch_computations={%region_4.5_spmd, %region_5.6_spmd} | conditional | flops 294920 | bytes 4325554 | solution.py:366
  93.7 1.9 %collective-permute-done.11 = f32[256,256]{1,0:T(8,128)} collective-permute-done((f32[256,256]{1,0:T(8,128)}, f32[256,256]{1,0:T(8,128)}, u32[]{:S(2)}, u32[]{:S(2)}) %collective-permute-start.11) | collective-permute-done | bytes 262176 | tf_op jit(solution)/shard_map/cond/branch_1_fun/ppermute | solution.py:23
  95.6 1.0 select_add_fusion.2
  97.2 5.0 %collective-permute-done.12 = f32[128,256]{1,0:T(8,128)S(1)} collective-permute-done((f32[128,256]{1,0:T(8,128)S(1)}, f32[128,256]{1,0:T(8,128)S(1)}, u32[]{:S(2)}, u32[]{:S(2)}) %collective-permute-start.12) | collective-permute-done | bytes 131104 | tf_op jit(solution)/shard_map/cond/branch_1_fun/ppermute | solution.py:23
  102.3 14.7 %conditional.9 = (bf16[1,1,128,256]{3,2,1,0:T(8,128)(2,1)S(1)}, bf16[256,1024]{1,0:T(8,128)(2,1)}, bf16[256,1024]{1,0:T(8,128)(2,1)}) conditional(s32[]{:T(128)} %convert_element_type.8, () %tuple.76, (f32[128,256]{1,0:T(8,128)S(1)}, bf16[256,1024]{1,0:T(8,128)(2,1)}, bf16[256,1024]{1,0:T(8,128)(2,1)}) %tuple.85), branch_computations={%region_6.7_spmd, %region_7.8_spmd} | conditional | flops 98304 | bytes 5963960 | solution.py:366
  103.3 5.2 %collective-permute-done.13 = f32[128,256]{1,0:T(8,128)S(1)} collective-permute-done((f32[128,256]{1,0:T(8,128)S(1)}, f32[128,256]{1,0:T(8,128)S(1)}, u32[]{:S(2)}, u32[]{:S(2)}) %collective-permute-start.13) | collective-permute-done | bytes 131104 | tf_op jit(solution)/shard_map/cond/branch_1_fun/ppermute | solution.py:23
  108.6 1.0 collective-permute-start.14
  109.6 7.3 %collective-permute-done.14 = f32[128,256]{1,0:T(8,128)S(1)} collective-permute-done((f32[128,256]{1,0:T(8,128)S(1)}, f32[128,256]{1,0:T(8,128)S(1)}, u32[]{:S(2)}, u32[]{:S(2)}) %collective-permute-start.14) | collective-permute-done | bytes 131104 | tf_op jit(solution)/shard_map/cond/branch_1_fun/ppermute | solution.py:23
  117.4 2.5 %collective-permute-start.36 = (bf16[256,1024]{1,0:T(8,128)(2,1)}, bf16[256,1024]{1,0:T(8,128)(2,1)}, u32[]{:S(2)}, u32[]{:S(2)}) collective-permute-start(bf16[256,1024]{1,0:T(8,128)(2,1)} %get-tuple-element.243), channel_id=1, source_target_pairs={{0,8},{1,9},{2,10},{3,11},{4,12},{5,13},{6,14},{7,15},{8,0},{9,1},... | collective-permute-start | bytes 1572872 | tf_op jit(solution)/shard_map/ppermute | solution.py:23
  120.7 8.4 %conditional.10 = (bf16[4,2,128,256]{3,2,1,0:T(8,128)(2,1)S(1)}, bf16[256,1024]{1,0:T(8,128)(2,1)}, bf16[512,512]{1,0:T(8,128)(2,1)}) conditional(s32[]{:T(128)} %convert_element_type.8, () %tuple.86, (bf16[1,2,128,256]{3,2,1,0:T(8,128)(2,1)S(1)}, bf16[256,1024]{1,0:T(8,128)(2,1)}, bf16[512,512]{1,0:T(8,128)(2,1)}) %tuple.115), branch_computations={%region_8.9_spmd, %region_9.10_spmd} | conditional | flops 393216 | bytes 7340216 | solution.py:366
  120.8 1.6 %collective-permute-start.17 = (bf16[1,2,128,256]{3,2,1,0:T(8,128)(2,1)S(1)}, bf16[1,2,128,256]{3,2,1,0:T(8,128)(2,1)S(1)}, u32[]{:S(2)}, u32[]{:S(2)}) collective-permute-start(bf16[1,2,128,256]{3,2,1,0:T(8,128)(2,1)S(1)} %get-tuple-element.102), channel_id=1, source_target_pairs={{0,2},{1,3},{2,0},{3,1},{4,6},{5,7},{6,4},{7,5},{8,10},{9,11},{10,... | collective-permute-start | bytes 393224 | tf_op jit(solution)/shard_map/cond/branch_1_fun/ppermute | solution.py:23
  122.4 4.3 %collective-permute-done.17 = bf16[1,2,128,256]{3,2,1,0:T(8,128)(2,1)S(1)} collective-permute-done((bf16[1,2,128,256]{3,2,1,0:T(8,128)(2,1)S(1)}, bf16[1,2,128,256]{3,2,1,0:T(8,128)(2,1)S(1)}, u32[]{:S(2)}, u32[]{:S(2)}) %collective-permute-start.17) | collective-permute-done | bytes 131104 | tf_op jit(solution)/shard_map/cond/branch_1_fun/ppermute | solution.py:23
  127.3 1.8 %collective-permute-done.19 = bf16[2,2,128,256]{3,2,1,0:T(8,128)(2,1)S(1)} collective-permute-done((bf16[2,2,128,256]{3,2,1,0:T(8,128)(2,1)S(1)}, bf16[2,2,128,256]{3,2,1,0:T(8,128)(2,1)S(1)}, u32[]{:S(2)}, u32[]{:S(2)}) %collective-permute-start.19) | collective-permute-done | bytes 262176 | tf_op jit(solution)/shard_map/cond/branch_1_fun/ppermute | solution.py:23
  129.2 14.4 %conditional.11 = (bf16[4,1,128,256]{3,2,1,0:T(8,128)(2,1)}, bf16[256,1024]{1,0:T(8,128)(2,1)}, bf16[7,128,2048]{2,1,0:T(8,128)(2,1)}, bf16[256,2048]{1,0:T(8,128)(2,1)}) conditional(s32[]{:T(128)} %convert_element_type.8, () %tuple.88, (bf16[4,2,128,256]{3,2,1,0:T(8,128)(2,1)S(1)}, bf16[256,1024]{1,0:T(8,128)(2,1)}, s32[2]{0:T(128)S(1)}, ...), branch_computations={%region_10.11_spmd, %region_11.12_spmd} | conditional | flops 301989888 | bytes 5505064 | solution.py:366
  129.2 1.6 %collective-permute-start.1 = (bf16[256,1024]{1,0:T(8,128)(2,1)}, bf16[256,1024]{1,0:T(8,128)(2,1)}, u32[]{:S(2)}, u32[]{:S(2)}) collective-permute-start(bf16[256,1024]{1,0:T(8,128)(2,1)} %get-tuple-element.109), channel_id=1, source_target_pairs={{0,2},{1,3},{2,0},{3,1},{4,6},{5,7},{6,4},{7,5},{8,10},{9,11},{10,... | collective-permute-start | bytes 1572872 | tf_op jit(solution)/shard_map/cond/branch_1_fun/ppermute | solution.py:23
  131.4 10.0 %weight_grads.1 = (bf16[7,128,2048]{2,1,0:T(8,128)(2,1)}, bf16[256,2048]{1,0:T(8,128)(2,1)}) custom-call(s32[2]{0:T(128)S(1)} %get-tuple-element.110.idx_ref, bf16[512,1024]{1,0:T(8,128)(2,1)S(1)} %get-tuple-element.111.refs_0_.refs_1_.refs_2_, bf16[512,1024]{1,0:T(8,128)(2,1)S(1)} %get-tuple-element.111.refs_0_.refs_1_.refs_2_, ...), custom_call_target="tpu_custom_call" | custom-call | flops 301989888 | bytes 917504 | tf_op jit(solution)/shard_map/cond/branch_1_fun/weight_grads/pallas_call | solution.py:243
  141.4 2.1 %collective-permute-done.1 = bf16[256,1024]{1,0:T(8,128)(2,1)} collective-permute-done((bf16[256,1024]{1,0:T(8,128)(2,1)}, bf16[256,1024]{1,0:T(8,128)(2,1)}, u32[]{:S(2)}, u32[]{:S(2)}) %collective-permute-start.1) | collective-permute-done | bytes 524320 | tf_op jit(solution)/shard_map/cond/branch_1_fun/ppermute | solution.py:23
  143.5 5.4 %input_grads.1 = (bf16[512,1024]{1,0:T(8,128)(2,1)}, bf16[1024,256]{1,0:T(8,128)(2,1)}) custom-call(s32[2]{0:T(128)S(1)} %pad_add_fusion.idx_ref, f32[256,1024]{1,0:T(8,128)} %get-tuple-element.208.refs_0_, f32[256,1024]{1,0:T(8,128)} %get-tuple-element.209.refs_1_, bf16[256,1024]{1,0:T(8,128)(2,1)} %get-tuple-element.225.refs_2_, ...), custom_call_target="tpu_custom_call" | custom-call | flops 50331648 | bytes 655360 | tf_op jit(solution)/shard_map/input_grads/pallas_call | solution.py:330
  (81 shorter events, 12.7 us)
Async XLA Ops:
  1.6 16.1 %collective-permute-start.25 = (bf16[128,1024]{1,0:T(8,128)(2,1)S(1)}, bf16[128,1024]{1,0:T(8,128)(2,1)S(1)}, u32[]{:S(2)}, u32[]{:S(2)}) collective-permute-start(bf16[128,1024]{1,0:T(8,128)(2,1)S(1)} %slice.15), channel_id=1, source_target_pairs={{0,8},{1,9},{2,10},{3,11},{4,12},{5,13},{6,14},{7,15},{8,0},{9,1},... | collective-permute-start | bytes 786440 | tf_op jit(solution)/shard_map/ppermute | solution.py:23
  5.7 12.2 %collective-permute-start.24 = (bf16[128,1024]{1,0:T(8,128)(2,1)S(1)}, bf16[128,1024]{1,0:T(8,128)(2,1)S(1)}, u32[]{:S(2)}, u32[]{:S(2)}) collective-permute-start(bf16[128,1024]{1,0:T(8,128)(2,1)S(1)} %slice.15), channel_id=1, source_target_pairs={{0,4},{1,5},{2,6},{3,7},{4,0},{5,1},{6,2},{7,3},{8,12},{9,13},{10,... | collective-permute-start | bytes 786440 | tf_op jit(solution)/shard_map/ppermute | solution.py:23
  7.3 3.6 %copy-start.1 = (bf16[512,1024]{1,0:T(8,128)(2,1)S(1)}, bf16[512,1024]{1,0:T(8,128)(2,1)}, u32[]{:S(2)}) copy-start(bf16[512,1024]{1,0:T(8,128)(2,1)} %get-tuple-element.85) | copy-start | bytes 3145732 | tf_op jit(solution)/shard_map/cond
  9.2 1.6 %collective-permute-start.21 = (f32[256,256]{1,0:T(8,128)S(1)}, f32[256,256]{1,0:T(8,128)S(1)}, u32[]{:S(2)}, u32[]{:S(2)}) collective-permute-start(f32[256,256]{1,0:T(8,128)S(1)} %slice_select_fusion), channel_id=1, source_target_pairs={{0,1},{1,0},{2,3},{3,2},{4,5},{5,4},{6,7},{7,6},{8,9},{9,8},{10,11... | collective-permute-start | bytes 786440 | tf_op jit(solution)/shard_map/cond/branch_1_fun/ppermute | solution.py:23
  10.9 6.1 %collective-permute-start.23 = (bf16[512,1024]{1,0:T(8,128)(2,1)S(1)}, bf16[512,1024]{1,0:T(8,128)(2,1)}, u32[]{:S(2)}, u32[]{:S(2)}) collective-permute-start(bf16[512,1024]{1,0:T(8,128)(2,1)S(1)} %copy-done.1), channel_id=1, source_target_pairs={{0,1},{1,0},{2,3},{3,2},{4,5},{5,4},{6,7},{7,6},{8,9},{9,8},{10,11... | collective-permute-start | bytes 3145736 | tf_op jit(solution)/shard_map/cond/branch_1_fun/ppermute | solution.py:23
  11.1 5.8 %collective-permute-start.22 = (f32[128,256]{1,0:T(8,128)S(1)}, f32[128,256]{1,0:T(8,128)S(1)}, u32[]{:S(2)}, u32[]{:S(2)}) collective-permute-start(f32[128,256]{1,0:T(8,128)S(1)} %slice_select_fusion.1), channel_id=1, source_target_pairs={{0,2},{1,3},{2,0},{3,1},{4,6},{5,7},{6,4},{7,5},{8,10},{9,11},{10,... | collective-permute-start | bytes 393224 | tf_op jit(solution)/shard_map/cond/branch_1_fun/ppermute | solution.py:23
  17.7 38.5 %copy-start.6 = (bf16[128,1024]{1,0:T(8,128)(2,1)}, bf16[128,1024]{1,0:T(8,128)(2,1)S(1)}, u32[]{:S(2)}) copy-start(bf16[128,1024]{1,0:T(8,128)(2,1)S(1)} %collective-permute-done.25.refs_7_) | copy-start | bytes 786436
  17.9 38.3 %copy-start.7 = (bf16[128,1024]{1,0:T(8,128)(2,1)}, bf16[128,1024]{1,0:T(8,128)(2,1)S(1)}, u32[]{:S(2)}) copy-start(bf16[128,1024]{1,0:T(8,128)(2,1)S(1)} %collective-permute-done.24.refs_5_) | copy-start | bytes 786436
  17.9 25.2 %collective-permute-start.7 = (bf16[512,1024]{1,0:T(8,128)(2,1)}, bf16[512,1024]{1,0:T(8,128)(2,1)}, u32[]{:S(2)}, u32[]{:S(2)}) collective-permute-start(bf16[512,1024]{1,0:T(8,128)(2,1)} %get-tuple-element.90), channel_id=1, source_target_pairs={{0,16},{16,0},{1,17},{17,1},{2,18},{18,2},{3,19},{19,3},{4,20},{20... | collective-permute-start | bytes 3145736 | tf_op jit(solution)/shard_map/cond/branch_1_fun/ppermute | solution.py:23
  19.5 14.0 %collective-permute-start.4 = (bf16[256,1024]{1,0:T(8,128)(2,1)S(1)}, bf16[256,1024]{1,0:T(8,128)(2,1)}, u32[]{:S(2)}, u32[]{:S(2)}) collective-permute-start(bf16[256,1024]{1,0:T(8,128)(2,1)S(1)} %get-tuple-element.87), channel_id=1, source_target_pairs={{0,2},{1,3},{2,0},{3,1},{4,6},{5,7},{6,4},{7,5},{8,10},{9,11},{10,... | collective-permute-start | bytes 1572872 | tf_op jit(solution)/shard_map/cond/branch_1_fun/ppermute | solution.py:23
  21.0 5.0 %collective-permute-start.2 = (f32[128,256]{1,0:T(8,128)S(1)}, f32[128,256]{1,0:T(8,128)S(1)}, u32[]{:S(2)}, u32[]{:S(2)}) collective-permute-start(f32[128,256]{1,0:T(8,128)S(1)} %get-tuple-element.86), channel_id=1, source_target_pairs={{0,4},{1,5},{2,6},{3,7},{4,0},{5,1},{6,2},{7,3},{8,12},{9,13},{10,... | collective-permute-start | bytes 393224 | tf_op jit(solution)/shard_map/cond/branch_1_fun/ppermute | solution.py:23
  26.0 7.5 %collective-permute-start.3 = (f32[128,256]{1,0:T(8,128)S(1)}, f32[128,256]{1,0:T(8,128)S(1)}, u32[]{:S(2)}, u32[]{:S(2)}) collective-permute-start(f32[128,256]{1,0:T(8,128)S(1)} %add.20), channel_id=1, source_target_pairs={{0,8},{1,9},{2,10},{3,11},{4,12},{5,13},{6,14},{7,15},{8,0},{9,1},... | collective-permute-start | bytes 393224 | tf_op jit(solution)/shard_map/cond/branch_1_fun/ppermute | solution.py:23
  33.5 5.6 %collective-permute-start.5 = (bf16[1,1,128,256]{3,2,1,0:T(8,128)(2,1)S(1)}, bf16[1,1,128,256]{3,2,1,0:T(8,128)(2,1)S(1)}, u32[]{:S(2)}, u32[]{:S(2)}) collective-permute-start(bf16[1,1,128,256]{3,2,1,0:T(8,128)(2,1)S(1)} %fusion), channel_id=1, source_target_pairs={{0,2},{1,3},{2,0},{3,1},{4,6},{5,7},{6,4},{7,5},{8,10},{9,11},{10,... | collective-permute-start | bytes 196616 | tf_op jit(solution)/shard_map/cond/branch_1_fun/ppermute | solution.py:23
  34.0 12.3 %collective-permute-start.10 = (bf16[128,1024]{1,0:T(8,128)(2,1)}, bf16[128,1024]{1,0:T(8,128)(2,1)}, u32[]{:S(2)}, u32[]{:S(2)}) collective-permute-start(bf16[128,1024]{1,0:T(8,128)(2,1)} %get-tuple-element.93), channel_id=1, source_target_pairs={{0,8},{1,9},{2,10},{3,11},{4,12},{5,13},{6,14},{7,15},{8,0},{9,1},... | collective-permute-start | bytes 786440 | tf_op jit(solution)/shard_map/cond/branch_1_fun/ppermute | solution.py:23
  35.0 11.6 %collective-permute-start.9 = (bf16[128,1024]{1,0:T(8,128)(2,1)}, bf16[128,1024]{1,0:T(8,128)(2,1)}, u32[]{:S(2)}, u32[]{:S(2)}) collective-permute-start(bf16[128,1024]{1,0:T(8,128)(2,1)} %get-tuple-element.93), channel_id=1, source_target_pairs={{0,4},{1,5},{2,6},{3,7},{4,0},{5,1},{6,2},{7,3},{8,12},{9,13},{10,... | collective-permute-start | bytes 786440 | tf_op jit(solution)/shard_map/cond/branch_1_fun/ppermute | solution.py:23
  38.5 6.0 %collective-permute-start.6 = (bf16[1,1,128,256]{3,2,1,0:T(8,128)(2,1)S(1)}, bf16[1,1,128,256]{3,2,1,0:T(8,128)(2,1)}, u32[]{:S(2)}, u32[]{:S(2)}) collective-permute-start(bf16[1,1,128,256]{3,2,1,0:T(8,128)(2,1)S(1)} %fusion), channel_id=1, source_target_pairs={{0,16},{16,0},{1,17},{17,1},{2,18},{18,2},{3,19},{19,3},{4,20},{20... | collective-permute-start | bytes 196616 | tf_op jit(solution)/shard_map/cond/branch_1_fun/ppermute | solution.py:23
  44.5 4.0 %collective-permute-start.8 = (bf16[2,1,128,256]{3,2,1,0:T(8,128)(2,1)S(1)}, bf16[2,1,128,256]{3,2,1,0:T(8,128)(2,1)S(1)}, u32[]{:S(2)}, u32[]{:S(2)}) collective-permute-start(bf16[2,1,128,256]{3,2,1,0:T(8,128)(2,1)S(1)} %pad_maximum_fusion.1), channel_id=1, source_target_pairs={{0,1},{1,0},{2,3},{3,2},{4,5},{5,4},{6,7},{7,6},{8,9},{9,8},{10,11... | collective-permute-start | bytes 393224 | tf_op jit(solution)/shard_map/cond/branch_1_fun/ppermute | solution.py:23
  48.5 0.8 copy-start.9
  49.3 24.8 %collective-permute-start.28 = (bf16[256,1024]{1,0:T(8,128)(2,1)}, bf16[256,1024]{1,0:T(8,128)(2,1)S(1)}, u32[]{:S(2)}, u32[]{:S(2)}) collective-permute-start(bf16[256,1024]{1,0:T(8,128)(2,1)} %get-tuple-element.202), channel_id=1, source_target_pairs={{0,8},{1,9},{2,10},{3,11},{4,12},{5,13},{6,14},{7,15},{8,0},{9,1},... | collective-permute-start | bytes 1572872 | tf_op jit(solution)/shard_map/ppermute | solution.py:23
  52.4 21.8 %collective-permute-start.27 = (bf16[256,1024]{1,0:T(8,128)(2,1)}, bf16[256,1024]{1,0:T(8,128)(2,1)S(1)}, u32[]{:S(2)}, u32[]{:S(2)}) collective-permute-start(bf16[256,1024]{1,0:T(8,128)(2,1)} %get-tuple-element.202), channel_id=1, source_target_pairs={{0,4},{1,5},{2,6},{3,7},{4,0},{5,1},{6,2},{7,3},{8,12},{9,13},{10,... | collective-permute-start | bytes 1572872 | tf_op jit(solution)/shard_map/ppermute | solution.py:23
  54.1 15.7 %collective-permute-start.26 = (bf16[256,1024]{1,0:T(8,128)(2,1)}, bf16[256,1024]{1,0:T(8,128)(2,1)S(1)}, u32[]{:S(2)}, u32[]{:S(2)}) collective-permute-start(bf16[256,1024]{1,0:T(8,128)(2,1)} %get-tuple-element.202), channel_id=1, source_target_pairs={{0,2},{1,3},{2,0},{3,1},{4,6},{5,7},{6,4},{7,5},{8,10},{9,11},{10,... | collective-permute-start | bytes 1572872 | tf_op jit(solution)/shard_map/ppermute | solution.py:23
  55.7 12.6 %collective-permute-start.29 = (bf16[512,512]{1,0:T(8,128)(2,1)}, bf16[512,512]{1,0:T(8,128)(2,1)S(1)}, u32[]{:S(2)}, u32[]{:S(2)}) collective-permute-start(bf16[512,512]{1,0:T(8,128)(2,1)} %get-tuple-element.212), channel_id=1, source_target_pairs={{0,16},{16,0},{1,17},{17,1},{2,18},{18,2},{3,19},{19,3},{4,20},{20... | collective-permute-start | bytes 1572872 | tf_op jit(solution)/shard_map/ppermute | solution.py:23
  56.2 23.9 %copy-start = (bf16[512,1024]{1,0:T(8,128)(2,1)S(1)}, bf16[512,1024]{1,0:T(8,128)(2,1)}, u32[]{:S(2)}) copy-start(bf16[512,1024]{1,0:T(8,128)(2,1)} %refs_13_.3) | copy-start | bytes 3145732
  68.3 23.7 %copy-start.5 = (bf16[512,512]{1,0:T(8,128)(2,1)}, bf16[512,512]{1,0:T(8,128)(2,1)S(1)}, u32[]{:S(2)}) copy-start(bf16[512,512]{1,0:T(8,128)(2,1)S(1)} %collective-permute-done.29) | copy-start | bytes 1572868
  68.3 24.7 %collective-permute-start.30 = (bf16[256,2048]{1,0:T(8,128)(2,1)}, bf16[256,2048]{1,0:T(8,128)(2,1)}, u32[]{:S(2)}, u32[]{:S(2)}) collective-permute-start(bf16[256,2048]{1,0:T(8,128)(2,1)} %get-tuple-element.213), channel_id=1, source_target_pairs={{0,16},{16,0},{1,17},{17,1},{2,18},{18,2},{3,19},{19,3},{4,20},{20... | collective-permute-start | bytes 3145736 | tf_op jit(solution)/shard_map/ppermute | solution.py:23
  69.9 22.2 %copy-start.4 = (bf16[256,1024]{1,0:T(8,128)(2,1)}, bf16[256,1024]{1,0:T(8,128)(2,1)S(1)}, u32[]{:S(2)}) copy-start(bf16[256,1024]{1,0:T(8,128)(2,1)S(1)} %collective-permute-done.26.refs_4_) | copy-start | bytes 1572868
  74.1 17.9 %copy-start.2 = (bf16[256,1024]{1,0:T(8,128)(2,1)}, bf16[256,1024]{1,0:T(8,128)(2,1)S(1)}, u32[]{:S(2)}) copy-start(bf16[256,1024]{1,0:T(8,128)(2,1)S(1)} %collective-permute-done.28.refs_6_) | copy-start | bytes 1572868
  74.3 17.8 %copy-start.3 = (bf16[256,1024]{1,0:T(8,128)(2,1)}, bf16[256,1024]{1,0:T(8,128)(2,1)S(1)}, u32[]{:S(2)}) copy-start(bf16[256,1024]{1,0:T(8,128)(2,1)S(1)} %collective-permute-done.27.refs_5_) | copy-start | bytes 1572868
  74.3 28.0 %collective-permute-start.31 = (bf16[512,512]{1,0:T(8,128)(2,1)}, bf16[512,512]{1,0:T(8,128)(2,1)}, u32[]{:S(2)}, u32[]{:S(2)}) collective-permute-start(bf16[512,512]{1,0:T(8,128)(2,1)} %copy-done.9), channel_id=1, source_target_pairs={{0,2},{1,3},{2,0},{3,1},{4,6},{5,7},{6,4},{7,5},{8,10},{9,11},{10,... | collective-permute-start | bytes 1572872 | tf_op jit(solution)/shard_map/ppermute | solution.py:23
  76.1 26.2 %collective-permute-start.33 = (bf16[256,1024]{1,0:T(8,128)(2,1)}, bf16[256,1024]{1,0:T(8,128)(2,1)}, u32[]{:S(2)}, u32[]{:S(2)}) collective-permute-start(bf16[256,1024]{1,0:T(8,128)(2,1)} %get-tuple-element.221), channel_id=1, source_target_pairs={{0,8},{1,9},{2,10},{3,11},{4,12},{5,13},{6,14},{7,15},{8,0},{9,1},... | collective-permute-start | bytes 1572872 | tf_op jit(solution)/shard_map/ppermute | solution.py:23
  77.8 24.6 %collective-permute-start.32 = (bf16[256,1024]{1,0:T(8,128)(2,1)}, bf16[256,1024]{1,0:T(8,128)(2,1)}, u32[]{:S(2)}, u32[]{:S(2)}) collective-permute-start(bf16[256,1024]{1,0:T(8,128)(2,1)} %get-tuple-element.219), channel_id=1, source_target_pairs={{0,4},{1,5},{2,6},{3,7},{4,0},{5,1},{6,2},{7,3},{8,12},{9,13},{10,... | collective-permute-start | bytes 1572872 | tf_op jit(solution)/shard_map/ppermute | solution.py:23
  80.1 12.9 %copy-start.8 = (f32[256,256]{1,0:T(8,128)S(1)}, f32[256,256]{1,0:T(8,128)}, u32[]{:S(2)}) copy-start(f32[256,256]{1,0:T(8,128)} %get-tuple-element.214) | copy-start | bytes 786436
  92.1 37.1 %collective-permute-start.34 = (bf16[384,2048]{1,0:T(8,128)(2,1)}, bf16[384,2048]{1,0:T(8,128)(2,1)S(1)}, u32[]{:S(2)}, u32[]{:S(2)}) collective-permute-start(bf16[384,2048]{1,0:T(8,128)(2,1)} %get-tuple-element.236), channel_id=1, source_target_pairs={{0,16},{16,0},{1,17},{17,1},{2,18},{18,2},{3,19},{19,3},{4,20},{20... | collective-permute-start | bytes 4718600 | tf_op jit(solution)/shard_map/ppermute | solution.py:23
  93.7 1.9 %collective-permute-start.11 = (f32[256,256]{1,0:T(8,128)}, f32[256,256]{1,0:T(8,128)}, u32[]{:S(2)}, u32[]{:S(2)}) collective-permute-start(f32[256,256]{1,0:T(8,128)} %broadcast_select_fusion), channel_id=1, source_target_pairs={{0,1},{1,0},{2,3},{3,2},{4,5},{5,4},{6,7},{7,6},{8,9},{9,8},{10,11... | collective-permute-start | bytes 786440 | tf_op jit(solution)/shard_map/cond/branch_1_fun/ppermute | solution.py:23
  96.6 5.6 %collective-permute-start.12 = (f32[128,256]{1,0:T(8,128)S(1)}, f32[128,256]{1,0:T(8,128)S(1)}, u32[]{:S(2)}, u32[]{:S(2)}) collective-permute-start(f32[128,256]{1,0:T(8,128)S(1)} %slice_select_fusion.2), channel_id=1, source_target_pairs={{0,2},{1,3},{2,0},{3,1},{4,6},{5,7},{6,4},{7,5},{8,10},{9,11},{10,... | collective-permute-start | bytes 393224 | tf_op jit(solution)/shard_map/cond/branch_1_fun/ppermute | solution.py:23
  102.3 14.6 %collective-permute-start.15 = (bf16[256,1024]{1,0:T(8,128)(2,1)}, bf16[256,1024]{1,0:T(8,128)(2,1)}, u32[]{:S(2)}, u32[]{:S(2)}) collective-permute-start(bf16[256,1024]{1,0:T(8,128)(2,1)} %get-tuple-element.100), channel_id=1, source_target_pairs={{0,1},{1,0},{2,3},{3,2},{4,5},{5,4},{6,7},{7,6},{8,9},{9,8},{10,11... | collective-permute-start | bytes 1572872 | tf_op jit(solution)/shard_map/cond/branch_1_fun/ppermute | solution.py:23
  102.4 14.7 %collective-permute-start.16 = (bf16[256,1024]{1,0:T(8,128)(2,1)}, bf16[256,1024]{1,0:T(8,128)(2,1)}, u32[]{:S(2)}, u32[]{:S(2)}) collective-permute-start(bf16[256,1024]{1,0:T(8,128)(2,1)} %get-tuple-element.101), channel_id=1, source_target_pairs={{0,2},{1,3},{2,0},{3,1},{4,6},{5,7},{6,4},{7,5},{8,10},{9,11},{10,... | collective-permute-start | bytes 1572872 | tf_op jit(solution)/shard_map/cond/branch_1_fun/ppermute | solution.py:23
  103.0 5.6 %collective-permute-start.13 = (f32[128,256]{1,0:T(8,128)S(1)}, f32[128,256]{1,0:T(8,128)S(1)}, u32[]{:S(2)}, u32[]{:S(2)}) collective-permute-start(f32[128,256]{1,0:T(8,128)S(1)} %get-tuple-element.99), channel_id=1, source_target_pairs={{0,4},{1,5},{2,6},{3,7},{4,0},{5,1},{6,2},{7,3},{8,12},{9,13},{10,... | collective-permute-start | bytes 393224 | tf_op jit(solution)/shard_map/cond/branch_1_fun/ppermute | solution.py:23
  108.6 8.4 %collective-permute-start.14 = (f32[128,256]{1,0:T(8,128)S(1)}, f32[128,256]{1,0:T(8,128)S(1)}, u32[]{:S(2)}, u32[]{:S(2)}) collective-permute-start(f32[128,256]{1,0:T(8,128)S(1)} %add.24), channel_id=1, source_target_pairs={{0,8},{1,9},{2,10},{3,11},{4,12},{5,13},{6,14},{7,15},{8,0},{9,1},... | collective-permute-start | bytes 393224 | tf_op jit(solution)/shard_map/cond/branch_1_fun/ppermute | solution.py:23
  117.1 26.5 %collective-permute-start.35 = (bf16[256,1024]{1,0:T(8,128)(2,1)}, bf16[256,1024]{1,0:T(8,128)(2,1)}, u32[]{:S(2)}, u32[]{:S(2)}) collective-permute-start(bf16[256,1024]{1,0:T(8,128)(2,1)} %get-tuple-element.240), channel_id=1, source_target_pairs={{0,4},{1,5},{2,6},{3,7},{4,0},{5,1},{6,2},{7,3},{8,12},{9,13},{10,... | collective-permute-start | bytes 1572872 | tf_op jit(solution)/shard_map/ppermute | solution.py:23
  117.4 26.1 %collective-permute-start.36 = (bf16[256,1024]{1,0:T(8,128)(2,1)}, bf16[256,1024]{1,0:T(8,128)(2,1)}, u32[]{:S(2)}, u32[]{:S(2)}) collective-permute-start(bf16[256,1024]{1,0:T(8,128)(2,1)} %get-tuple-element.243), channel_id=1, source_target_pairs={{0,8},{1,9},{2,10},{3,11},{4,12},{5,13},{6,14},{7,15},{8,0},{9,1},... | collective-permute-start | bytes 1572872 | tf_op jit(solution)/shard_map/ppermute | solution.py:23
  120.7 6.0 %collective-permute-start.18 = (bf16[256,1024]{1,0:T(8,128)(2,1)}, bf16[256,1024]{1,0:T(8,128)(2,1)}, u32[]{:S(2)}, u32[]{:S(2)}) collective-permute-start(bf16[256,1024]{1,0:T(8,128)(2,1)} %get-tuple-element.103), channel_id=1, source_target_pairs={{0,1},{1,0},{2,3},{3,2},{4,5},{5,4},{6,7},{7,6},{8,9},{9,8},{10,11... | collective-permute-start | bytes 1572872 | tf_op jit(solution)/shard_map/cond/branch_1_fun/ppermute | solution.py:23
  120.8 5.9 %collective-permute-start.17 = (bf16[1,2,128,256]{3,2,1,0:T(8,128)(2,1)S(1)}, bf16[1,2,128,256]{3,2,1,0:T(8,128)(2,1)S(1)}, u32[]{:S(2)}, u32[]{:S(2)}) collective-permute-start(bf16[1,2,128,256]{3,2,1,0:T(8,128)(2,1)S(1)} %get-tuple-element.102), channel_id=1, source_target_pairs={{0,2},{1,3},{2,0},{3,1},{4,6},{5,7},{6,4},{7,5},{8,10},{9,11},{10,... | collective-permute-start | bytes 393224 | tf_op jit(solution)/shard_map/cond/branch_1_fun/ppermute | solution.py:23
  126.7 2.4 %collective-permute-start.20 = (bf16[512,512]{1,0:T(8,128)(2,1)}, bf16[512,512]{1,0:T(8,128)(2,1)}, u32[]{:S(2)}, u32[]{:S(2)}) collective-permute-start(bf16[512,512]{1,0:T(8,128)(2,1)} %get-tuple-element.107), channel_id=1, source_target_pairs={{0,1},{1,0},{2,3},{3,2},{4,5},{5,4},{6,7},{7,6},{8,9},{9,8},{10,11... | collective-permute-start | bytes 1572872 | tf_op jit(solution)/shard_map/cond/branch_1_fun/ppermute | solution.py:23
  126.8 2.3 %collective-permute-start.19 = (bf16[2,2,128,256]{3,2,1,0:T(8,128)(2,1)S(1)}, bf16[2,2,128,256]{3,2,1,0:T(8,128)(2,1)S(1)}, u32[]{:S(2)}, u32[]{:S(2)}) collective-permute-start(bf16[2,2,128,256]{3,2,1,0:T(8,128)(2,1)S(1)} %pad_maximum_fusion.3), channel_id=1, source_target_pairs={{0,1},{1,0},{2,3},{3,2},{4,5},{5,4},{6,7},{7,6},{8,9},{9,8},{10,11... | collective-permute-start | bytes 786440 | tf_op jit(solution)/shard_map/cond/branch_1_fun/ppermute | solution.py:23
  129.2 14.3 %collective-permute-start.1 = (bf16[256,1024]{1,0:T(8,128)(2,1)}, bf16[256,1024]{1,0:T(8,128)(2,1)}, u32[]{:S(2)}, u32[]{:S(2)}) collective-permute-start(bf16[256,1024]{1,0:T(8,128)(2,1)} %get-tuple-element.109), channel_id=1, source_target_pairs={{0,2},{1,3},{2,0},{3,1},{4,6},{5,7},{6,4},{7,5},{8,10},{9,11},{10,... | collective-permute-start | bytes 1572872 | tf_op jit(solution)/shard_map/cond/branch_1_fun/ppermute | solution.py:23
  130.8 10.6 %collective-permute-start = (bf16[4,1,128,256]{3,2,1,0:T(8,128)(2,1)S(1)}, bf16[4,1,128,256]{3,2,1,0:T(8,128)(2,1)}, u32[]{:S(2)}, u32[]{:S(2)}) collective-permute-start(bf16[4,1,128,256]{3,2,1,0:T(8,128)(2,1)S(1)} %slice.13), channel_id=1, source_target_pairs={{0,16},{16,0},{1,17},{17,1},{2,18},{18,2},{3,19},{19,3},{4,20},{20... | collective-permute-start | bytes 786440 | tf_op jit(solution)/shard_map/cond/branch_1_fun/ppermute | solution.py:23

commit v5 on v4

--- a/solution.py
+++ b/solution.py
@@ -52,7 +52,7 @@
 
 def forward_body(local_taps, pieces, aliased, packed, idx_ref, *refs):
     take = taken(refs)
-    own = [r[...] for r in take(local_taps)]
+    tokens_ref = take(1)[0]
     remote_refs = [take(n) for n in pieces]
     remote = [rows_of(r) for r in remote_refs]
     remote_refs = [r[0] for r in remote_refs]
@@ -64,6 +64,8 @@
     local_ref, latent_term_ref = take(2)
     group = pl.program_id(0)
     taps, block, hidden = weight_ref.shape
+    flips = [group if k == 0 else group ^ (1 << (k - 1)) for k in range(local_taps)]
+    own = [tokens_ref[:, pl.ds(pl.multiple_of(j * block, block), block)] for j in flips]
     weights = weight_ref[...].reshape(taps * block, hidden)
     right = right_ref[...]
     preact = jnp.dot(jnp.concatenate(own + remote, axis=1), weights, preferred_element_type=f32)
@@ -107,14 +109,11 @@
     local_taps = taps - len(remote)
     quarter, rank = latent.shape[2:]
     height = packed * rows * (block // 2) // hidden
-    own_spec = lambda k: pl.BlockSpec(
-        (rows, block), lambda g, idx: (chunk, g if k == 0 else g ^ (1 << (k - 1)))
-    )
     piece_spec = lambda piece: pl.BlockSpec((piece[2], block), lambda g, idx: (piece[1], g))
     latent_spec = lambda k: pl.BlockSpec(
         (1, None, quarter, rank), lambda g, idx: (idx[0] ^ k, 0, 0, 0)
     )
-    in_specs = [own_spec(k) for k in range(local_taps)]
+    in_specs = [pl.BlockSpec((rows, width), lambda g, idx: (chunk, 0))]
     in_specs += [piece_spec(p) for tap in remote for p in tap]
     in_specs += [latent_spec(2 * chunk), latent_spec(2 * chunk + 1)]
     in_specs += [
@@ -122,7 +121,7 @@
         pl.BlockSpec((rank, hidden), lambda g, idx: (0, g)),
         pl.BlockSpec((rows, hidden), lambda g, idx: (chunk, g)),
     ]
-    args = [tokens] * local_taps + [p[0] for tap in remote for p in tap]
+    args = [tokens] + [p[0] for tap in remote for p in tap]
     args += [latent, latent, weight, right, cotangent]
     aliases = {}
     if act_before is not None:

time: 149 us -> 149 us (level)
  transfers between devices with their start and end apart: 37 -> 37, of which waited for: 19 -> 18; matrix products, arithmetic and copies ran while one was open for 4% -> 4% of each run, Pallas kernels for 26% -> 26%
where the time goes in v5:
time: 149 us
  waiting for transfers between devices  51.3 us (34%)
  starting transfers between devices  45.3 us (30%)
  Pallas kernels  43.9 us (29%)
  local copies, waits for them, and re-layouts  3.39 us (2%)
  other arithmetic  2.17 us (1%)
  matrix products  1.88 us (1%)
    ppermute x37, waiting for transfers between devices, from_partner(): lax.ppermute(shard, axis, [(i, i ^ 1 << distance) for i in range(lax.axis...  51.3 us
    ppermute x37, starting transfers between devices, from_partner(): lax.ppermute(shard, axis, [(i, i ^ 1 << distance) for i in range(lax.axis...  45.3 us
    pallas_call x2, Pallas kernels, forward_chunk(): pl.pallas_call(functools.partial(forward_body, local_taps, [len(t) for t...  24.4 us
    pallas_call x1, Pallas kernels, weight_grads(): pl.pallas_call(functools.partial(weights_body, local_taps, [len(t) for t...  9.97 us
    pallas_call x1, Pallas kernels, input_grads(): pl.pallas_call(functools.partial(inputs_body, len(terms)), grid_spec=pltp...  5.37 us
    pallas_call x2, Pallas kernels, column_halves(): pl.pallas_call(functools.partial(halves_body, block), in_specs=[pl.BlockS...  3.32 us
  transfers between devices with their start and end apart: 37, of which 18 were waited for; matrix products, arithmetic and copies ran while one was open for 4% of the time, Pallas kernels for 26%

profile of v5, /device:TPU:0, one launch (start us, length us, event | category | flops | bytes accessed | tf_op | source)
XLA Modules:
  0.0 148.9 jit_solution(4409729667566514659)
XLA Ops:
  0.6 1.0 slice.15
  1.6 4.1 %collective-permute-start.25 = (bf16[128,1024]{1,0:T(8,128)(2,1)S(1)}, bf16[128,1024]{1,0:T(8,128)(2,1)S(1)}, u32[]{:S(2)}, u32[]{:S(2)}) collective-permute-start(bf16[128,1024]{1,0:T(8,128)(2,1)S(1)} %slice.15), channel_id=1, source_target_pairs={{0,8},{1,9},{2,10},{3,11},{4,12},{5,13},{6,14},{7,15},{8,0},{9,1},... | collective-permute-start | bytes 786440 | tf_op jit(solution)/shard_map/ppermute | solution.py:23
  5.7 1.6 %collective-permute-start.24 = (bf16[128,1024]{1,0:T(8,128)(2,1)S(1)}, bf16[128,1024]{1,0:T(8,128)(2,1)S(1)}, u32[]{:S(2)}, u32[]{:S(2)}) collective-permute-start(bf16[128,1024]{1,0:T(8,128)(2,1)S(1)} %slice.15), channel_id=1, source_target_pairs={{0,4},{1,5},{2,6},{3,7},{4,0},{5,1},{6,2},{7,3},{8,12},{9,13},{10,... | collective-permute-start | bytes 786440 | tf_op jit(solution)/shard_map/ppermute | solution.py:23
  7.3 9.7 %conditional.6 = (f32[128,256]{1,0:T(8,128)S(1)}, bf16[512,1024]{1,0:T(8,128)(2,1)}, bf16[256,1024]{1,0:T(8,128)(2,1)S(1)}, bf16[128,1024]{1,0:T(8,128)(2,1)}, bf16[256,1024]{1,0:T(8,128)(2,1)}) conditional(s32[]{:T(128)} %convert_element_type.8, () %tuple.70, (bf16[512,1024]{1,0:T(8,128)(2,1)}, bf16[1024,256]{1,0:T(8,128)(2,1)}) %tuple.71), branch_computations={%region_0.0_spmd, %region_1.2_spmd} | conditional | flops 268730368 | bytes 17432854 | solution.py:365
  7.3 1.9 %fusion.3 = f32[512,256]{1,0:T(8,128)S(1)} fusion(bf16[512,1024]{1,0:T(8,128)(2,1)} %get-tuple-element.85, bf16[1024,256]{1,0:T(8,128)(2,1)} %get-tuple-element.84), kind=kOutput, calls=%fused_computation.18 | convolution fusion | flops 268435456 | bytes 2097152 | tf_op jit(solution)/shard_map/cond/branch_1_fun/dot_general | solution.py:414
  9.3 1.5 %collective-permute-done.21 = f32[256,256]{1,0:T(8,128)S(1)} collective-permute-done((f32[256,256]{1,0:T(8,128)S(1)}, f32[256,256]{1,0:T(8,128)S(1)}, u32[]{:S(2)}, u32[]{:S(2)}) %collective-permute-start.21) | collective-permute-done | bytes 262176 | tf_op jit(solution)/shard_map/cond/branch_1_fun/ppermute | solution.py:23
  11.1 1.6 %collective-permute-start.22 = (f32[128,256]{1,0:T(8,128)S(1)}, f32[128,256]{1,0:T(8,128)S(1)}, u32[]{:S(2)}, u32[]{:S(2)}) collective-permute-start(f32[128,256]{1,0:T(8,128)S(1)} %slice_select_fusion.1), channel_id=1, source_target_pairs={{0,2},{1,3},{2,0},{3,1},{4,6},{5,7},{6,4},{7,5},{8,10},{9,11},{10,... | collective-permute-start | bytes 393224 | tf_op jit(solution)/shard_map/cond/branch_1_fun/ppermute | solution.py:23
  14.3 2.7 %collective-permute-done.22 = f32[128,256]{1,0:T(8,128)S(1)} collective-permute-done((f32[128,256]{1,0:T(8,128)S(1)}, f32[128,256]{1,0:T(8,128)S(1)}, u32[]{:S(2)}, u32[]{:S(2)}) %collective-permute-start.22) | collective-permute-done | bytes 131104 | tf_op jit(solution)/shard_map/cond/branch_1_fun/ppermute | solution.py:23
  17.9 30.6 %conditional.7 = (bf16[4,1,128,256]{3,2,1,0:T(8,128)(2,1)S(1)}, bf16[1,1,128,256]{3,2,1,0:T(8,128)(2,1)}, bf16[512,1024]{1,0:T(8,128)(2,1)}, bf16[512,512]{1,0:T...) conditional(s32[]{:T(128)} %convert_element_type.8, () %tuple.72, ...), branch_computations={%region_2.3_spmd, %region_3.4_spmd} | conditional | flops 425985 | bytes 12124596 | solution.py:365
  17.9 1.5 %collective-permute-start.7 = (bf16[512,1024]{1,0:T(8,128)(2,1)}, bf16[512,1024]{1,0:T(8,128)(2,1)}, u32[]{:S(2)}, u32[]{:S(2)}) collective-permute-start(bf16[512,1024]{1,0:T(8,128)(2,1)} %get-tuple-element.90), channel_id=1, source_target_pairs={{0,16},{16,0},{1,17},{17,1},{2,18},{18,2},{3,19},{19,3},{4,20},{20... | collective-permute-start | bytes 3145736 | tf_op jit(solution)/shard_map/cond/branch_1_fun/ppermute | solution.py:23
  19.5 1.5 %collective-permute-start.4 = (bf16[256,1024]{1,0:T(8,128)(2,1)S(1)}, bf16[256,1024]{1,0:T(8,128)(2,1)}, u32[]{:S(2)}, u32[]{:S(2)}) collective-permute-start(bf16[256,1024]{1,0:T(8,128)(2,1)S(1)} %get-tuple-element.87), channel_id=1, source_target_pairs={{0,2},{1,3},{2,0},{3,1},{4,6},{5,7},{6,4},{7,5},{8,10},{9,11},{10,... | collective-permute-start | bytes 1572872 | tf_op jit(solution)/shard_map/cond/branch_1_fun/ppermute | solution.py:23
  21.0 1.4 collective-permute-start.2
  22.4 3.5 %collective-permute-done.2 = f32[128,256]{1,0:T(8,128)S(1)} collective-permute-done((f32[128,256]{1,0:T(8,128)S(1)}, f32[128,256]{1,0:T(8,128)S(1)}, u32[]{:S(2)}, u32[]{:S(2)}) %collective-permute-start.2) | collective-permute-done | bytes 131104 | tf_op jit(solution)/shard_map/cond/branch_1_fun/ppermute | solution.py:23
  26.0 2.0 %collective-permute-start.3 = (f32[128,256]{1,0:T(8,128)S(1)}, f32[128,256]{1,0:T(8,128)S(1)}, u32[]{:S(2)}, u32[]{:S(2)}) collective-permute-start(f32[128,256]{1,0:T(8,128)S(1)} %add.20), channel_id=1, source_target_pairs={{0,8},{1,9},{2,10},{3,11},{4,12},{5,13},{6,14},{7,15},{8,0},{9,1},... | collective-permute-start | bytes 393224 | tf_op jit(solution)/shard_map/cond/branch_1_fun/ppermute | solution.py:23
  28.0 5.4 %collective-permute-done.3 = f32[128,256]{1,0:T(8,128)S(1)} collective-permute-done((f32[128,256]{1,0:T(8,128)S(1)}, f32[128,256]{1,0:T(8,128)S(1)}, u32[]{:S(2)}, u32[]{:S(2)}) %collective-permute-start.3) | collective-permute-done | bytes 131104 | tf_op jit(solution)/shard_map/cond/branch_1_fun/ppermute | solution.py:23
  35.0 3.5 %collective-permute-start.9 = (bf16[128,1024]{1,0:T(8,128)(2,1)}, bf16[128,1024]{1,0:T(8,128)(2,1)}, u32[]{:S(2)}, u32[]{:S(2)}) collective-permute-start(bf16[128,1024]{1,0:T(8,128)(2,1)} %get-tuple-element.93), channel_id=1, source_target_pairs={{0,4},{1,5},{2,6},{3,7},{4,0},{5,1},{6,2},{7,3},{8,12},{9,13},{10,... | collective-permute-start | bytes 786440 | tf_op jit(solution)/shard_map/cond/branch_1_fun/ppermute | solution.py:23
  39.0 4.1 %collective-permute-done.7.refs_0_ = bf16[512,1024]{1,0:T(8,128)(2,1)} collective-permute-done((bf16[512,1024]{1,0:T(8,128)(2,1)}, bf16[512,1024]{1,0:T(8,128)(2,1)}, u32[]{:S(2)}, u32[]{:S(2)}) %collective-permute-start.7) | collective-permute-done | bytes 1048608 | tf_op jit(solution)/shard_map/cond/branch_1_fun/ppermute | solution.py:23
  43.1 1.4 column_halves.2
  44.6 1.8 %collective-permute-done.10.refs_3_ = bf16[128,1024]{1,0:T(8,128)(2,1)} collective-permute-done((bf16[128,1024]{1,0:T(8,128)(2,1)}, bf16[128,1024]{1,0:T(8,128)(2,1)}, u32[]{:S(2)}, u32[]{:S(2)}) %collective-permute-start.10) | collective-permute-done | bytes 262176 | tf_op jit(solution)/shard_map/cond/branch_1_fun/ppermute | solution.py:23
  46.5 2.0 %column_halves.3 = bf16[512,512]{1,0:T(8,128)(2,1)} custom-call(s32[1]{0:T(128)S(6)} %sub.4.which, bf16[128,1024]{1,0:T(8,128)(2,1)S(1)} %get-tuple-element.95.refs_0_, bf16[128,1024]{1,0:T(8,128)(2,1)} %collective-permute-done.9.refs_1_, bf16[128,1024]{1,0:T(8,128)(2,1)S(1)} %get-tuple-element.96.refs_2_, bf16[128,1024]{1,0:T(8,128)(2,1)} %collective-permute-done.10.refs_3_), custom_call_target="tpu_custom_call" | custom-call | bytes 65536 | tf_op jit(solution)/shard_map/cond/branch_1_fun/column_halves/pallas_call | solution.py:179
  49.3 3.1 %collective-permute-start.28 = (bf16[256,1024]{1,0:T(8,128)(2,1)}, bf16[256,1024]{1,0:T(8,128)(2,1)S(1)}, u32[]{:S(2)}, u32[]{:S(2)}) collective-permute-start(bf16[256,1024]{1,0:T(8,128)(2,1)} %get-tuple-element.202), channel_id=1, source_target_pairs={{0,8},{1,9},{2,10},{3,11},{4,12},{5,13},{6,14},{7,15},{8,0},{9,1},... | collective-permute-start | bytes 1572872 | tf_op jit(solution)/shard_map/ppermute | solution.py:23
  52.4 1.7 %collective-permute-start.27 = (bf16[256,1024]{1,0:T(8,128)(2,1)}, bf16[256,1024]{1,0:T(8,128)(2,1)S(1)}, u32[]{:S(2)}, u32[]{:S(2)}) collective-permute-start(bf16[256,1024]{1,0:T(8,128)(2,1)} %get-tuple-element.202), channel_id=1, source_target_pairs={{0,4},{1,5},{2,6},{3,7},{4,0},{5,1},{6,2},{7,3},{8,12},{9,13},{10,... | collective-permute-start | bytes 1572872 | tf_op jit(solution)/shard_map/ppermute | solution.py:23
  54.1 1.5 %collective-permute-start.26 = (bf16[256,1024]{1,0:T(8,128)(2,1)}, bf16[256,1024]{1,0:T(8,128)(2,1)S(1)}, u32[]{:S(2)}, u32[]{:S(2)}) collective-permute-start(bf16[256,1024]{1,0:T(8,128)(2,1)} %get-tuple-element.202), channel_id=1, source_target_pairs={{0,2},{1,3},{2,0},{3,1},{4,6},{5,7},{6,4},{7,5},{8,10},{9,11},{10,... | collective-permute-start | bytes 1572872 | tf_op jit(solution)/shard_map/ppermute | solution.py:23
  56.2 12.7 %forward_chunk.2 = (bf16[512,2048]{1,0:T(8,128)(2,1)}, bf16[256,2048]{1,0:T(8,128)(2,1)}, bf16[256,1024]{1,0:T(8,128)(2,1)}, bf16[256,1024]{1,0:T(8,128)(2,1)}, ...) custom-call(s32[2]{0:T(128)S(1)} %pad_add_fusion.idx_ref, ...), custom_call_target="tpu_custom_call" | custom-call | flops 17179869184 | bytes 71303168 | tf_op jit(solution)/shard_map/forward_chunk/pallas_call | solution.py:144
  68.9 1.6 %collective-permute-start.30 = (bf16[256,2048]{1,0:T(8,128)(2,1)}, bf16[256,2048]{1,0:T(8,128)(2,1)}, u32[]{:S(2)}, u32[]{:S(2)}) collective-permute-start(bf16[256,2048]{1,0:T(8,128)(2,1)} %get-tuple-element.213), channel_id=1, source_target_pairs={{0,16},{16,0},{1,17},{17,1},{2,18},{18,2},{3,19},{19,3},{4,20},{20... | collective-permute-start | bytes 3145736 | tf_op jit(solution)/shard_map/ppermute | solution.py:23
  70.5 3.7 %collective-permute-done.28.refs_4_ = bf16[256,1024]{1,0:T(8,128)(2,1)S(1)} collective-permute-done((bf16[256,1024]{1,0:T(8,128)(2,1)}, bf16[256,1024]{1,0:T(8,128)(2,1)S(1)}, u32[]{:S(2)}, u32[]{:S(2)}) %collective-permute-start.28) | collective-permute-done | bytes 524320 | tf_op jit(solution)/shard_map/ppermute | solution.py:23
  74.3 1.9 %collective-permute-start.31 = (bf16[512,512]{1,0:T(8,128)(2,1)}, bf16[512,512]{1,0:T(8,128)(2,1)}, u32[]{:S(2)}, u32[]{:S(2)}) collective-permute-start(bf16[512,512]{1,0:T(8,128)(2,1)} %copy-done.9), channel_id=1, source_target_pairs={{0,2},{1,3},{2,0},{3,1},{4,6},{5,7},{6,4},{7,5},{8,10},{9,11},{10,... | collective-permute-start | bytes 1572872 | tf_op jit(solution)/shard_map/ppermute | solution.py:23
  76.1 1.6 %collective-permute-start.33 = (bf16[256,1024]{1,0:T(8,128)(2,1)}, bf16[256,1024]{1,0:T(8,128)(2,1)}, u32[]{:S(2)}, u32[]{:S(2)}) collective-permute-start(bf16[256,1024]{1,0:T(8,128)(2,1)} %get-tuple-element.221), channel_id=1, source_target_pairs={{0,8},{1,9},{2,10},{3,11},{4,12},{5,13},{6,14},{7,15},{8,0},{9,1},... | collective-permute-start | bytes 1572872 | tf_op jit(solution)/shard_map/ppermute | solution.py:23
  77.8 2.3 %collective-permute-start.32 = (bf16[256,1024]{1,0:T(8,128)(2,1)}, bf16[256,1024]{1,0:T(8,128)(2,1)}, u32[]{:S(2)}, u32[]{:S(2)}) collective-permute-start(bf16[256,1024]{1,0:T(8,128)(2,1)} %get-tuple-element.219), channel_id=1, source_target_pairs={{0,4},{1,5},{2,6},{3,7},{4,0},{5,1},{6,2},{7,3},{8,12},{9,13},{10,... | collective-permute-start | bytes 1572872 | tf_op jit(solution)/shard_map/ppermute | solution.py:23
  80.1 11.7 %forward_chunk.3 = (bf16[512,2048]{1,0:T(8,128)(2,1)}, bf16[384,2048]{1,0:T(8,128)(2,1)}, bf16[256,1024]{1,0:T(8,128)(2,1)}, bf16[256,1024]{1,0:T(8,128)(2,1)}, ...) custom-call(s32[2]{0:T(128)S(1)} %pad_add_fusion.idx_ref, ...), custom_call_target="tpu_custom_call", output_to_operand_aliasing={{0}: (11, {})} | custom-call | flops 4294967296 | bytes 17825792 | tf_op jit(solution)/shard_map/forward_chunk/pallas_call | solution.py:144
  92.8 9.3 %conditional.8 = (f32[128,256]{1,0:T(8,128)S(1)}) conditional(s32[]{:T(128)} %convert_element_type.8, () %tuple.77, (f32[256,256]{1,0:T(8,128)S(1)}, f32[256,256]{1,0:T(8,128)S(1)}) %tuple.114), branch_computations={%region_4.5_spmd, %region_5.6_spmd} | conditional | flops 294920 | bytes 4325554 | solution.py:365
  93.5 1.9 %collective-permute-done.11 = f32[256,256]{1,0:T(8,128)} collective-permute-done((f32[256,256]{1,0:T(8,128)}, f32[256,256]{1,0:T(8,128)}, u32[]{:S(2)}, u32[]{:S(2)}) %collective-permute-start.11) | collective-permute-done | bytes 262176 | tf_op jit(solution)/shard_map/cond/branch_1_fun/ppermute | solution.py:23
  95.4 1.0 select_add_fusion.2
  97.0 5.0 %collective-permute-done.12 = f32[128,256]{1,0:T(8,128)S(1)} collective-permute-done((f32[128,256]{1,0:T(8,128)S(1)}, f32[128,256]{1,0:T(8,128)S(1)}, u32[]{:S(2)}, u32[]{:S(2)}) %collective-permute-start.12) | collective-permute-done | bytes 131104 | tf_op jit(solution)/shard_map/cond/branch_1_fun/ppermute | solution.py:23
  102.1 14.7 %conditional.9 = (bf16[1,1,128,256]{3,2,1,0:T(8,128)(2,1)S(1)}, bf16[256,1024]{1,0:T(8,128)(2,1)}, bf16[256,1024]{1,0:T(8,128)(2,1)}) conditional(s32[]{:T(128)} %convert_element_type.8, () %tuple.76, (f32[128,256]{1,0:T(8,128)S(1)}, bf16[256,1024]{1,0:T(8,128)(2,1)}, bf16[256,1024]{1,0:T(8,128)(2,1)}) %tuple.85), branch_computations={%region_6.7_spmd, %region_7.8_spmd} | conditional | flops 98304 | bytes 5963960 | solution.py:365
  103.1 5.2 %collective-permute-done.13 = f32[128,256]{1,0:T(8,128)S(1)} collective-permute-done((f32[128,256]{1,0:T(8,128)S(1)}, f32[128,256]{1,0:T(8,128)S(1)}, u32[]{:S(2)}, u32[]{:S(2)}) %collective-permute-start.13) | collective-permute-done | bytes 131104 | tf_op jit(solution)/shard_map/cond/branch_1_fun/ppermute | solution.py:23
  108.4 1.3 collective-permute-start.14
  109.6 7.2 %collective-permute-done.14 = f32[128,256]{1,0:T(8,128)S(1)} collective-permute-done((f32[128,256]{1,0:T(8,128)S(1)}, f32[128,256]{1,0:T(8,128)S(1)}, u32[]{:S(2)}, u32[]{:S(2)}) %collective-permute-start.14) | collective-permute-done | bytes 131104 | tf_op jit(solution)/shard_map/cond/branch_1_fun/ppermute | solution.py:23
  117.2 2.7 %collective-permute-start.36 = (bf16[256,1024]{1,0:T(8,128)(2,1)}, bf16[256,1024]{1,0:T(8,128)(2,1)}, u32[]{:S(2)}, u32[]{:S(2)}) collective-permute-start(bf16[256,1024]{1,0:T(8,128)(2,1)} %get-tuple-element.243), channel_id=1, source_target_pairs={{0,8},{1,9},{2,10},{3,11},{4,12},{5,13},{6,14},{7,15},{8,0},{9,1},... | collective-permute-start | bytes 1572872 | tf_op jit(solution)/shard_map/ppermute | solution.py:23
  120.7 8.4 %conditional.10 = (bf16[4,2,128,256]{3,2,1,0:T(8,128)(2,1)S(1)}, bf16[256,1024]{1,0:T(8,128)(2,1)}, bf16[512,512]{1,0:T(8,128)(2,1)}) conditional(s32[]{:T(128)} %convert_element_type.8, () %tuple.86, (bf16[1,2,128,256]{3,2,1,0:T(8,128)(2,1)S(1)}, bf16[256,1024]{1,0:T(8,128)(2,1)}, bf16[512,512]{1,0:T(8,128)(2,1)}) %tuple.115), branch_computations={%region_8.9_spmd, %region_9.10_spmd} | conditional | flops 393216 | bytes 7340216 | solution.py:365
  120.8 1.6 %collective-permute-start.17 = (bf16[1,2,128,256]{3,2,1,0:T(8,128)(2,1)S(1)}, bf16[1,2,128,256]{3,2,1,0:T(8,128)(2,1)S(1)}, u32[]{:S(2)}, u32[]{:S(2)}) collective-permute-start(bf16[1,2,128,256]{3,2,1,0:T(8,128)(2,1)S(1)} %get-tuple-element.102), channel_id=1, source_target_pairs={{0,2},{1,3},{2,0},{3,1},{4,6},{5,7},{6,4},{7,5},{8,10},{9,11},{10,... | collective-permute-start | bytes 393224 | tf_op jit(solution)/shard_map/cond/branch_1_fun/ppermute | solution.py:23
  122.4 4.3 %collective-permute-done.17 = bf16[1,2,128,256]{3,2,1,0:T(8,128)(2,1)S(1)} collective-permute-done((bf16[1,2,128,256]{3,2,1,0:T(8,128)(2,1)S(1)}, bf16[1,2,128,256]{3,2,1,0:T(8,128)(2,1)S(1)}, u32[]{:S(2)}, u32[]{:S(2)}) %collective-permute-start.17) | collective-permute-done | bytes 131104 | tf_op jit(solution)/shard_map/cond/branch_1_fun/ppermute | solution.py:23
  127.3 1.8 %collective-permute-done.19 = bf16[2,2,128,256]{3,2,1,0:T(8,128)(2,1)S(1)} collective-permute-done((bf16[2,2,128,256]{3,2,1,0:T(8,128)(2,1)S(1)}, bf16[2,2,128,256]{3,2,1,0:T(8,128)(2,1)S(1)}, u32[]{:S(2)}, u32[]{:S(2)}) %collective-permute-start.19) | collective-permute-done | bytes 262176 | tf_op jit(solution)/shard_map/cond/branch_1_fun/ppermute | solution.py:23
  129.2 14.4 %conditional.11 = (bf16[4,1,128,256]{3,2,1,0:T(8,128)(2,1)}, bf16[256,1024]{1,0:T(8,128)(2,1)}, bf16[7,128,2048]{2,1,0:T(8,128)(2,1)}, bf16[256,2048]{1,0:T(8,128)(2,1)}) conditional(s32[]{:T(128)} %convert_element_type.8, () %tuple.88, (bf16[4,2,128,256]{3,2,1,0:T(8,128)(2,1)S(1)}, bf16[256,1024]{1,0:T(8,128)(2,1)}, s32[2]{0:T(128)S(1)}, ...), branch_computations={%region_10.11_spmd, %region_11.12_spmd} | conditional | flops 301989888 | bytes 5505064 | solution.py:365
  129.2 1.6 %collective-permute-start.1 = (bf16[256,1024]{1,0:T(8,128)(2,1)}, bf16[256,1024]{1,0:T(8,128)(2,1)}, u32[]{:S(2)}, u32[]{:S(2)}) collective-permute-start(bf16[256,1024]{1,0:T(8,128)(2,1)} %get-tuple-element.109), channel_id=1, source_target_pairs={{0,2},{1,3},{2,0},{3,1},{4,6},{5,7},{6,4},{7,5},{8,10},{9,11},{10,... | collective-permute-start | bytes 1572872 | tf_op jit(solution)/shard_map/cond/branch_1_fun/ppermute | solution.py:23
  131.5 10.0 %weight_grads.1 = (bf16[7,128,2048]{2,1,0:T(8,128)(2,1)}, bf16[256,2048]{1,0:T(8,128)(2,1)}) custom-call(s32[2]{0:T(128)S(1)} %get-tuple-element.110.idx_ref, bf16[512,1024]{1,0:T(8,128)(2,1)S(1)} %get-tuple-element.111.refs_0_.refs_1_.refs_2_, bf16[512,1024]{1,0:T(8,128)(2,1)S(1)} %get-tuple-element.111.refs_0_.refs_1_.refs_2_, ...), custom_call_target="tpu_custom_call" | custom-call | flops 301989888 | bytes 917504 | tf_op jit(solution)/shard_map/cond/branch_1_fun/weight_grads/pallas_call | solution.py:242
  141.5 2.0 %collective-permute-done.1 = bf16[256,1024]{1,0:T(8,128)(2,1)} collective-permute-done((bf16[256,1024]{1,0:T(8,128)(2,1)}, bf16[256,1024]{1,0:T(8,128)(2,1)}, u32[]{:S(2)}, u32[]{:S(2)}) %collective-permute-start.1) | collective-permute-done | bytes 524320 | tf_op jit(solution)/shard_map/cond/branch_1_fun/ppermute | solution.py:23
  143.5 5.4 %input_grads.1 = (bf16[512,1024]{1,0:T(8,128)(2,1)}, bf16[1024,256]{1,0:T(8,128)(2,1)}) custom-call(s32[2]{0:T(128)S(1)} %pad_add_fusion.idx_ref, f32[256,1024]{1,0:T(8,128)} %get-tuple-element.208.refs_0_, f32[256,1024]{1,0:T(8,128)} %get-tuple-element.209.refs_1_, bf16[256,1024]{1,0:T(8,128)(2,1)} %get-tuple-element.225.refs_2_, ...), custom_call_target="tpu_custom_call" | custom-call | flops 50331648 | bytes 655360 | tf_op jit(solution)/shard_map/input_grads/pallas_call | solution.py:329
  (81 shorter events, 12.7 us)
Async XLA Ops:
  1.6 16.1 %collective-permute-start.25 = (bf16[128,1024]{1,0:T(8,128)(2,1)S(1)}, bf16[128,1024]{1,0:T(8,128)(2,1)S(1)}, u32[]{:S(2)}, u32[]{:S(2)}) collective-permute-start(bf16[128,1024]{1,0:T(8,128)(2,1)S(1)} %slice.15), channel_id=1, source_target_pairs={{0,8},{1,9},{2,10},{3,11},{4,12},{5,13},{6,14},{7,15},{8,0},{9,1},... | collective-permute-start | bytes 786440 | tf_op jit(solution)/shard_map/ppermute | solution.py:23
  5.7 12.2 %collective-permute-start.24 = (bf16[128,1024]{1,0:T(8,128)(2,1)S(1)}, bf16[128,1024]{1,0:T(8,128)(2,1)S(1)}, u32[]{:S(2)}, u32[]{:S(2)}) collective-permute-start(bf16[128,1024]{1,0:T(8,128)(2,1)S(1)} %slice.15), channel_id=1, source_target_pairs={{0,4},{1,5},{2,6},{3,7},{4,0},{5,1},{6,2},{7,3},{8,12},{9,13},{10,... | collective-permute-start | bytes 786440 | tf_op jit(solution)/shard_map/ppermute | solution.py:23
  7.3 3.6 %copy-start.1 = (bf16[512,1024]{1,0:T(8,128)(2,1)S(1)}, bf16[512,1024]{1,0:T(8,128)(2,1)}, u32[]{:S(2)}) copy-start(bf16[512,1024]{1,0:T(8,128)(2,1)} %get-tuple-element.85) | copy-start | bytes 3145732 | tf_op jit(solution)/shard_map/cond
  9.2 1.6 %collective-permute-start.21 = (f32[256,256]{1,0:T(8,128)S(1)}, f32[256,256]{1,0:T(8,128)S(1)}, u32[]{:S(2)}, u32[]{:S(2)}) collective-permute-start(f32[256,256]{1,0:T(8,128)S(1)} %slice_select_fusion), channel_id=1, source_target_pairs={{0,1},{1,0},{2,3},{3,2},{4,5},{5,4},{6,7},{7,6},{8,9},{9,8},{10,11... | collective-permute-start | bytes 786440 | tf_op jit(solution)/shard_map/cond/branch_1_fun/ppermute | solution.py:23
  10.9 6.1 %collective-permute-start.23 = (bf16[512,1024]{1,0:T(8,128)(2,1)S(1)}, bf16[512,1024]{1,0:T(8,128)(2,1)}, u32[]{:S(2)}, u32[]{:S(2)}) collective-permute-start(bf16[512,1024]{1,0:T(8,128)(2,1)S(1)} %copy-done.1), channel_id=1, source_target_pairs={{0,1},{1,0},{2,3},{3,2},{4,5},{5,4},{6,7},{7,6},{8,9},{9,8},{10,11... | collective-permute-start | bytes 3145736 | tf_op jit(solution)/shard_map/cond/branch_1_fun/ppermute | solution.py:23
  11.1 5.8 %collective-permute-start.22 = (f32[128,256]{1,0:T(8,128)S(1)}, f32[128,256]{1,0:T(8,128)S(1)}, u32[]{:S(2)}, u32[]{:S(2)}) collective-permute-start(f32[128,256]{1,0:T(8,128)S(1)} %slice_select_fusion.1), channel_id=1, source_target_pairs={{0,2},{1,3},{2,0},{3,1},{4,6},{5,7},{6,4},{7,5},{8,10},{9,11},{10,... | collective-permute-start | bytes 393224 | tf_op jit(solution)/shard_map/cond/branch_1_fun/ppermute | solution.py:23
  17.7 38.5 %copy-start.6 = (bf16[128,1024]{1,0:T(8,128)(2,1)}, bf16[128,1024]{1,0:T(8,128)(2,1)S(1)}, u32[]{:S(2)}) copy-start(bf16[128,1024]{1,0:T(8,128)(2,1)S(1)} %collective-permute-done.25.refs_5_) | copy-start | bytes 786436
  17.9 38.3 %copy-start.7 = (bf16[128,1024]{1,0:T(8,128)(2,1)}, bf16[128,1024]{1,0:T(8,128)(2,1)S(1)}, u32[]{:S(2)}) copy-start(bf16[128,1024]{1,0:T(8,128)(2,1)S(1)} %collective-permute-done.24.refs_3_) | copy-start | bytes 786436
  17.9 25.2 %collective-permute-start.7 = (bf16[512,1024]{1,0:T(8,128)(2,1)}, bf16[512,1024]{1,0:T(8,128)(2,1)}, u32[]{:S(2)}, u32[]{:S(2)}) collective-permute-start(bf16[512,1024]{1,0:T(8,128)(2,1)} %get-tuple-element.90), channel_id=1, source_target_pairs={{0,16},{16,0},{1,17},{17,1},{2,18},{18,2},{3,19},{19,3},{4,20},{20... | collective-permute-start | bytes 3145736 | tf_op jit(solution)/shard_map/cond/branch_1_fun/ppermute | solution.py:23
  19.5 14.0 %collective-permute-start.4 = (bf16[256,1024]{1,0:T(8,128)(2,1)S(1)}, bf16[256,1024]{1,0:T(8,128)(2,1)}, u32[]{:S(2)}, u32[]{:S(2)}) collective-permute-start(bf16[256,1024]{1,0:T(8,128)(2,1)S(1)} %get-tuple-element.87), channel_id=1, source_target_pairs={{0,2},{1,3},{2,0},{3,1},{4,6},{5,7},{6,4},{7,5},{8,10},{9,11},{10,... | collective-permute-start | bytes 1572872 | tf_op jit(solution)/shard_map/cond/branch_1_fun/ppermute | solution.py:23
  21.0 5.0 %collective-permute-start.2 = (f32[128,256]{1,0:T(8,128)S(1)}, f32[128,256]{1,0:T(8,128)S(1)}, u32[]{:S(2)}, u32[]{:S(2)}) collective-permute-start(f32[128,256]{1,0:T(8,128)S(1)} %get-tuple-element.86), channel_id=1, source_target_pairs={{0,4},{1,5},{2,6},{3,7},{4,0},{5,1},{6,2},{7,3},{8,12},{9,13},{10,... | collective-permute-start | bytes 393224 | tf_op jit(solution)/shard_map/cond/branch_1_fun/ppermute | solution.py:23
  26.0 7.5 %collective-permute-start.3 = (f32[128,256]{1,0:T(8,128)S(1)}, f32[128,256]{1,0:T(8,128)S(1)}, u32[]{:S(2)}, u32[]{:S(2)}) collective-permute-start(f32[128,256]{1,0:T(8,128)S(1)} %add.20), channel_id=1, source_target_pairs={{0,8},{1,9},{2,10},{3,11},{4,12},{5,13},{6,14},{7,15},{8,0},{9,1},... | collective-permute-start | bytes 393224 | tf_op jit(solution)/shard_map/cond/branch_1_fun/ppermute | solution.py:23
  33.5 5.6 %collective-permute-start.5 = (bf16[1,1,128,256]{3,2,1,0:T(8,128)(2,1)S(1)}, bf16[1,1,128,256]{3,2,1,0:T(8,128)(2,1)S(1)}, u32[]{:S(2)}, u32[]{:S(2)}) collective-permute-start(bf16[1,1,128,256]{3,2,1,0:T(8,128)(2,1)S(1)} %fusion), channel_id=1, source_target_pairs={{0,2},{1,3},{2,0},{3,1},{4,6},{5,7},{6,4},{7,5},{8,10},{9,11},{10,... | collective-permute-start | bytes 196616 | tf_op jit(solution)/shard_map/cond/branch_1_fun/ppermute | solution.py:23
  34.0 12.3 %collective-permute-start.10 = (bf16[128,1024]{1,0:T(8,128)(2,1)}, bf16[128,1024]{1,0:T(8,128)(2,1)}, u32[]{:S(2)}, u32[]{:S(2)}) collective-permute-start(bf16[128,1024]{1,0:T(8,128)(2,1)} %get-tuple-element.93), channel_id=1, source_target_pairs={{0,8},{1,9},{2,10},{3,11},{4,12},{5,13},{6,14},{7,15},{8,0},{9,1},... | collective-permute-start | bytes 786440 | tf_op jit(solution)/shard_map/cond/branch_1_fun/ppermute | solution.py:23
  35.0 11.6 %collective-permute-start.9 = (bf16[128,1024]{1,0:T(8,128)(2,1)}, bf16[128,1024]{1,0:T(8,128)(2,1)}, u32[]{:S(2)}, u32[]{:S(2)}) collective-permute-start(bf16[128,1024]{1,0:T(8,128)(2,1)} %get-tuple-element.93), channel_id=1, source_target_pairs={{0,4},{1,5},{2,6},{3,7},{4,0},{5,1},{6,2},{7,3},{8,12},{9,13},{10,... | collective-permute-start | bytes 786440 | tf_op jit(solution)/shard_map/cond/branch_1_fun/ppermute | solution.py:23
  38.5 6.0 %collective-permute-start.6 = (bf16[1,1,128,256]{3,2,1,0:T(8,128)(2,1)S(1)}, bf16[1,1,128,256]{3,2,1,0:T(8,128)(2,1)}, u32[]{:S(2)}, u32[]{:S(2)}) collective-permute-start(bf16[1,1,128,256]{3,2,1,0:T(8,128)(2,1)S(1)} %fusion), channel_id=1, source_target_pairs={{0,16},{16,0},{1,17},{17,1},{2,18},{18,2},{3,19},{19,3},{4,20},{20... | collective-permute-start | bytes 196616 | tf_op jit(solution)/shard_map/cond/branch_1_fun/ppermute | solution.py:23
  44.5 4.0 %collective-permute-start.8 = (bf16[2,1,128,256]{3,2,1,0:T(8,128)(2,1)S(1)}, bf16[2,1,128,256]{3,2,1,0:T(8,128)(2,1)S(1)}, u32[]{:S(2)}, u32[]{:S(2)}) collective-permute-start(bf16[2,1,128,256]{3,2,1,0:T(8,128)(2,1)S(1)} %pad_maximum_fusion.1), channel_id=1, source_target_pairs={{0,1},{1,0},{2,3},{3,2},{4,5},{5,4},{6,7},{7,6},{8,9},{9,8},{10,11... | collective-permute-start | bytes 393224 | tf_op jit(solution)/shard_map/cond/branch_1_fun/ppermute | solution.py:23
  48.5 0.8 copy-start.9
  49.3 24.8 %collective-permute-start.28 = (bf16[256,1024]{1,0:T(8,128)(2,1)}, bf16[256,1024]{1,0:T(8,128)(2,1)S(1)}, u32[]{:S(2)}, u32[]{:S(2)}) collective-permute-start(bf16[256,1024]{1,0:T(8,128)(2,1)} %get-tuple-element.202), channel_id=1, source_target_pairs={{0,8},{1,9},{2,10},{3,11},{4,12},{5,13},{6,14},{7,15},{8,0},{9,1},... | collective-permute-start | bytes 1572872 | tf_op jit(solution)/shard_map/ppermute | solution.py:23
  52.4 21.8 %collective-permute-start.27 = (bf16[256,1024]{1,0:T(8,128)(2,1)}, bf16[256,1024]{1,0:T(8,128)(2,1)S(1)}, u32[]{:S(2)}, u32[]{:S(2)}) collective-permute-start(bf16[256,1024]{1,0:T(8,128)(2,1)} %get-tuple-element.202), channel_id=1, source_target_pairs={{0,4},{1,5},{2,6},{3,7},{4,0},{5,1},{6,2},{7,3},{8,12},{9,13},{10,... | collective-permute-start | bytes 1572872 | tf_op jit(solution)/shard_map/ppermute | solution.py:23
  54.1 16.3 %collective-permute-start.26 = (bf16[256,1024]{1,0:T(8,128)(2,1)}, bf16[256,1024]{1,0:T(8,128)(2,1)S(1)}, u32[]{:S(2)}, u32[]{:S(2)}) collective-permute-start(bf16[256,1024]{1,0:T(8,128)(2,1)} %get-tuple-element.202), channel_id=1, source_target_pairs={{0,2},{1,3},{2,0},{3,1},{4,6},{5,7},{6,4},{7,5},{8,10},{9,11},{10,... | collective-permute-start | bytes 1572872 | tf_op jit(solution)/shard_map/ppermute | solution.py:23
  55.7 13.2 %collective-permute-start.29 = (bf16[512,512]{1,0:T(8,128)(2,1)}, bf16[512,512]{1,0:T(8,128)(2,1)S(1)}, u32[]{:S(2)}, u32[]{:S(2)}) collective-permute-start(bf16[512,512]{1,0:T(8,128)(2,1)} %get-tuple-element.212), channel_id=1, source_target_pairs={{0,16},{16,0},{1,17},{17,1},{2,18},{18,2},{3,19},{19,3},{4,20},{20... | collective-permute-start | bytes 1572872 | tf_op jit(solution)/shard_map/ppermute | solution.py:23
  56.2 23.9 %copy-start = (bf16[512,1024]{1,0:T(8,128)(2,1)S(1)}, bf16[512,1024]{1,0:T(8,128)(2,1)}, u32[]{:S(2)}) copy-start(bf16[512,1024]{1,0:T(8,128)(2,1)} %refs_13_.1) | copy-start | bytes 3145732
  68.9 22.9 %copy-start.5 = (bf16[512,512]{1,0:T(8,128)(2,1)}, bf16[512,512]{1,0:T(8,128)(2,1)S(1)}, u32[]{:S(2)}) copy-start(bf16[512,512]{1,0:T(8,128)(2,1)S(1)} %collective-permute-done.29) | copy-start | bytes 1572868
  68.9 23.9 %collective-permute-start.30 = (bf16[256,2048]{1,0:T(8,128)(2,1)}, bf16[256,2048]{1,0:T(8,128)(2,1)}, u32[]{:S(2)}, u32[]{:S(2)}) collective-permute-start(bf16[256,2048]{1,0:T(8,128)(2,1)} %get-tuple-element.213), channel_id=1, source_target_pairs={{0,16},{16,0},{1,17},{17,1},{2,18},{18,2},{3,19},{19,3},{4,20},{20... | collective-permute-start | bytes 3145736 | tf_op jit(solution)/shard_map/ppermute | solution.py:23
  70.5 21.4 %copy-start.4 = (bf16[256,1024]{1,0:T(8,128)(2,1)}, bf16[256,1024]{1,0:T(8,128)(2,1)S(1)}, u32[]{:S(2)}) copy-start(bf16[256,1024]{1,0:T(8,128)(2,1)S(1)} %collective-permute-done.26.refs_2_) | copy-start | bytes 1572868
  74.1 17.7 %copy-start.2 = (bf16[256,1024]{1,0:T(8,128)(2,1)}, bf16[256,1024]{1,0:T(8,128)(2,1)S(1)}, u32[]{:S(2)}) copy-start(bf16[256,1024]{1,0:T(8,128)(2,1)S(1)} %collective-permute-done.28.refs_4_) | copy-start | bytes 1572868
  74.3 17.6 %copy-start.3 = (bf16[256,1024]{1,0:T(8,128)(2,1)}, bf16[256,1024]{1,0:T(8,128)(2,1)S(1)}, u32[]{:S(2)}) copy-start(bf16[256,1024]{1,0:T(8,128)(2,1)S(1)} %collective-permute-done.27.refs_3_) | copy-start | bytes 1572868
  74.3 27.8 %collective-permute-start.31 = (bf16[512,512]{1,0:T(8,128)(2,1)}, bf16[512,512]{1,0:T(8,128)(2,1)}, u32[]{:S(2)}, u32[]{:S(2)}) collective-permute-start(bf16[512,512]{1,0:T(8,128)(2,1)} %copy-done.9), channel_id=1, source_target_pairs={{0,2},{1,3},{2,0},{3,1},{4,6},{5,7},{6,4},{7,5},{8,10},{9,11},{10,... | collective-permute-start | bytes 1572872 | tf_op jit(solution)/shard_map/ppermute | solution.py:23
  76.1 26.0 %collective-permute-start.33 = (bf16[256,1024]{1,0:T(8,128)(2,1)}, bf16[256,1024]{1,0:T(8,128)(2,1)}, u32[]{:S(2)}, u32[]{:S(2)}) collective-permute-start(bf16[256,1024]{1,0:T(8,128)(2,1)} %get-tuple-element.221), channel_id=1, source_target_pairs={{0,8},{1,9},{2,10},{3,11},{4,12},{5,13},{6,14},{7,15},{8,0},{9,1},... | collective-permute-start | bytes 1572872 | tf_op jit(solution)/shard_map/ppermute | solution.py:23
  77.8 24.3 %collective-permute-start.32 = (bf16[256,1024]{1,0:T(8,128)(2,1)}, bf16[256,1024]{1,0:T(8,128)(2,1)}, u32[]{:S(2)}, u32[]{:S(2)}) collective-permute-start(bf16[256,1024]{1,0:T(8,128)(2,1)} %get-tuple-element.219), channel_id=1, source_target_pairs={{0,4},{1,5},{2,6},{3,7},{4,0},{5,1},{6,2},{7,3},{8,12},{9,13},{10,... | collective-permute-start | bytes 1572872 | tf_op jit(solution)/shard_map/ppermute | solution.py:23
  80.1 12.7 %copy-start.8 = (f32[256,256]{1,0:T(8,128)S(1)}, f32[256,256]{1,0:T(8,128)}, u32[]{:S(2)}) copy-start(f32[256,256]{1,0:T(8,128)} %get-tuple-element.214) | copy-start | bytes 786436
  91.9 37.3 %collective-permute-start.34 = (bf16[384,2048]{1,0:T(8,128)(2,1)}, bf16[384,2048]{1,0:T(8,128)(2,1)S(1)}, u32[]{:S(2)}, u32[]{:S(2)}) collective-permute-start(bf16[384,2048]{1,0:T(8,128)(2,1)} %get-tuple-element.236), channel_id=1, source_target_pairs={{0,16},{16,0},{1,17},{17,1},{2,18},{18,2},{3,19},{19,3},{4,20},{20... | collective-permute-start | bytes 4718600 | tf_op jit(solution)/shard_map/ppermute | solution.py:23
  93.5 1.9 %collective-permute-start.11 = (f32[256,256]{1,0:T(8,128)}, f32[256,256]{1,0:T(8,128)}, u32[]{:S(2)}, u32[]{:S(2)}) collective-permute-start(f32[256,256]{1,0:T(8,128)} %broadcast_select_fusion), channel_id=1, source_target_pairs={{0,1},{1,0},{2,3},{3,2},{4,5},{5,4},{6,7},{7,6},{8,9},{9,8},{10,11... | collective-permute-start | bytes 786440 | tf_op jit(solution)/shard_map/cond/branch_1_fun/ppermute | solution.py:23
  96.4 5.6 %collective-permute-start.12 = (f32[128,256]{1,0:T(8,128)S(1)}, f32[128,256]{1,0:T(8,128)S(1)}, u32[]{:S(2)}, u32[]{:S(2)}) collective-permute-start(f32[128,256]{1,0:T(8,128)S(1)} %slice_select_fusion.2), channel_id=1, source_target_pairs={{0,2},{1,3},{2,0},{3,1},{4,6},{5,7},{6,4},{7,5},{8,10},{9,11},{10,... | collective-permute-start | bytes 393224 | tf_op jit(solution)/shard_map/cond/branch_1_fun/ppermute | solution.py:23
  102.1 14.7 %collective-permute-start.15 = (bf16[256,1024]{1,0:T(8,128)(2,1)}, bf16[256,1024]{1,0:T(8,128)(2,1)}, u32[]{:S(2)}, u32[]{:S(2)}) collective-permute-start(bf16[256,1024]{1,0:T(8,128)(2,1)} %get-tuple-element.100), channel_id=1, source_target_pairs={{0,1},{1,0},{2,3},{3,2},{4,5},{5,4},{6,7},{7,6},{8,9},{9,8},{10,11... | collective-permute-start | bytes 1572872 | tf_op jit(solution)/shard_map/cond/branch_1_fun/ppermute | solution.py:23
  102.2 14.7 %collective-permute-start.16 = (bf16[256,1024]{1,0:T(8,128)(2,1)}, bf16[256,1024]{1,0:T(8,128)(2,1)}, u32[]{:S(2)}, u32[]{:S(2)}) collective-permute-start(bf16[256,1024]{1,0:T(8,128)(2,1)} %get-tuple-element.101), channel_id=1, source_target_pairs={{0,2},{1,3},{2,0},{3,1},{4,6},{5,7},{6,4},{7,5},{8,10},{9,11},{10,... | collective-permute-start | bytes 1572872 | tf_op jit(solution)/shard_map/cond/branch_1_fun/ppermute | solution.py:23
  102.8 5.6 %collective-permute-start.13 = (f32[128,256]{1,0:T(8,128)S(1)}, f32[128,256]{1,0:T(8,128)S(1)}, u32[]{:S(2)}, u32[]{:S(2)}) collective-permute-start(f32[128,256]{1,0:T(8,128)S(1)} %get-tuple-element.99), channel_id=1, source_target_pairs={{0,4},{1,5},{2,6},{3,7},{4,0},{5,1},{6,2},{7,3},{8,12},{9,13},{10,... | collective-permute-start | bytes 393224 | tf_op jit(solution)/shard_map/cond/branch_1_fun/ppermute | solution.py:23
  108.4 8.4 %collective-permute-start.14 = (f32[128,256]{1,0:T(8,128)S(1)}, f32[128,256]{1,0:T(8,128)S(1)}, u32[]{:S(2)}, u32[]{:S(2)}) collective-permute-start(f32[128,256]{1,0:T(8,128)S(1)} %add.24), channel_id=1, source_target_pairs={{0,8},{1,9},{2,10},{3,11},{4,12},{5,13},{6,14},{7,15},{8,0},{9,1},... | collective-permute-start | bytes 393224 | tf_op jit(solution)/shard_map/cond/branch_1_fun/ppermute | solution.py:23
  116.9 26.7 %collective-permute-start.35 = (bf16[256,1024]{1,0:T(8,128)(2,1)}, bf16[256,1024]{1,0:T(8,128)(2,1)}, u32[]{:S(2)}, u32[]{:S(2)}) collective-permute-start(bf16[256,1024]{1,0:T(8,128)(2,1)} %get-tuple-element.240), channel_id=1, source_target_pairs={{0,4},{1,5},{2,6},{3,7},{4,0},{5,1},{6,2},{7,3},{8,12},{9,13},{10,... | collective-permute-start | bytes 1572872 | tf_op jit(solution)/shard_map/ppermute | solution.py:23
  117.2 26.4 %collective-permute-start.36 = (bf16[256,1024]{1,0:T(8,128)(2,1)}, bf16[256,1024]{1,0:T(8,128)(2,1)}, u32[]{:S(2)}, u32[]{:S(2)}) collective-permute-start(bf16[256,1024]{1,0:T(8,128)(2,1)} %get-tuple-element.243), channel_id=1, source_target_pairs={{0,8},{1,9},{2,10},{3,11},{4,12},{5,13},{6,14},{7,15},{8,0},{9,1},... | collective-permute-start | bytes 1572872 | tf_op jit(solution)/shard_map/ppermute | solution.py:23
  120.7 6.0 %collective-permute-start.18 = (bf16[256,1024]{1,0:T(8,128)(2,1)}, bf16[256,1024]{1,0:T(8,128)(2,1)}, u32[]{:S(2)}, u32[]{:S(2)}) collective-permute-start(bf16[256,1024]{1,0:T(8,128)(2,1)} %get-tuple-element.103), channel_id=1, source_target_pairs={{0,1},{1,0},{2,3},{3,2},{4,5},{5,4},{6,7},{7,6},{8,9},{9,8},{10,11... | collective-permute-start | bytes 1572872 | tf_op jit(solution)/shard_map/cond/branch_1_fun/ppermute | solution.py:23
  120.8 5.9 %collective-permute-start.17 = (bf16[1,2,128,256]{3,2,1,0:T(8,128)(2,1)S(1)}, bf16[1,2,128,256]{3,2,1,0:T(8,128)(2,1)S(1)}, u32[]{:S(2)}, u32[]{:S(2)}) collective-permute-start(bf16[1,2,128,256]{3,2,1,0:T(8,128)(2,1)S(1)} %get-tuple-element.102), channel_id=1, source_target_pairs={{0,2},{1,3},{2,0},{3,1},{4,6},{5,7},{6,4},{7,5},{8,10},{9,11},{10,... | collective-permute-start | bytes 393224 | tf_op jit(solution)/shard_map/cond/branch_1_fun/ppermute | solution.py:23
  126.7 2.4 %collective-permute-start.20 = (bf16[512,512]{1,0:T(8,128)(2,1)}, bf16[512,512]{1,0:T(8,128)(2,1)}, u32[]{:S(2)}, u32[]{:S(2)}) collective-permute-start(bf16[512,512]{1,0:T(8,128)(2,1)} %get-tuple-element.107), channel_id=1, source_target_pairs={{0,1},{1,0},{2,3},{3,2},{4,5},{5,4},{6,7},{7,6},{8,9},{9,8},{10,11... | collective-permute-start | bytes 1572872 | tf_op jit(solution)/shard_map/cond/branch_1_fun/ppermute | solution.py:23
  126.8 2.3 %collective-permute-start.19 = (bf16[2,2,128,256]{3,2,1,0:T(8,128)(2,1)S(1)}, bf16[2,2,128,256]{3,2,1,0:T(8,128)(2,1)S(1)}, u32[]{:S(2)}, u32[]{:S(2)}) collective-permute-start(bf16[2,2,128,256]{3,2,1,0:T(8,128)(2,1)S(1)} %pad_maximum_fusion.3), channel_id=1, source_target_pairs={{0,1},{1,0},{2,3},{3,2},{4,5},{5,4},{6,7},{7,6},{8,9},{9,8},{10,11... | collective-permute-start | bytes 786440 | tf_op jit(solution)/shard_map/cond/branch_1_fun/ppermute | solution.py:23
  129.2 14.3 %collective-permute-start.1 = (bf16[256,1024]{1,0:T(8,128)(2,1)}, bf16[256,1024]{1,0:T(8,128)(2,1)}, u32[]{:S(2)}, u32[]{:S(2)}) collective-permute-start(bf16[256,1024]{1,0:T(8,128)(2,1)} %get-tuple-element.109), channel_id=1, source_target_pairs={{0,2},{1,3},{2,0},{3,1},{4,6},{5,7},{6,4},{7,5},{8,10},{9,11},{10,... | collective-permute-start | bytes 1572872 | tf_op jit(solution)/shard_map/cond/branch_1_fun/ppermute | solution.py:23
  130.8 10.6 %collective-permute-start = (bf16[4,1,128,256]{3,2,1,0:T(8,128)(2,1)S(1)}, bf16[4,1,128,256]{3,2,1,0:T(8,128)(2,1)}, u32[]{:S(2)}, u32[]{:S(2)}) collective-permute-start(bf16[4,1,128,256]{3,2,1,0:T(8,128)(2,1)S(1)} %slice.13), channel_id=1, source_target_pairs={{0,16},{16,0},{1,17},{17,1},{2,18},{18,2},{3,19},{19,3},{4,20},{20... | collective-permute-start | bytes 786440 | tf_op jit(solution)/shard_map/cond/branch_1_fun/ppermute | solution.py:23
